TPU v7x, 32 devices: a whole 2x2x4 slice. The times are simulated.
32 devices in a mesh: groups: 2 (over x), row: 16 (over z, y, core).
Axes of the slice: x: 2, y: 2, z: 4, core: 2. Of those that a mesh axis runs over, the one named last changes fastest.
Arguments:
- pair_act: bfloat16 [3072, 256, 128], P(('groups', 'row')), parts along dimension 0, may hold values from -36 to 36
- pair_mask: int32 [3072, 256], P(('groups', 'row')), parts along dimension 0, may hold values from 0 to 1, as said below
- in_gain: float32 [128], replicated, may hold values from 0.25 to 1.75
- in_bias: float32 [128], replicated, may hold values from -3 to 3
- w_proj: bfloat16 [128, 256], replicated, may hold values from -0.5 to 0.5
- w_gate: bfloat16 [128, 128], replicated, may hold values from -0.5 to 0.5
- out_gain: float32 [64], replicated, may hold values from 0.25 to 1.75
- out_bias: float32 [64], replicated, may hold values from -3 to 3
- w_out: bfloat16 [64, 128], replicated, may hold values from -0.75 to 0.75
Outputs:
- update: bfloat16 [512, 256, 128], P(('groups', 'row')), parts along dimension 0
There are 2 independent parts, one for each index of `groups`. A program takes and returns all parts, laid end to end along the dimension named above; an argument that names none is the same for every part. Nothing has to cross between parts.
Inputs may be any that keep to these rules, and one draw needn't show every extreme that they name: pair_mask[k, w] is 1 exactly where both token k and the token of window token w are below the complex's length, which is 768 or more, else 0.
All inputs are finite; a program needn't handle non-finite values.
Results may differ from a plain program's by a relative error of at most 0.0053.
Values may be sent and summed in bfloat16 or wider, within the bound.
No kernel may reach another device: no remote copies, remote signals or barrier semaphores. Data moves between devices by JAX's collectives and lax.ppermute only.
A program may use at most 320 MiB of HBM per device.

v0:
```python
import jax
import jax.numpy as jnp
from jax import lax
from jax.sharding import PartitionSpec as P


def normalize(values, gain_vec, bias_vec, reduce_axis):
    mean_val = jnp.mean(values, axis=reduce_axis, keepdims=True)
    centered = values - mean_val
    variance = jnp.mean(centered * centered, axis=reduce_axis, keepdims=True)
    return centered * lax.rsqrt(variance + 1e-05) * gain_vec + bias_vec


def on_device(pair_act, pair_mask, in_gain, in_bias, w_proj, w_gate, out_gain, out_bias, w_out):
    row_count, window_count, chan_count = pair_act.shape
    hidden_width = w_out.shape[0]
    out_rows = window_count // lax.axis_size("row")
    normed = normalize(pair_act.astype(jnp.float32), in_gain, in_bias, 2).astype(jnp.bfloat16)
    keep_mask = pair_mask.astype(jnp.float32)[None]
    left_proj = jnp.einsum(
        "kic,cf->fki", normed, w_proj[:, : 2 * hidden_width], preferred_element_type=jnp.float32
    )
    left_act = (
        jax.nn.sigmoid(left_proj[:hidden_width]) * left_proj[hidden_width:] * keep_mask
    ).astype(jnp.bfloat16)
    right_proj = jnp.einsum(
        "kic,cf->fki", normed, w_proj[:, 2 * hidden_width :], preferred_element_type=jnp.float32
    )
    right_act = (
        jax.nn.sigmoid(right_proj[:hidden_width]) * right_proj[hidden_width:] * keep_mask
    ).astype(jnp.bfloat16)
    triangle = lax.psum_scatter(
        jnp.einsum("hki,hkj->ihj", left_act, right_act, preferred_element_type=jnp.float32),
        "row",
        scatter_dimension=0,
        tiled=True,
    )
    triangle_norm = normalize(triangle, out_gain[None, :, None], out_bias[None, :, None], 1).astype(
        jnp.bfloat16
    )
    gate_act = jax.nn.sigmoid(
        jnp.einsum("ijc,cd->ijd", normed[:out_rows], w_gate, preferred_element_type=jnp.float32)
    )
    mixed = jnp.einsum("ihj,hc->ijc", triangle_norm, w_out, preferred_element_type=jnp.float32)
    return (gate_act * mixed).astype(jnp.bfloat16)


def solution(mesh):
    return jax.shard_map(
        on_device,
        mesh=mesh,
        in_specs=(
            P(("groups", "row"), None, None),
            P(("groups", "row"), None),
            P(),
            P(),
            P(),
            P(),
            P(),
            P(),
            P(),
        ),
        out_specs=P(("groups", "row"), None, None),
        check_vma=False,
    )
```

profile of v0, /device:TPU:0, one launch (start us, length us, event | category | flops | bytes accessed | tf_op | source)
XLA Modules:
  0.0 278.2 jit_solution(11029599196891940587)
XLA Ops:
  6.5 0.0 copy-start
  6.5 0.0 copy-start.5
  6.5 0.0 copy-start.6
  6.5 0.0 copy-start.3
  6.5 0.0 reduce-scatter.2.cloned.1.call-start
  6.6 0.0 copy-start.1
  6.6 4.7 %convert_reduce_fusion = f32[96,256]{1,0:T(8,128)S(1)} fusion(bf16[96,256,128]{2,1,0:T(8,128)(2,1)} %param.9), kind=kLoop, calls=%fused_computation.1 | loop fusion | flops 6266880 | bytes 6389760 | tf_op jit(solution)/shard_map/reduce_sum | solution.py:8
  11.3 0.0 copy-done.1
  11.3 7.3 %fusion.2 = f32[96,256]{1,0:T(8,128)S(1)} fusion(bf16[96,256,128]{2,1,0:T(8,128)(2,1)S(1)} %copy-done.1, f32[96,256]{1,0:T(8,128)S(1)} %broadcast_multiply_fusion), kind=kLoop, calls=%fused_computation.4 | loop fusion | flops 12558336 | bytes 6488064 | tf_op jit(solution)/shard_map/reduce_sum | solution.py:10
  18.6 0.0 copy-done.5
  18.7 0.0 copy-done.6
  18.7 0.0 copy-done.3
  18.7 14.8 %convolution_bitcast_fusion.2 = f32[128,96,256]{2,0,1:T(8,128)S(1)} fusion(bf16[96,256,128]{2,1,0:T(8,128)(2,1)S(1)} %copy-done.1, f32[128]{0:T(128)S(1)} %copy-done.5, f32[128]{0:T(128)S(1)} %copy-done.6, f32[96,256]{1,0:T(8,128)S(1)} %add_rsqrt_fusion, f32[96,256]{1,0:T(8,128)S(1)} %broadcast_multiply_fusion, bf16[128,256]{1,0:T(8,128)(2,1)S(1)} %copy-done.3), kind=kOutput, calls=%fused_computation.24 | convolution fusion | flops 824180736 | bytes 19104768 | tf_op jit(solution)/shard_map/kic,cf->fki/dot_general | solution.py:26
  33.5 0.0 copy-start.2
  33.5 12.2 %convolution_bitcast_fusion.1 = f32[128,96,256]{2,0,1:T(8,128)} fusion(bf16[96,256,128]{2,1,0:T(8,128)(2,1)S(1)} %copy-done.1, f32[128]{0:T(128)S(1)} %copy-done.5, f32[128]{0:T(128)S(1)} %copy-done.6, f32[96,256]{1,0:T(8,128)S(1)} %add_rsqrt_fusion, f32[96,256]{1,0:T(8,128)S(1)} %broadcast_multiply_fusion, bf16[128,256]{1,0:T(8,128)(2,1)S(1)} %copy-done.3), kind=kOutput, calls=%fused_computation.23 | convolution fusion | flops 824180736 | bytes 19104768 | tf_op jit(solution)/shard_map/kic,cf->fki/dot_general | solution.py:20
  45.7 0.0 copy-done.2
  45.7 7.4 %fusion.12 = (bf16[64,96,256]{2,0,1:T(8,128)(2,1)S(1)}, bf16[64,96,256]{2,0,1:T(8,128)(2,1)S(1)}) fusion(f32[128,96,256]{2,0,1:T(8,128)S(1)} %convolution_bitcast_fusion.2, f32[96,256]{1,0:T(8,128)S(1)} %convert_element_type.23, f32[128,96,256]{2,0,1:T(8,128)} %convolution_bitcast_fusion.1), kind=kLoop, calls=%fused_computation.18 | loop fusion | flops 18874368 | bytes 31555584 | tf_op jit(solution)/shard_map/convert_element_type | solution.py:31
  53.1 11.2 %convolution_bitcast_fusion = f32[256,64,256]{0,2,1:T(8,128)} fusion(bf16[64,96,256]{2,0,1:T(8,128)(2,1)S(1)} %get-tuple-element.6, bf16[64,96,256]{2,0,1:T(8,128)(2,1)S(1)} %get-tuple-element.5), kind=kOutput, calls=%fused_computation.8 | convolution fusion | flops 805306368 | bytes 23068672 | tf_op jit(solution)/shard_map/hki,hkj->ihj/dot_general | solution.py:33
  64.3 17.7 %copy.19 = f32[256,64,256]{2,1,0:T(8,128)} copy(f32[256,64,256]{0,2,1:T(8,128)} %convolution_bitcast_fusion) | data formatting | bytes 33554432 | tf_op jit(solution)/shard_map/hki,hkj->ihj/transpose | solution.py:33
  82.0 0.0 copy-start.4
  82.0 0.0 copy-start.7
  82.0 0.0 copy-start.8
  82.0 0.0 reduce-scatter.2.cloned.1.call-update
  82.0 181.4 %reduce-scatter.2.cloned.1.call-done = f32[16,64,256]{2,1,0:T(8,128)} async-done(((f32[256,64,256]{2,1,0:T(8,128)}), f32[16,64,256]{2,1,0:T(8,128)}) %reduce-scatter.2.cloned.1.call-update) | async-done | bytes 1048592 | tf_op jit(solution)/shard_map/reduce_scatter | solution.py:32
  263.4 1.3 reduce_sum.38
  264.7 1.4 multiply_reduce_fusion
  266.1 0.0 copy-done.4
  266.1 0.0 copy-done.7
  266.1 0.0 copy-done.8
  266.2 1.8 fusion.18
  268.0 0.0 copy-done
  268.0 3.4 %multiply_convert_fusion = bf16[16,256,128]{2,1,0:T(8,128)(2,1)} fusion(f32[16,256,128]{2,1,0:T(8,128)S(1)} %fusion.18, bf16[96,256,128]{2,1,0:T(8,128)(2,1)} %param.9, f32[128]{0:T(128)S(1)} %copy-done.5, f32[128]{0:T(128)S(1)} %copy-done.6, f32[96,256]{1,0:T(8,128)S(1)} %add_rsqrt_fusion, f32[96,256]{1,0:T(8,128)S(1)} %broadcast_multiply_fusion, ...), kind=kOutput, calls=%fused_computation.27 | convolution fusion | flops 155713536 | bytes 9667584 | tf_op jit(solution)/shard_map/ijc,cd->ijd/dot_general | solution.py:42
  (5 shorter events, 0.1 us)
Async XLA Ops:
  6.5 261.4 %copy-start = (bf16[128,128]{1,0:T(8,128)(2,1)S(1)}, bf16[128,128]{1,0:T(8,128)(2,1)}, u32[]{:S(2)}) copy-start(bf16[128,128]{1,0:T(8,128)(2,1)} %param.14) | copy-start | bytes 98308
  6.5 12.1 %copy-start.5 = (f32[128]{0:T(128)S(1)}, f32[128]{0:T(128)}, u32[]{:S(2)}) copy-start(f32[128]{0:T(128)} %param.12) | copy-start | bytes 1540
  6.5 12.1 %copy-start.6 = (f32[128]{0:T(128)S(1)}, f32[128]{0:T(128)}, u32[]{:S(2)}) copy-start(f32[128]{0:T(128)} %param.11) | copy-start | bytes 1540
  6.5 12.1 %copy-start.3 = (bf16[128,256]{1,0:T(8,128)(2,1)S(1)}, bf16[128,256]{1,0:T(8,128)(2,1)}, u32[]{:S(2)}) copy-start(bf16[128,256]{1,0:T(8,128)(2,1)} %param.13) | copy-start | bytes 196612
  6.5 256.9 %reduce-scatter.2.cloned.1.call-start = ((), (), s32[]{:S(2)}) async-start(), calls=%async_computation.1 | async-start | bytes 17825792 | tf_op jit(solution)/shard_map/reduce_scatter | solution.py:32
  6.6 4.7 %copy-start.1 = (bf16[96,256,128]{2,1,0:T(8,128)(2,1)S(1)}, bf16[96,256,128]{2,1,0:T(8,128)(2,1)}, u32[]{:S(2)}) copy-start(bf16[96,256,128]{2,1,0:T(8,128)(2,1)} %param.9) | copy-start | bytes 18874372
  33.5 12.2 %copy-start.2 = (s32[96,256]{1,0:T(8,128)S(1)}, s32[96,256]{1,0:T(8,128)}, u32[]{:S(2)}) copy-start(s32[96,256]{1,0:T(8,128)} %param.10) | copy-start | bytes 294916
  82.0 184.2 %copy-start.4 = (bf16[64,128]{1,0:T(8,128)(2,1)S(1)}, bf16[64,128]{1,0:T(8,128)(2,1)}, u32[]{:S(2)}) copy-start(bf16[64,128]{1,0:T(8,128)(2,1)} %param.17) | copy-start | bytes 49156
  82.0 184.2 %copy-start.7 = (f32[64]{0:T(128)S(1)}, f32[64]{0:T(128)}, u32[]{:S(2)}) copy-start(f32[64]{0:T(128)} %param.16) | copy-start | bytes 772
  82.0 184.2 %copy-start.8 = (f32[64]{0:T(128)S(1)}, f32[64]{0:T(128)}, u32[]{:S(2)}) copy-start(f32[64]{0:T(128)} %param.15) | copy-start | bytes 772
Sparse Core Ops, SparseCore 0:
  82.1 181.2 reduce-scatter.1
where the time goes:
time: 279 us; the launch traced here: 278 us
  waiting for transfers between devices  181 us (65%)
  matrix products  43.3 us (16%)
  other arithmetic  22.1 us (8%)
  local copies, waits for them, and re-layouts  17.7 us (6%)
  between operations  13.6 us (5%)
    reduce_scatter x1, waiting for transfers between devices, on_device(): lax.psum_scatter(jnp.einsum('hki,hkj->ihj', left_act, right_act, preferre...  181 us
    transpose x1, local copies, waits for them, and re-layouts, on_device(): jnp.einsum('hki,hkj->ihj', left_act, right_act, preferred_element_type=jn...  17.7 us
    dot_general x1, matrix products, on_device(): jnp.einsum('kic,cf->fki', normed, w_proj[:, 2 * hidden_width:], preferred...  14.8 us
    dot_general x1, matrix products, on_device(): jnp.einsum('kic,cf->fki', normed, w_proj[:, :2 * hidden_width], preferred...  12.2 us
    dot_general x1, matrix products, on_device(): jnp.einsum('hki,hkj->ihj', left_act, right_act, preferred_element_type=jn...  11.2 us
    reduce_sum x2, other arithmetic, normalize(): variance = jnp.mean(centered * centered, axis=reduce_axis, keepdims=True)  8.69 us
    convert_element_type x1, other arithmetic, on_device(): right_act = (jax.nn.sigmoid(right_proj[:hidden_width]) * right_proj[hidde...  7.39 us
    reduce_sum x2, other arithmetic, normalize(): mean_val = jnp.mean(values, axis=reduce_axis, keepdims=True)  5.97 us
  transfers between devices with their start and end apart: 1, of which 1 were waited for; matrix products, arithmetic and copies ran while one was open for 0% of the time, Pallas kernels for 0%

commit v1 on v0

v1 whole, which is shorter than its diff:
```python
import functools

import jax
import jax.numpy as jnp
from jax import lax
from jax.experimental import pallas as pl
from jax.experimental.pallas import tpu as pltpu
from jax.sharding import PartitionSpec as P

f32 = jnp.float32
bf16 = jnp.bfloat16
LANES = 128
EPS = 1e-05
VMEM_BYTES = 40 * 2**20


def sigmoid(values):
    return 0.5 * jnp.tanh(0.5 * values) + 0.5


def whole(shape):
    return pl.BlockSpec(shape, lambda *_: (0,) * len(shape))


def call(body, grid, in_specs, out_specs, out_shape, scratch, cost, prefetch=1):
    return pl.pallas_call(
        body,
        grid_spec=pltpu.PrefetchScalarGridSpec(
            num_scalar_prefetch=prefetch,
            grid=grid,
            in_specs=in_specs,
            out_specs=out_specs,
            scratch_shapes=scratch,
        ),
        out_shape=out_shape,
        compiler_params=pltpu.CompilerParams(vmem_limit_bytes=VMEM_BYTES),
        cost_estimate=pl.CostEstimate(flops=cost[0], bytes_accessed=cost[1], transcendentals=0),
    )


def norm_columns(tile, gain, bias):
    count = tile.shape[0]
    mean_val = jnp.sum(tile, axis=0, keepdims=True) * (1.0 / count)
    centered = tile - mean_val
    variance = jnp.sum(centered * centered, axis=0, keepdims=True) * (1.0 / count)
    return (centered * lax.rsqrt(variance + EPS) * gain + bias).astype(bf16)


def spread(vec_ref, width):
    tile = jnp.broadcast_to(vec_ref[...], (vec_ref.shape[0], LANES))
    return jnp.concatenate([tile] * (width // LANES), axis=1)


def project_body(chunks, stride, place, x_ref, mask_ref, gain_ref, bias_ref, w_ref, *rest):
    count = len(chunks)
    outs, hold = (rest[:count], rest[count : 2 * count]), rest[2 * count]
    rows, width, _ = x_ref.shape
    hidden = w_ref.shape[1] // 4
    half = hidden // 2
    gain, bias = spread(gain_ref, width), spread(bias_ref, width)
    weights = w_ref[...]
    for k in range(rows):
        normed = norm_columns(x_ref[k].T.astype(f32), gain, bias)
        proj = lax.dot_general(weights, normed, (((0,), (0,)), ((), ())), preferred_element_type=f32)
        keep = mask_ref[pl.ds(k, 1), :].astype(f32)
        for side in range(2):
            low = 2 * side * hidden
            act = sigmoid(proj[low : low + hidden]) * proj[low + hidden : low + 2 * hidden] * keep
            for part in range(width // LANES):
                hold[part, pl.ds(k * stride + side * hidden, hidden), :] = act[
                    :, part * LANES : (part + 1) * LANES
                ]
    core = place[2]
    for owner in range(2):
        base = jnp.where(core == owner, 0, half)
        first = 0
        for out, size in zip(outs[owner], chunks):
            for side in range(2):
                for h in range(size):
                    for part in range(width // LANES):
                        tile = hold[part, pl.ds(base + side * hidden + first + h, rows, stride=stride), :]
                        out[side, h, :, part * LANES : (part + 1) * LANES] = tile.astype(bf16)
            first += size


def project(place, x, mask, gain, bias, w_proj, chunks):
    depth, width, chan = x.shape
    rows = 16
    hidden = w_proj.shape[1] // 4
    stride = 2 * hidden + 8
    return call(
        functools.partial(project_body, chunks, stride),
        (depth // rows,),
        [
            pl.BlockSpec((rows, width, chan), lambda i, _: (i, 0, 0)),
            pl.BlockSpec((rows, width), lambda i, _: (i, 0)),
            whole((chan, 1)),
            whole((chan, 1)),
            whole(w_proj.shape),
        ],
        [pl.BlockSpec((2, size, rows, width), lambda i, _: (0, 0, i, 0)) for size in chunks] * 2,
        [jax.ShapeDtypeStruct((2, size, depth, width), bf16) for size in chunks] * 2,
        [pltpu.VMEM((width // LANES, rows * stride, LANES), f32)],
        (2 * depth * width * chan * 4 * hidden, 4 * depth * width * chan),
    )(place, x, mask, gain.reshape(chan, 1), bias.reshape(chan, 1), w_proj)


def gate_body(x_ref, gain_ref, bias_ref, w_ref, out_ref):
    width = x_ref.shape[1]
    gain, bias = spread(gain_ref, width), spread(bias_ref, width)
    weights = w_ref[...]
    for k in range(x_ref.shape[0]):
        normed = norm_columns(x_ref[k].T.astype(f32), gain, bias)
        proj = lax.dot_general(normed, weights, (((0,), (0,)), ((), ())), preferred_element_type=f32)
        out_ref[k] = sigmoid(proj)


def gate(x, gain, bias, w_gate, rows):
    _, width, chan = x.shape
    step = 8
    return call(
        gate_body,
        (rows // step,),
        [
            pl.BlockSpec((step, width, chan), lambda i: (i, 0, 0)),
            whole((chan, 1)),
            whole((chan, 1)),
            whole(w_gate.shape),
        ],
        pl.BlockSpec((step, width, chan), lambda i: (i, 0, 0)),
        jax.ShapeDtypeStruct((rows, width, chan), f32),
        [],
        (2 * rows * width * chan * chan, 6 * rows * width * chan),
        prefetch=0,
    )(x, gain.reshape(chan, 1), bias.reshape(chan, 1), w_gate)


def triangle_body(place, own_ref, got_ref, keep_ref, send_ref, hold):
    _, step, layers, block, width = (0,) + keep_ref.shape
    layer, column = place[0], place[1]
    for h in range(step):
        left = jnp.concatenate([own_ref[0, h], got_ref[0, h]], axis=0)
        right = jnp.concatenate([own_ref[1, h], got_ref[1, h]], axis=0)
        hold[h] = lax.dot_general(left, right, (((0,), (0,)), ((), ())), preferred_element_type=f32)
        for slot in range(layers):
            first = ((layer ^ slot) * 2 + column) * block
            other = ((layer ^ slot) * 2 + 1 - column) * block
            keep_ref[h, slot] = hold[h, pl.ds(pl.multiple_of(first, block), block), :]
            send_ref[h, slot] = hold[h, pl.ds(pl.multiple_of(other, block), block), :].astype(bf16)


def triangle(place, own, got, layers):
    _, size, depth, width = own.shape
    step = min(size, 4)
    block = width // (2 * layers)
    spec = pl.BlockSpec((2, step, depth, width), lambda i, _: (0, i, 0, 0))
    out_spec = pl.BlockSpec((step, layers, block, width), lambda i, _: (i, 0, 0, 0))
    shape = (size, layers, block, width)
    return call(
        triangle_body,
        (size // step,),
        [spec, spec],
        [out_spec, out_spec],
        [jax.ShapeDtypeStruct(shape, f32), jax.ShapeDtypeStruct(shape, bf16)],
        [pltpu.VMEM((step, width, width), f32)],
        (4 * size * depth * width * width, 8 * size * depth * width + 3 * size * width * width),
    )(place, own, got)


def layer_body(keep_ref, got_ref, own_ref, *send_refs):
    own_ref[...] = keep_ref[:, 0] + got_ref[:, 0].astype(f32)
    for slot, send_ref in enumerate(send_refs, 1):
        send_ref[...] = (keep_ref[:, slot] + got_ref[:, slot].astype(f32)).astype(bf16)


def layer_sum(keep, got):
    size, layers, block, width = keep.shape
    step = min(size, 4)
    spec = pl.BlockSpec((step, layers, block, width), lambda i: (i, 0, 0, 0))
    out_spec = pl.BlockSpec((step, block, width), lambda i: (i, 0, 0))
    shape = (size, block, width)
    return call(
        layer_body,
        (size // step,),
        [spec, spec],
        [out_spec] * layers,
        [jax.ShapeDtypeStruct(shape, f32)] + [jax.ShapeDtypeStruct(shape, bf16)] * (layers - 1),
        [],
        (keep.size, keep.size * 8),
        prefetch=0,
    )(keep, got)


def total_body(place, own_ref, *rest):
    got_refs, (mine_ref, theirs_ref, hold) = rest[:-3], rest[-3:]
    total = own_ref[...]
    for got_ref in got_refs:
        total = total + got_ref[...].astype(f32)
    hold[...] = total
    rows = mine_ref.shape[1]
    core = place[2]
    mine_ref[...] = hold[:, pl.ds(pl.multiple_of(core * rows, rows), rows), :]
    theirs_ref[...] = hold[:, pl.ds(pl.multiple_of((1 - core) * rows, rows), rows), :]


def total_sum(place, own, gots):
    size, block, width = own.shape
    step = min(size, 4)
    spec = pl.BlockSpec((step, block, width), lambda i, _: (i, 0, 0))
    out_spec = pl.BlockSpec((step, block // 2, width), lambda i, _: (i, 0, 0))
    shape = jax.ShapeDtypeStruct((size, block // 2, width), f32)
    return call(
        total_body,
        (size // step,),
        [spec] * (1 + len(gots)),
        [out_spec] * 2,
        [shape, shape],
        [pltpu.VMEM((step, block, width), f32)],
        (own.size * len(gots), own.size * (8 + 2 * len(gots))),
    )(place, own, *gots)


def finish_body(chunks, place, *refs):
    count = len(chunks)
    mine, theirs = refs[:count], refs[count : 2 * count]
    gate_ref, gain_ref, bias_ref, w_ref, out_ref, hold = refs[2 * count :]
    hidden, _ = w_ref.shape
    half = hidden // 2
    _, rows, width = mine[0].shape
    stride = hold.shape[1] // hidden
    core = place[2]
    total = jnp.zeros((rows, width), f32)
    for part in mine + theirs:
        total = total + jnp.sum(part[...], axis=0)
    mean_val = total * (1.0 / hidden)
    square = jnp.zeros((rows, width), f32)
    for part in mine + theirs:
        for h in range(part.shape[0]):
            centered = part[h] - mean_val
            square = square + centered * centered
    scale = lax.rsqrt(square * (1.0 / hidden) + EPS)
    for owner, parts in ((0, mine), (1, theirs)):
        index = jnp.where(core == owner, 0, half)
        for part in parts:
            for h in range(part.shape[0]):
                value = (part[h] - mean_val) * scale * gain_ref[index] + bias_ref[index]
                for lane in range(width // LANES):
                    hold[lane, pl.ds(index * stride, rows), :] = value[:, lane * LANES : (lane + 1) * LANES]
                index = index + 1
    weights = w_ref[...]
    for row in range(rows):
        for lane in range(width // LANES):
            normed = hold[lane, pl.ds(row, hidden, stride=stride), :].astype(bf16)
            mixed = lax.dot_general(normed, weights, (((0,), (0,)), ((), ())), preferred_element_type=f32)
            span = pl.ds(lane * LANES, LANES)
            out_ref[row, span, :] = (gate_ref[row, span, :] * mixed).astype(bf16)


def finish(place, mine, theirs, gate_act, gain, bias, w_out):
    rows, width, chan = gate_act.shape
    hidden = w_out.shape[0]
    step = 8
    stride = step + 8
    parts = [pl.BlockSpec((part.shape[0], step, width), lambda i, _: (0, i, 0)) for part in mine]
    spec = pl.BlockSpec((step, width, chan), lambda i, _: (i, 0, 0))
    smem = pl.BlockSpec(memory_space=pltpu.SMEM)
    return call(
        functools.partial(finish_body, [part.shape[0] for part in mine]),
        (rows // step,),
        parts * 2 + [spec, smem, smem, whole(w_out.shape)],
        spec,
        jax.ShapeDtypeStruct((rows, width, chan), bf16),
        [pltpu.VMEM((width // LANES, hidden * stride, LANES), f32)],
        (2 * rows * width * chan * hidden, rows * width * (chan * 6 + hidden * 4)),
    )(place, *mine, *theirs, gate_act, gain, bias, w_out)


def on_device(pair_act, pair_mask, in_gain, in_bias, w_proj, w_gate, out_gain, out_bias, w_out):
    width = pair_act.shape[1]
    devices = lax.axis_size("row")
    layers = devices // 4
    half = w_out.shape[0] // 2
    chunks = (half // 4,) * 4
    index = lax.axis_index("row")
    place = jnp.stack([index // 4, index // 2 % 2, index % 2]).astype(jnp.int32)

    def swap(values, bit):
        return lax.ppermute(values, "row", [(d, d ^ bit) for d in range(devices)])

    acts = project(place, pair_act, pair_mask, in_gain, in_bias, w_proj, chunks)
    count = len(chunks)
    got = [swap(part, 1) for part in acts[count:]]
    gate_act = gate(pair_act, in_gain, in_bias, w_gate, width // devices)
    mine, theirs = [], []
    for own, other in zip(acts[:count], got):
        keep, send = triangle(place, own, other, layers)
        own_sum, *sends = layer_sum(keep, swap(send, 2))
        gots = [swap(part, 4 * slot) for slot, part in enumerate(sends, 1)]
        mine_part, send_part = total_sum(place, own_sum, gots)
        mine.append(mine_part)
        theirs.append(swap(send_part, 1))
    return finish(place, mine, theirs, gate_act, out_gain, out_bias, w_out)


def solution(mesh):
    return jax.shard_map(
        on_device,
        mesh=mesh,
        in_specs=(
            P(("groups", "row"), None, None),
            P(("groups", "row"), None),
            P(),
            P(),
            P(),
            P(),
            P(),
            P(),
            P(),
        ),
        out_specs=P(("groups", "row"), None, None),
        check_vma=False,
    )
```

time: 279 us -> 113 us (0.41)
  waiting for transfers between devices: 181 us -> 42.2 us
  matrix products: 43.3 us -> 0 us
  starting transfers between devices: 0.03 us -> 37.1 us
  Pallas kernels: 0 us -> 26.2 us
  other arithmetic: 22.1 us -> 0.08 us
  between operations: 13.6 us -> 0.3 us
  local copies, waits for them, and re-layouts: 17.7 us -> 6.06 us
    reduce_scatter x1 -> x0, waiting for transfers between devices: 181 us -> none  [on_device(): lax.psum_scatter(jnp.einsum('hki,hkj->ihj', left_act, right_act, preferre...]
    dot_general x5 -> x0, matrix products: 43.3 us -> none  [the longest x1 14.8 us: on_device(): jnp.einsum('kic,cf->fki', normed, w_proj[:, 2 * hidden_width:], preferred...]
    ppermute x0 -> x24, waiting for transfers between devices: none -> 42.2 us  [swap(): return lax.ppermute(values, 'row', [(d, d ^ bit) for d in range(devices)])]
    ppermute x0 -> x24, starting transfers between devices: none -> 37.1 us  [swap(): return lax.ppermute(values, 'row', [(d, d ^ bit) for d in range(devices)])]
    pallas_call x0 -> x15, Pallas kernels: none -> 26.2 us  [the longest x1 12.3 us: project(): call(functools.partial(project_body, chunks, stride), (depth // rows,), [...]
    transpose x1 -> x0, local copies, waits for them, and re-layouts: 17.7 us -> none  [on_device(): jnp.einsum('hki,hkj->ihj', left_act, right_act, preferred_element_type=jn...]
    reduce_sum x4 -> x0, other arithmetic: 14.7 us -> none  [the longest x2 8.69 us: normalize(): variance = jnp.mean(centered * centered, axis=reduce_axis, keepdims=True)]
    convert_element_type x2 -> x0, other arithmetic: 7.4 us -> none  [the longest x1 7.39 us: on_device(): right_act = (jax.nn.sigmoid(right_proj[:hidden_width]) * right_proj[hidde...]
  transfers between devices with their start and end apart: 1 -> 24, of which waited for: 1 -> 7; matrix products, arithmetic and copies ran while one was open for 0% -> 0% of each run, Pallas kernels for 0% -> 9%
where the time goes in v1:
time: 113 us; the launch traced here: 112 us
  waiting for transfers between devices  42.2 us (37%)
  starting transfers between devices  37.1 us (33%)
  Pallas kernels  26.2 us (23%)
  local copies, waits for them, and re-layouts  6.06 us (5%)
    ppermute x24, waiting for transfers between devices, swap(): return lax.ppermute(values, 'row', [(d, d ^ bit) for d in range(devices)])  42.2 us
    ppermute x24, starting transfers between devices, swap(): return lax.ppermute(values, 'row', [(d, d ^ bit) for d in range(devices)])  37.1 us
    pallas_call x1, Pallas kernels, project(): call(functools.partial(project_body, chunks, stride), (depth // rows,), [...  12.3 us
    pallas_call x4, Pallas kernels, triangle(): call(triangle_body, (size // step,), [spec, spec], [out_spec, out_spec],...  5.93 us
    unnamed x18, local copies, waits for them, and re-layouts  4.54 us
    pallas_call x1, Pallas kernels, finish(): call(functools.partial(finish_body, [part.shape[0] for part in mine]), (r...  3.25 us
    pallas_call x4, Pallas kernels, total_sum(): call(total_body, (size // step,), [spec] * (1 + len(gots)), [out_spec] *...  2.68 us
  transfers between devices with their start and end apart: 24, of which 7 were waited for; matrix products, arithmetic and copies ran while one was open for 0% of the time, Pallas kernels for 9%

profile of v1, /device:TPU:0, one launch (start us, length us, event | category | flops | bytes accessed | tf_op | source)
XLA Modules:
  0.0 111.9 jit_solution(4962835185390003576)
XLA Ops:
  0.0 0.8 copy.10.gain_ref
  0.8 0.8 copy.11.bias_ref
  1.6 2.8 %copy-done = bf16[96,256,128]{2,1,0:T(8,128)(2,1)S(1)} copy-done((bf16[96,256,128]{2,1,0:T(8,128)(2,1)S(1)}, bf16[96,256,128]{2,1,0:T(8,128)(2,1)}, u32[]{:S(2)}) %copy-start) | copy-done | bytes 6291480
  4.4 0.9 copy-done.1
  5.3 0.8 copy-done.2
  6.1 12.3 %shard_map.91 = (bf16[2,8,96,256]{3,2,1,0:T(8,128)(2,1)S(1)}, bf16[2,8,96,256]{3,2,1,0:T(8,128)(2,1)S(1)}, bf16[2,8,96,256]{3,2,1,0:T(8,128)(2,1)S(1)}, bf16[2,8...) custom-call(s32[3]{0:T(128)S(1)} %pad_add_fusion.place, ...), custom_call_target="tpu_custom_call" | custom-call | flops 1610612736 | bytes 12582912 | tf_op jit(solution)/shard_map/pallas_call | solution.py:91
  18.5 0.5 collective-permute-start.15
  19.0 0.1 collective-permute-start.10
  19.1 0.4 collective-permute-start.5
  19.5 0.1 collective-permute-start
  19.6 1.3 %collective-permute-done.15.got_ref = bf16[2,8,96,256]{3,2,1,0:T(8,128)(2,1)S(1)} collective-permute-done((bf16[2,8,96,256]{3,2,1,0:T(8,128)(2,1)S(1)}, bf16[2,8,96,256]{3,2,1,0:T(8,128)(2,1)S(1)}, u32[]{:S(2)}, u32[]{:S(2)}) %collective-permute-start.15) | collective-permute-done | bytes 786464 | tf_op jit(solution)/shard_map/ppermute | solution.py:288
  20.9 1.5 %shard_map.101 = (f32[8,4,32,256]{3,2,1,0:T(8,128)S(1)}, bf16[8,4,32,256]{3,2,1,0:T(8,128)(2,1)S(1)}) custom-call(s32[3]{0:T(128)S(1)} %pad_add_fusion.place, bf16[2,8,96,256]{3,2,1,0:T(8,128)(2,1)S(1)} %get-tuple-element.72.own_ref, bf16[2,8,96,256]{3,2,1,0:T(8,128)(2,1)S(1)} %collective-permute-done.15.got_ref), custom_call_target="tpu_custom_call" | custom-call | flops 201326592 | bytes 3145728 | tf_op jit(solution)/shard_map/pallas_call | solution.py:159
  22.4 3.0 %collective-permute-start.16 = (bf16[8,4,32,256]{3,2,1,0:T(8,128)(2,1)S(1)}, bf16[8,4,32,256]{3,2,1,0:T(8,128)(2,1)S(1)}, u32[]{:S(2)}, u32[]{:S(2)}) collective-permute-start(bf16[8,4,32,256]{3,2,1,0:T(8,128)(2,1)S(1)} %get-tuple-element.75), channel_id=1, source_target_pairs={{0,2},{1,3},{2,0},{3,1},{4,6},{5,7},{6,4},{7,5},{8,10},{9,11},{10,... | collective-permute-start | bytes 1572872 | tf_op jit(solution)/shard_map/ppermute | solution.py:288
  25.4 1.5 %shard_map.98 = (f32[8,4,32,256]{3,2,1,0:T(8,128)S(1)}, bf16[8,4,32,256]{3,2,1,0:T(8,128)(2,1)S(1)}) custom-call(s32[3]{0:T(128)S(1)} %pad_add_fusion.place, bf16[2,8,96,256]{3,2,1,0:T(8,128)(2,1)S(1)} %get-tuple-element.63.own_ref, bf16[2,8,96,256]{3,2,1,0:T(8,128)(2,1)S(1)} %collective-permute-done.10.got_ref), custom_call_target="tpu_custom_call" | custom-call | flops 201326592 | bytes 3145728 | tf_op jit(solution)/shard_map/pallas_call | solution.py:159
  26.9 0.1 collective-permute-start.11
  27.0 1.5 %shard_map.95 = (f32[8,4,32,256]{3,2,1,0:T(8,128)S(1)}, bf16[8,4,32,256]{3,2,1,0:T(8,128)(2,1)S(1)}) custom-call(s32[3]{0:T(128)S(1)} %pad_add_fusion.place, bf16[2,8,96,256]{3,2,1,0:T(8,128)(2,1)S(1)} %get-tuple-element.54.own_ref, bf16[2,8,96,256]{3,2,1,0:T(8,128)(2,1)S(1)} %collective-permute-done.5.got_ref), custom_call_target="tpu_custom_call" | custom-call | flops 201326592 | bytes 3145728 | tf_op jit(solution)/shard_map/pallas_call | solution.py:159
  28.4 2.1 %collective-permute-start.6 = (bf16[8,4,32,256]{3,2,1,0:T(8,128)(2,1)S(1)}, bf16[8,4,32,256]{3,2,1,0:T(8,128)(2,1)S(1)}, u32[]{:S(2)}, u32[]{:S(2)}) collective-permute-start(bf16[8,4,32,256]{3,2,1,0:T(8,128)(2,1)S(1)} %get-tuple-element.57), channel_id=1, source_target_pairs={{0,2},{1,3},{2,0},{3,1},{4,6},{5,7},{6,4},{7,5},{8,10},{9,11},{10,... | collective-permute-start | bytes 1572872 | tf_op jit(solution)/shard_map/ppermute | solution.py:288
  30.5 1.5 %shard_map.92 = (f32[8,4,32,256]{3,2,1,0:T(8,128)S(1)}, bf16[8,4,32,256]{3,2,1,0:T(8,128)(2,1)S(1)}) custom-call(s32[3]{0:T(128)S(1)} %pad_add_fusion.place, bf16[2,8,96,256]{3,2,1,0:T(8,128)(2,1)S(1)} %get-tuple-element.45.own_ref, bf16[2,8,96,256]{3,2,1,0:T(8,128)(2,1)S(1)} %collective-permute-done.got_ref), custom_call_target="tpu_custom_call" | custom-call | flops 201326592 | bytes 3145728 | tf_op jit(solution)/shard_map/pallas_call | solution.py:159
  32.0 0.1 collective-permute-start.1
  32.1 6.0 %collective-permute-done.16.got_ref = bf16[8,4,32,256]{3,2,1,0:T(8,128)(2,1)S(1)} collective-permute-done((bf16[8,4,32,256]{3,2,1,0:T(8,128)(2,1)S(1)}, bf16[8,4,32,256]{3,2,1,0:T(8,128)(2,1)S(1)}, u32[]{:S(2)}, u32[]{:S(2)}) %collective-permute-start.16) | collective-permute-done | bytes 524320 | tf_op jit(solution)/shard_map/ppermute | solution.py:288
  38.1 0.1 shard_map.102
  38.2 2.2 %collective-permute-start.17 = (bf16[8,32,256]{2,1,0:T(8,128)(2,1)S(1)}, bf16[8,32,256]{2,1,0:T(8,128)(2,1)S(1)}, u32[]{:S(2)}, u32[]{:S(2)}) collective-permute-start(bf16[8,32,256]{2,1,0:T(8,128)(2,1)S(1)} %get-tuple-element.77), channel_id=1, source_target_pairs={{0,4},{1,5},{2,6},{3,7},{4,0},{5,1},{6,2},{7,3},{8,12},{9,13},{10,... | collective-permute-start | bytes 393224 | tf_op jit(solution)/shard_map/ppermute | solution.py:288
  40.4 2.6 %collective-permute-start.18 = (bf16[8,32,256]{2,1,0:T(8,128)(2,1)S(1)}, bf16[8,32,256]{2,1,0:T(8,128)(2,1)S(1)}, u32[]{:S(2)}, u32[]{:S(2)}) collective-permute-start(bf16[8,32,256]{2,1,0:T(8,128)(2,1)S(1)} %get-tuple-element.78), channel_id=1, source_target_pairs={{0,8},{1,9},{2,10},{3,11},{4,12},{5,13},{6,14},{7,15},{8,0},{9,1},... | collective-permute-start | bytes 393224 | tf_op jit(solution)/shard_map/ppermute | solution.py:288
  43.0 6.3 %collective-permute-done.11.got_ref = bf16[8,4,32,256]{3,2,1,0:T(8,128)(2,1)S(1)} collective-permute-done((bf16[8,4,32,256]{3,2,1,0:T(8,128)(2,1)S(1)}, bf16[8,4,32,256]{3,2,1,0:T(8,128)(2,1)S(1)}, u32[]{:S(2)}, u32[]{:S(2)}) %collective-permute-start.11) | collective-permute-done | bytes 524320 | tf_op jit(solution)/shard_map/ppermute | solution.py:288
  49.3 4.1 %collective-permute-start.19 = (bf16[8,32,256]{2,1,0:T(8,128)(2,1)S(1)}, bf16[8,32,256]{2,1,0:T(8,128)(2,1)S(1)}, u32[]{:S(2)}, u32[]{:S(2)}) collective-permute-start(bf16[8,32,256]{2,1,0:T(8,128)(2,1)S(1)} %get-tuple-element.79), channel_id=1, source_target_pairs={{0,12},{1,13},{2,14},{3,15},{4,8},{5,9},{6,10},{7,11},{8,4},{9,5},... | collective-permute-start | bytes 393224 | tf_op jit(solution)/shard_map/ppermute | solution.py:288
  53.4 0.1 shard_map.99
  53.6 6.9 %collective-permute-done.6.got_ref = bf16[8,4,32,256]{3,2,1,0:T(8,128)(2,1)S(1)} collective-permute-done((bf16[8,4,32,256]{3,2,1,0:T(8,128)(2,1)S(1)}, bf16[8,4,32,256]{3,2,1,0:T(8,128)(2,1)S(1)}, u32[]{:S(2)}, u32[]{:S(2)}) %collective-permute-start.6) | collective-permute-done | bytes 524320 | tf_op jit(solution)/shard_map/ppermute | solution.py:288
  60.5 2.1 %collective-permute-start.12 = (bf16[8,32,256]{2,1,0:T(8,128)(2,1)S(1)}, bf16[8,32,256]{2,1,0:T(8,128)(2,1)S(1)}, u32[]{:S(2)}, u32[]{:S(2)}) collective-permute-start(bf16[8,32,256]{2,1,0:T(8,128)(2,1)S(1)} %get-tuple-element.68), channel_id=1, source_target_pairs={{0,4},{1,5},{2,6},{3,7},{4,0},{5,1},{6,2},{7,3},{8,12},{9,13},{10,... | collective-permute-start | bytes 393224 | tf_op jit(solution)/shard_map/ppermute | solution.py:288
  62.7 0.1 shard_map.96
  62.8 8.5 %collective-permute-done.1.got_ref = bf16[8,4,32,256]{3,2,1,0:T(8,128)(2,1)S(1)} collective-permute-done((bf16[8,4,32,256]{3,2,1,0:T(8,128)(2,1)S(1)}, bf16[8,4,32,256]{3,2,1,0:T(8,128)(2,1)S(1)}, u32[]{:S(2)}, u32[]{:S(2)}) %collective-permute-start.1) | collective-permute-done | bytes 524320 | tf_op jit(solution)/shard_map/ppermute | solution.py:288
  71.3 2.8 %collective-permute-start.13 = (bf16[8,32,256]{2,1,0:T(8,128)(2,1)S(1)}, bf16[8,32,256]{2,1,0:T(8,128)(2,1)S(1)}, u32[]{:S(2)}, u32[]{:S(2)}) collective-permute-start(bf16[8,32,256]{2,1,0:T(8,128)(2,1)S(1)} %get-tuple-element.69), channel_id=1, source_target_pairs={{0,8},{1,9},{2,10},{3,11},{4,12},{5,13},{6,14},{7,15},{8,0},{9,1},... | collective-permute-start | bytes 393224 | tf_op jit(solution)/shard_map/ppermute | solution.py:288
  74.1 1.4 %collective-permute-start.14 = (bf16[8,32,256]{2,1,0:T(8,128)(2,1)S(1)}, bf16[8,32,256]{2,1,0:T(8,128)(2,1)S(1)}, u32[]{:S(2)}, u32[]{:S(2)}) collective-permute-start(bf16[8,32,256]{2,1,0:T(8,128)(2,1)S(1)} %get-tuple-element.70), channel_id=1, source_target_pairs={{0,12},{1,13},{2,14},{3,15},{4,8},{5,9},{6,10},{7,11},{8,4},{9,5},... | collective-permute-start | bytes 393224 | tf_op jit(solution)/shard_map/ppermute | solution.py:288
  75.5 0.3 collective-permute-start.7
  75.8 0.1 shard_map.93
  75.9 2.8 %collective-permute-start.8 = (bf16[8,32,256]{2,1,0:T(8,128)(2,1)S(1)}, bf16[8,32,256]{2,1,0:T(8,128)(2,1)S(1)}, u32[]{:S(2)}, u32[]{:S(2)}) collective-permute-start(bf16[8,32,256]{2,1,0:T(8,128)(2,1)S(1)} %get-tuple-element.60), channel_id=1, source_target_pairs={{0,8},{1,9},{2,10},{3,11},{4,12},{5,13},{6,14},{7,15},{8,0},{9,1},... | collective-permute-start | bytes 393224 | tf_op jit(solution)/shard_map/ppermute | solution.py:288
  78.7 1.4 %collective-permute-start.9 = (bf16[8,32,256]{2,1,0:T(8,128)(2,1)S(1)}, bf16[8,32,256]{2,1,0:T(8,128)(2,1)S(1)}, u32[]{:S(2)}, u32[]{:S(2)}) collective-permute-start(bf16[8,32,256]{2,1,0:T(8,128)(2,1)S(1)} %get-tuple-element.61), channel_id=1, source_target_pairs={{0,12},{1,13},{2,14},{3,15},{4,8},{5,9},{6,10},{7,11},{8,4},{9,5},... | collective-permute-start | bytes 393224 | tf_op jit(solution)/shard_map/ppermute | solution.py:288
  80.1 4.8 %collective-permute-done.13.rest_1_ = bf16[8,32,256]{2,1,0:T(8,128)(2,1)S(1)} collective-permute-done((bf16[8,32,256]{2,1,0:T(8,128)(2,1)S(1)}, bf16[8,32,256]{2,1,0:T(8,128)(2,1)S(1)}, u32[]{:S(2)}, u32[]{:S(2)}) %collective-permute-start.13) | collective-permute-done | bytes 131104 | tf_op jit(solution)/shard_map/ppermute | solution.py:288
  84.9 8.9 %collective-permute-start.3 = (bf16[8,32,256]{2,1,0:T(8,128)(2,1)S(1)}, bf16[8,32,256]{2,1,0:T(8,128)(2,1)S(1)}, u32[]{:S(2)}, u32[]{:S(2)}) collective-permute-start(bf16[8,32,256]{2,1,0:T(8,128)(2,1)S(1)} %get-tuple-element.51), channel_id=1, source_target_pairs={{0,8},{1,9},{2,10},{3,11},{4,12},{5,13},{6,14},{7,15},{8,0},{9,1},... | collective-permute-start | bytes 393224 | tf_op jit(solution)/shard_map/ppermute | solution.py:288
  93.8 1.4 %collective-permute-start.4 = (bf16[8,32,256]{2,1,0:T(8,128)(2,1)S(1)}, bf16[8,32,256]{2,1,0:T(8,128)(2,1)S(1)}, u32[]{:S(2)}, u32[]{:S(2)}) collective-permute-start(bf16[8,32,256]{2,1,0:T(8,128)(2,1)S(1)} %get-tuple-element.52), channel_id=1, source_target_pairs={{0,12},{1,13},{2,14},{3,15},{4,8},{5,9},{6,10},{7,11},{8,4},{9,5},... | collective-permute-start | bytes 393224 | tf_op jit(solution)/shard_map/ppermute | solution.py:288
  95.2 0.7 shard_map.103
  95.9 0.7 shard_map.100
  96.7 0.5 collective-permute-start.22
  97.2 0.7 shard_map.97
  97.9 0.2 collective-permute-start.21
  98.0 8.3 %collective-permute-done.3.rest_1_ = bf16[8,32,256]{2,1,0:T(8,128)(2,1)S(1)} collective-permute-done((bf16[8,32,256]{2,1,0:T(8,128)(2,1)S(1)}, bf16[8,32,256]{2,1,0:T(8,128)(2,1)S(1)}, u32[]{:S(2)}, u32[]{:S(2)}) %collective-permute-start.3) | collective-permute-done | bytes 131104 | tf_op jit(solution)/shard_map/ppermute | solution.py:288
  106.4 0.7 shard_map.94
  107.2 1.4 %shard_map.104.refs_8_ = f32[16,256,128]{2,1,0:T(8,128)S(1)} custom-call(bf16[96,256,128]{2,1,0:T(8,128)(2,1)S(1)} %bitcast.6, f32[128,1]{1,0:T(8,128)S(1)} %copy.10.gain_ref, f32[128,1]{1,0:T(8,128)S(1)} %copy.11.bias_ref, bf16[128,128]{1,0:T(8,128)(2,1)S(1)} %copy-done.3), custom_call_target="tpu_custom_call" | custom-call | flops 134217728 | bytes 3145728 | tf_op jit(solution)/shard_map/pallas_call | solution.py:121
  108.7 3.3 %shard_map.105 = bf16[16,256,128]{2,1,0:T(8,128)(2,1)} custom-call(s32[3]{0:T(128)S(1)} %pad_add_fusion.place, f32[8,16,256]{2,1,0:T(8,128)S(1)} %get-tuple-element.53.refs_0_, f32[8,16,256]{2,1,0:T(8,128)S(1)} %get-tuple-element.62.refs_1_, f32[8,16,256]{2,1,0:T(8,128)S(1)} %get-tuple-element.71.refs_2_, f32[8,16,256]{2,1,0:T(8,128)S(1)} %get-tuple-element.80.refs_3_, ...), custom_call_target="tpu_custom_call" | custom-call | flops 67108864 | bytes 4194304 | tf_op jit(solution)/shard_map/pallas_call | solution.py:267
  (37 shorter events, 0.3 us)
Async XLA Ops:
  1.6 2.8 %copy-start = (bf16[96,256,128]{2,1,0:T(8,128)(2,1)S(1)}, bf16[96,256,128]{2,1,0:T(8,128)(2,1)}, u32[]{:S(2)}) copy-start(bf16[96,256,128]{2,1,0:T(8,128)(2,1)} %x_ref.3) | copy-start | bytes 18874372
  4.4 0.9 copy-start.1
  5.3 0.8 copy-start.2
  18.5 2.4 %collective-permute-start.15 = (bf16[2,8,96,256]{3,2,1,0:T(8,128)(2,1)S(1)}, bf16[2,8,96,256]{3,2,1,0:T(8,128)(2,1)S(1)}, u32[]{:S(2)}, u32[]{:S(2)}) collective-permute-start(bf16[2,8,96,256]{3,2,1,0:T(8,128)(2,1)S(1)} %get-tuple-element.73), channel_id=1, source_target_pairs={{0,1},{1,0},{2,3},{3,2},{4,5},{5,4},{6,7},{7,6},{8,9},{9,8},{10,11... | collective-permute-start | bytes 2359304 | tf_op jit(solution)/shard_map/ppermute | solution.py:288
  19.0 6.4 %collective-permute-start.10 = (bf16[2,8,96,256]{3,2,1,0:T(8,128)(2,1)S(1)}, bf16[2,8,96,256]{3,2,1,0:T(8,128)(2,1)S(1)}, u32[]{:S(2)}, u32[]{:S(2)}) collective-permute-start(bf16[2,8,96,256]{3,2,1,0:T(8,128)(2,1)S(1)} %get-tuple-element.64), channel_id=1, source_target_pairs={{0,1},{1,0},{2,3},{3,2},{4,5},{5,4},{6,7},{7,6},{8,9},{9,8},{10,11... | collective-permute-start | bytes 2359304 | tf_op jit(solution)/shard_map/ppermute | solution.py:288
  19.1 7.9 %collective-permute-start.5 = (bf16[2,8,96,256]{3,2,1,0:T(8,128)(2,1)S(1)}, bf16[2,8,96,256]{3,2,1,0:T(8,128)(2,1)S(1)}, u32[]{:S(2)}, u32[]{:S(2)}) collective-permute-start(bf16[2,8,96,256]{3,2,1,0:T(8,128)(2,1)S(1)} %get-tuple-element.55), channel_id=1, source_target_pairs={{0,1},{1,0},{2,3},{3,2},{4,5},{5,4},{6,7},{7,6},{8,9},{9,8},{10,11... | collective-permute-start | bytes 2359304 | tf_op jit(solution)/shard_map/ppermute | solution.py:288
  19.5 11.0 %collective-permute-start = (bf16[2,8,96,256]{3,2,1,0:T(8,128)(2,1)S(1)}, bf16[2,8,96,256]{3,2,1,0:T(8,128)(2,1)S(1)}, u32[]{:S(2)}, u32[]{:S(2)}) collective-permute-start(bf16[2,8,96,256]{3,2,1,0:T(8,128)(2,1)S(1)} %get-tuple-element.46), channel_id=1, source_target_pairs={{0,1},{1,0},{2,3},{3,2},{4,5},{5,4},{6,7},{7,6},{8,9},{9,8},{10,11... | collective-permute-start | bytes 2359304 | tf_op jit(solution)/shard_map/ppermute | solution.py:288
  20.9 86.2 %slice-start = ((s8[6291456]{0:T(1024)(128)(4,1)}), s8[4194304]{0:T(1024)(128)(4,1)S(1)}, s32[]{:S(2)}) async-start(s8[6291456]{0:T(1024)(128)(4,1)} %bitcast.5), calls=%async_computation | async-start | bytes 8388608
  22.4 15.7 %collective-permute-start.16 = (bf16[8,4,32,256]{3,2,1,0:T(8,128)(2,1)S(1)}, bf16[8,4,32,256]{3,2,1,0:T(8,128)(2,1)S(1)}, u32[]{:S(2)}, u32[]{:S(2)}) collective-permute-start(bf16[8,4,32,256]{3,2,1,0:T(8,128)(2,1)S(1)} %get-tuple-element.75), channel_id=1, source_target_pairs={{0,2},{1,3},{2,0},{3,1},{4,6},{5,7},{6,4},{7,5},{8,10},{9,11},{10,... | collective-permute-start | bytes 1572872 | tf_op jit(solution)/shard_map/ppermute | solution.py:288
  26.9 80.3 %copy-start.3 = (bf16[128,128]{1,0:T(8,128)(2,1)S(1)}, bf16[128,128]{1,0:T(8,128)(2,1)}, u32[]{:S(2)}) copy-start(bf16[128,128]{1,0:T(8,128)(2,1)} %w_ref.3) | copy-start | bytes 98308
  26.9 22.4 %collective-permute-start.11 = (bf16[8,4,32,256]{3,2,1,0:T(8,128)(2,1)S(1)}, bf16[8,4,32,256]{3,2,1,0:T(8,128)(2,1)S(1)}, u32[]{:S(2)}, u32[]{:S(2)}) collective-permute-start(bf16[8,4,32,256]{3,2,1,0:T(8,128)(2,1)S(1)} %get-tuple-element.66), channel_id=1, source_target_pairs={{0,2},{1,3},{2,0},{3,1},{4,6},{5,7},{6,4},{7,5},{8,10},{9,11},{10,... | collective-permute-start | bytes 1572872 | tf_op jit(solution)/shard_map/ppermute | solution.py:288
  28.4 32.1 %collective-permute-start.6 = (bf16[8,4,32,256]{3,2,1,0:T(8,128)(2,1)S(1)}, bf16[8,4,32,256]{3,2,1,0:T(8,128)(2,1)S(1)}, u32[]{:S(2)}, u32[]{:S(2)}) collective-permute-start(bf16[8,4,32,256]{3,2,1,0:T(8,128)(2,1)S(1)} %get-tuple-element.57), channel_id=1, source_target_pairs={{0,2},{1,3},{2,0},{3,1},{4,6},{5,7},{6,4},{7,5},{8,10},{9,11},{10,... | collective-permute-start | bytes 1572872 | tf_op jit(solution)/shard_map/ppermute | solution.py:288
  32.0 39.3 %collective-permute-start.1 = (bf16[8,4,32,256]{3,2,1,0:T(8,128)(2,1)S(1)}, bf16[8,4,32,256]{3,2,1,0:T(8,128)(2,1)S(1)}, u32[]{:S(2)}, u32[]{:S(2)}) collective-permute-start(bf16[8,4,32,256]{3,2,1,0:T(8,128)(2,1)S(1)} %get-tuple-element.48), channel_id=1, source_target_pairs={{0,2},{1,3},{2,0},{3,1},{4,6},{5,7},{6,4},{7,5},{8,10},{9,11},{10,... | collective-permute-start | bytes 1572872 | tf_op jit(solution)/shard_map/ppermute | solution.py:288
  38.1 69.1 %slice-start.1 = ((s8[6291456]{0:T(1024)(128)(4,1)}), s8[2097152]{0:T(1024)(128)(4,1)S(1)}, s32[]{:S(2)}) async-start(s8[6291456]{0:T(1024)(128)(4,1)} %bitcast.5), calls=%async_computation.1 | async-start | bytes 4194304
  38.2 35.9 %collective-permute-start.17 = (bf16[8,32,256]{2,1,0:T(8,128)(2,1)S(1)}, bf16[8,32,256]{2,1,0:T(8,128)(2,1)S(1)}, u32[]{:S(2)}, u32[]{:S(2)}) collective-permute-start(bf16[8,32,256]{2,1,0:T(8,128)(2,1)S(1)} %get-tuple-element.77), channel_id=1, source_target_pairs={{0,4},{1,5},{2,6},{3,7},{4,0},{5,1},{6,2},{7,3},{8,12},{9,13},{10,... | collective-permute-start | bytes 393224 | tf_op jit(solution)/shard_map/ppermute | solution.py:288
  40.4 35.1 %collective-permute-start.18 = (bf16[8,32,256]{2,1,0:T(8,128)(2,1)S(1)}, bf16[8,32,256]{2,1,0:T(8,128)(2,1)S(1)}, u32[]{:S(2)}, u32[]{:S(2)}) collective-permute-start(bf16[8,32,256]{2,1,0:T(8,128)(2,1)S(1)} %get-tuple-element.78), channel_id=1, source_target_pairs={{0,8},{1,9},{2,10},{3,11},{4,12},{5,13},{6,14},{7,15},{8,0},{9,1},... | collective-permute-start | bytes 393224 | tf_op jit(solution)/shard_map/ppermute | solution.py:288
  49.3 26.6 %collective-permute-start.19 = (bf16[8,32,256]{2,1,0:T(8,128)(2,1)S(1)}, bf16[8,32,256]{2,1,0:T(8,128)(2,1)S(1)}, u32[]{:S(2)}, u32[]{:S(2)}) collective-permute-start(bf16[8,32,256]{2,1,0:T(8,128)(2,1)S(1)} %get-tuple-element.79), channel_id=1, source_target_pairs={{0,12},{1,13},{2,14},{3,15},{4,8},{5,9},{6,10},{7,11},{8,4},{9,5},... | collective-permute-start | bytes 393224 | tf_op jit(solution)/shard_map/ppermute | solution.py:288
  60.5 18.1 %collective-permute-start.12 = (bf16[8,32,256]{2,1,0:T(8,128)(2,1)S(1)}, bf16[8,32,256]{2,1,0:T(8,128)(2,1)S(1)}, u32[]{:S(2)}, u32[]{:S(2)}) collective-permute-start(bf16[8,32,256]{2,1,0:T(8,128)(2,1)S(1)} %get-tuple-element.68), channel_id=1, source_target_pairs={{0,4},{1,5},{2,6},{3,7},{4,0},{5,1},{6,2},{7,3},{8,12},{9,13},{10,... | collective-permute-start | bytes 393224 | tf_op jit(solution)/shard_map/ppermute | solution.py:288
  71.3 13.6 %collective-permute-start.13 = (bf16[8,32,256]{2,1,0:T(8,128)(2,1)S(1)}, bf16[8,32,256]{2,1,0:T(8,128)(2,1)S(1)}, u32[]{:S(2)}, u32[]{:S(2)}) collective-permute-start(bf16[8,32,256]{2,1,0:T(8,128)(2,1)S(1)} %get-tuple-element.69), channel_id=1, source_target_pairs={{0,8},{1,9},{2,10},{3,11},{4,12},{5,13},{6,14},{7,15},{8,0},{9,1},... | collective-permute-start | bytes 393224 | tf_op jit(solution)/shard_map/ppermute | solution.py:288
  74.1 10.8 %collective-permute-start.14 = (bf16[8,32,256]{2,1,0:T(8,128)(2,1)S(1)}, bf16[8,32,256]{2,1,0:T(8,128)(2,1)S(1)}, u32[]{:S(2)}, u32[]{:S(2)}) collective-permute-start(bf16[8,32,256]{2,1,0:T(8,128)(2,1)S(1)} %get-tuple-element.70), channel_id=1, source_target_pairs={{0,12},{1,13},{2,14},{3,15},{4,8},{5,9},{6,10},{7,11},{8,4},{9,5},... | collective-permute-start | bytes 393224 | tf_op jit(solution)/shard_map/ppermute | solution.py:288
  75.5 18.3 %collective-permute-start.7 = (bf16[8,32,256]{2,1,0:T(8,128)(2,1)S(1)}, bf16[8,32,256]{2,1,0:T(8,128)(2,1)S(1)}, u32[]{:S(2)}, u32[]{:S(2)}) collective-permute-start(bf16[8,32,256]{2,1,0:T(8,128)(2,1)S(1)} %get-tuple-element.59), channel_id=1, source_target_pairs={{0,4},{1,5},{2,6},{3,7},{4,0},{5,1},{6,2},{7,3},{8,12},{9,13},{10,... | collective-permute-start | bytes 393224 | tf_op jit(solution)/shard_map/ppermute | solution.py:288
  75.8 32.9 %copy-start.4 = (bf16[64,128]{1,0:T(8,128)(2,1)S(1)}, bf16[64,128]{1,0:T(8,128)(2,1)}, u32[]{:S(2)}) copy-start(bf16[64,128]{1,0:T(8,128)(2,1)} %refs_11_.1) | copy-start | bytes 49156
  75.8 32.9 %copy-start.5 = (f32[64]{0:T(128)S(1)}, f32[64]{0:T(128)}, u32[]{:S(2)}) copy-start(f32[64]{0:T(128)} %refs_9_.1) | copy-start | bytes 772
  75.8 32.9 %copy-start.6 = (f32[64]{0:T(128)S(1)}, f32[64]{0:T(128)}, u32[]{:S(2)}) copy-start(f32[64]{0:T(128)} %refs_10_.1) | copy-start | bytes 772
  75.9 20.7 %collective-permute-start.8 = (bf16[8,32,256]{2,1,0:T(8,128)(2,1)S(1)}, bf16[8,32,256]{2,1,0:T(8,128)(2,1)S(1)}, u32[]{:S(2)}, u32[]{:S(2)}) collective-permute-start(bf16[8,32,256]{2,1,0:T(8,128)(2,1)S(1)} %get-tuple-element.60), channel_id=1, source_target_pairs={{0,8},{1,9},{2,10},{3,11},{4,12},{5,13},{6,14},{7,15},{8,0},{9,1},... | collective-permute-start | bytes 393224 | tf_op jit(solution)/shard_map/ppermute | solution.py:288
  78.7 18.0 %collective-permute-start.9 = (bf16[8,32,256]{2,1,0:T(8,128)(2,1)S(1)}, bf16[8,32,256]{2,1,0:T(8,128)(2,1)S(1)}, u32[]{:S(2)}, u32[]{:S(2)}) collective-permute-start(bf16[8,32,256]{2,1,0:T(8,128)(2,1)S(1)} %get-tuple-element.61), channel_id=1, source_target_pairs={{0,12},{1,13},{2,14},{3,15},{4,8},{5,9},{6,10},{7,11},{8,4},{9,5},... | collective-permute-start | bytes 393224 | tf_op jit(solution)/shard_map/ppermute | solution.py:288
  84.9 13.0 %collective-permute-start.2 = (bf16[8,32,256]{2,1,0:T(8,128)(2,1)S(1)}, bf16[8,32,256]{2,1,0:T(8,128)(2,1)S(1)}, u32[]{:S(2)}, u32[]{:S(2)}) collective-permute-start(bf16[8,32,256]{2,1,0:T(8,128)(2,1)S(1)} %get-tuple-element.50), channel_id=1, source_target_pairs={{0,4},{1,5},{2,6},{3,7},{4,0},{5,1},{6,2},{7,3},{8,12},{9,13},{10,... | collective-permute-start | bytes 393224 | tf_op jit(solution)/shard_map/ppermute | solution.py:288
  84.9 21.5 %collective-permute-start.3 = (bf16[8,32,256]{2,1,0:T(8,128)(2,1)S(1)}, bf16[8,32,256]{2,1,0:T(8,128)(2,1)S(1)}, u32[]{:S(2)}, u32[]{:S(2)}) collective-permute-start(bf16[8,32,256]{2,1,0:T(8,128)(2,1)S(1)} %get-tuple-element.51), channel_id=1, source_target_pairs={{0,8},{1,9},{2,10},{3,11},{4,12},{5,13},{6,14},{7,15},{8,0},{9,1},... | collective-permute-start | bytes 393224 | tf_op jit(solution)/shard_map/ppermute | solution.py:288
  93.8 12.6 %collective-permute-start.4 = (bf16[8,32,256]{2,1,0:T(8,128)(2,1)S(1)}, bf16[8,32,256]{2,1,0:T(8,128)(2,1)S(1)}, u32[]{:S(2)}, u32[]{:S(2)}) collective-permute-start(bf16[8,32,256]{2,1,0:T(8,128)(2,1)S(1)} %get-tuple-element.52), channel_id=1, source_target_pairs={{0,12},{1,13},{2,14},{3,15},{4,8},{5,9},{6,10},{7,11},{8,4},{9,5},... | collective-permute-start | bytes 393224 | tf_op jit(solution)/shard_map/ppermute | solution.py:288
  96.6 12.0 %collective-permute-start.23 = (f32[8,16,256]{2,1,0:T(8,128)S(1)}, f32[8,16,256]{2,1,0:T(8,128)S(1)}, u32[]{:S(2)}, u32[]{:S(2)}) collective-permute-start(f32[8,16,256]{2,1,0:T(8,128)S(1)} %get-tuple-element.84), channel_id=1, source_target_pairs={{0,1},{1,0},{2,3},{3,2},{4,5},{5,4},{6,7},{7,6},{8,9},{9,8},{10,11... | collective-permute-start | bytes 393224 | tf_op jit(solution)/shard_map/ppermute | solution.py:288
  96.7 11.9 %collective-permute-start.22 = (f32[8,16,256]{2,1,0:T(8,128)S(1)}, f32[8,16,256]{2,1,0:T(8,128)S(1)}, u32[]{:S(2)}, u32[]{:S(2)}) collective-permute-start(f32[8,16,256]{2,1,0:T(8,128)S(1)} %get-tuple-element.83), channel_id=1, source_target_pairs={{0,1},{1,0},{2,3},{3,2},{4,5},{5,4},{6,7},{7,6},{8,9},{9,8},{10,11... | collective-permute-start | bytes 393224 | tf_op jit(solution)/shard_map/ppermute | solution.py:288
  97.9 10.8 %collective-permute-start.21 = (f32[8,16,256]{2,1,0:T(8,128)S(1)}, f32[8,16,256]{2,1,0:T(8,128)S(1)}, u32[]{:S(2)}, u32[]{:S(2)}) collective-permute-start(f32[8,16,256]{2,1,0:T(8,128)S(1)} %get-tuple-element.82), channel_id=1, source_target_pairs={{0,1},{1,0},{2,3},{3,2},{4,5},{5,4},{6,7},{7,6},{8,9},{9,8},{10,11... | collective-permute-start | bytes 393224 | tf_op jit(solution)/shard_map/ppermute | solution.py:288
  107.0 1.6 %collective-permute-start.20 = (f32[8,16,256]{2,1,0:T(8,128)S(1)}, f32[8,16,256]{2,1,0:T(8,128)S(1)}, u32[]{:S(2)}, u32[]{:S(2)}) collective-permute-start(f32[8,16,256]{2,1,0:T(8,128)S(1)} %get-tuple-element.81), channel_id=1, source_target_pairs={{0,1},{1,0},{2,3},{3,2},{4,5},{5,4},{6,7},{7,6},{8,9},{9,8},{10,11... | collective-permute-start | bytes 393224 | tf_op jit(solution)/shard_map/ppermute | solution.py:288

commit v2 on v1

v2 whole, which is shorter than its diff:
```python
import functools

import jax
import jax.numpy as jnp
from jax import lax
from jax.experimental import pallas as pl
from jax.experimental.pallas import tpu as pltpu
from jax.sharding import PartitionSpec as P

f32 = jnp.float32
bf16 = jnp.bfloat16
LANES = 128
EPS = 1e-05
VMEM_BYTES = 12 * 2**20
PROJECT_ROWS = 16


def whole(shape):
    return pl.BlockSpec(shape, lambda *_: (0,) * len(shape))


def call(body, grid, in_specs, out_specs, out_shape, scratch, cost, operands, after=(), vmem=VMEM_BYTES):
    count = len(operands)
    extra = len(after)

    def run(*refs):
        return body(*refs[:count], *refs[count + extra :])

    return pl.pallas_call(
        run,
        grid_spec=pltpu.PrefetchScalarGridSpec(
            num_scalar_prefetch=1,
            grid=grid,
            in_specs=list(in_specs) + [pl.BlockSpec(memory_space=pl.ANY)] * extra,
            out_specs=out_specs,
            scratch_shapes=scratch,
        ),
        out_shape=out_shape,
        compiler_params=pltpu.CompilerParams(vmem_limit_bytes=vmem),
        cost_estimate=pl.CostEstimate(flops=cost[0], bytes_accessed=cost[1], transcendentals=0),
    )(*operands, *after)


def norm_columns(tile, gain, bias):
    count = tile.shape[0]
    mean_val = jnp.sum(tile, axis=0, keepdims=True) * (1.0 / count)
    centered = tile - mean_val
    variance = jnp.sum(centered * centered, axis=0, keepdims=True) * (1.0 / count)
    return (centered * lax.rsqrt(variance + EPS) * gain + bias).astype(bf16)


def gather_weights(w_ref, wt_ref, first, size):
    hidden = w_ref.shape[1] // 4
    half = hidden // 2
    turned = w_ref[...].astype(f32).T * 0.5
    row = 0
    for value in range(2):
        for side in range(2):
            for part in range(2):
                low = (2 * side + value) * hidden + part * half + first
                wt_ref[row : row + size, :] = turned[low : low + size]
                row += size


def turn_affine(gain_ref, bias_ref, affine_ref):
    chan = gain_ref.shape[1]
    affine_ref[0] = jnp.broadcast_to(gain_ref[...], (LANES, chan)).T
    affine_ref[1] = jnp.broadcast_to(bias_ref[...], (LANES, chan)).T


def normed_row(x_ref, affine_ref, k):
    parts = [
        norm_columns(x_ref[k, low : low + LANES, :].T.astype(f32), affine_ref[0], affine_ref[1])
        for low in range(0, x_ref.shape[1], LANES)
    ]
    return jnp.concatenate(parts, axis=1)


def project_body(chunks, first, stride, place, x_ref, mask_ref, gain_ref, bias_ref, w_ref, *rest):
    count = len(chunks)
    outs, (hold, wt_ref, affine_ref) = (rest[:count], rest[count : 2 * count]), rest[2 * count :]
    rows, width, _ = x_ref.shape
    size = sum(chunks)

    @pl.when(pl.program_id(0) == 0)
    def _():
        gather_weights(w_ref, wt_ref, first, size)
        turn_affine(gain_ref, bias_ref, affine_ref)

    weights = wt_ref[...].astype(bf16)
    for k in range(rows):
        proj = jnp.dot(weights, normed_row(x_ref, affine_ref, k), preferred_element_type=f32)
        keep = mask_ref[pl.ds(k, 1), :].astype(f32)
        act = (jnp.tanh(proj[: 4 * size]) + 1.0) * proj[4 * size :] * keep
        for lane in range(width // LANES):
            hold[lane, pl.ds(k * stride, 4 * size), :] = act[:, lane * LANES : (lane + 1) * LANES]
    for owner in range(2):
        base = jnp.where(place[2] == owner, 0, size)
        offset = 0
        for out, count in zip(outs[owner], chunks):
            for side in range(2):
                for h in range(count):
                    for lane in range(width // LANES):
                        start = base + 2 * side * size + offset + h
                        tile = hold[lane, pl.ds(start, rows, stride=stride), :]
                        out[side, h, :, lane * LANES : (lane + 1) * LANES] = tile.astype(bf16)
            offset += count


def project(place, x, mask, gain, bias, w_proj, chunks, first, vmem, after):
    depth, width, chan = x.shape
    rows, size = PROJECT_ROWS, sum(chunks)
    stride = 4 * size + 8
    return call(
        functools.partial(project_body, chunks, first, stride),
        (depth // rows,),
        [
            pl.BlockSpec((rows, width, chan), lambda i, _: (i, 0, 0)),
            pl.BlockSpec((rows, width), lambda i, _: (i, 0)),
            whole((1, chan)),
            whole((1, chan)),
            whole(w_proj.shape),
        ],
        [pl.BlockSpec((2, size, rows, width), lambda i, _: (0, 0, i, 0)) for size in chunks] * 2,
        [jax.ShapeDtypeStruct((2, size, depth, width), bf16) for size in chunks] * 2,
        [
            pltpu.VMEM((width // LANES, rows * stride, LANES), f32),
            pltpu.VMEM((8 * size, chan), f32),
            pltpu.VMEM((2, chan, LANES), f32),
        ],
        (2 * depth * width * chan * 8 * size, 4 * depth * width * chan),
        (place, x, mask, gain.reshape(1, chan), bias.reshape(1, chan), w_proj),
        after,
        vmem,
    )


def gate_body(place, x_ref, gain_ref, bias_ref, w_ref, out_ref, affine_ref):
    @pl.when(pl.program_id(0) == 0)
    def _():
        turn_affine(gain_ref, bias_ref, affine_ref)

    weights = w_ref[...]
    for k in range(x_ref.shape[0]):
        normed = normed_row(x_ref, affine_ref, k)
        proj = lax.dot_general(normed, weights, (((0,), (0,)), ((), ())), preferred_element_type=f32)
        out_ref[k] = 0.5 * jnp.tanh(0.5 * proj) + 0.5


def gate(place, x, gain, bias, w_gate, rows, after):
    _, width, chan = x.shape
    step = 8
    spec = pl.BlockSpec((step, width, chan), lambda i, _: (i, 0, 0))
    return call(
        gate_body,
        (rows // step,),
        [spec, whole((1, chan)), whole((1, chan)), whole(w_gate.shape)],
        spec,
        jax.ShapeDtypeStruct((rows, width, chan), f32),
        [pltpu.VMEM((2, chan, LANES), f32)],
        (2 * rows * width * chan * chan, 6 * rows * width * chan),
        (place, x, gain.reshape(1, chan), bias.reshape(1, chan), w_gate),
        after,
    )


def triangle_body(order, place, own_ref, got_ref, keep_ref, send_ref, hold):
    step, slots, block, _ = keep_ref.shape
    for h in range(step):
        left = jnp.concatenate([own_ref[0, h], got_ref[0, h]], axis=0)
        right = jnp.concatenate([own_ref[1, h], got_ref[1, h]], axis=0)
        hold[h] = lax.dot_general(left, right, (((0,), (0,)), ((), ())), preferred_element_type=f32)
        for slot in range(2 * slots):
            mask = 0
            for digit, bit in enumerate(reversed(order)):
                mask |= (slot >> digit & 1) << bit
            rows = pl.ds(pl.multiple_of((place[1] ^ mask) * block, block), block)
            if slot < slots:
                keep_ref[h, slot] = hold[h, rows, :]
            else:
                send_ref[h, slot - slots] = hold[h, rows, :].astype(bf16)


def triangle(place, own, got, order, after):
    _, size, depth, width = own.shape
    step = min(size, 4)
    slots = 2 ** (len(order) - 1)
    block = width // (2 * slots)
    spec = pl.BlockSpec((2, step, depth, width), lambda i, _: (0, i, 0, 0))
    out_spec = pl.BlockSpec((step, slots, block, width), lambda i, _: (i, 0, 0, 0))
    shape = (size, slots, block, width)
    return call(
        functools.partial(triangle_body, order),
        (size // step,),
        [spec, spec],
        [out_spec, out_spec],
        [jax.ShapeDtypeStruct(shape, f32), jax.ShapeDtypeStruct(shape, bf16)],
        [pltpu.VMEM((step, width, width), f32)],
        (4 * size * depth * width * width, 8 * size * depth * width + 3 * size * width * width),
        (place, own, got),
        after,
    )


def halve_body(place, held_ref, got_ref, keep_ref, send_ref):
    slots = keep_ref.shape[1]
    keep_ref[...] = held_ref[:, :slots] + got_ref[:, :slots].astype(f32)
    send_ref[...] = (held_ref[:, slots:] + got_ref[:, slots:].astype(f32)).astype(bf16)


def halve(place, held, got, after):
    size, slots, block, width = held.shape
    step = min(size, 4)
    spec = pl.BlockSpec((step, slots, block, width), lambda i, _: (i, 0, 0, 0))
    out_spec = pl.BlockSpec((step, slots // 2, block, width), lambda i, _: (i, 0, 0, 0))
    shape = (size, slots // 2, block, width)
    return call(
        halve_body,
        (size // step,),
        [spec, spec],
        [out_spec, out_spec],
        [jax.ShapeDtypeStruct(shape, f32), jax.ShapeDtypeStruct(shape, bf16)],
        [],
        (held.size, held.size * 9),
        (place, held, got),
        after,
    )


def total_body(place, held_ref, got_ref, mine_ref, theirs_ref, hold):
    hold[...] = held_ref[:, 0] + got_ref[:, 0].astype(f32)
    rows = mine_ref.shape[1]
    core = place[2]
    mine_ref[...] = hold[:, pl.ds(pl.multiple_of(core * rows, rows), rows), :]
    theirs_ref[...] = hold[:, pl.ds(pl.multiple_of((1 - core) * rows, rows), rows), :]


def total(place, held, got, after):
    size, _, block, width = held.shape
    spec = pl.BlockSpec((size, 1, block, width), lambda i, _: (i, 0, 0, 0))
    out_spec = pl.BlockSpec((size, block // 2, width), lambda i, _: (i, 0, 0))
    shape = jax.ShapeDtypeStruct((size, block // 2, width), f32)
    return call(
        total_body,
        (1,),
        [spec, spec],
        [out_spec] * 2,
        [shape, shape],
        [pltpu.VMEM((size, block, width), f32)],
        (held.size, held.size * 10),
        (place, held, got),
        after,
    )


def finish_body(chunks, place, *refs):
    count = len(chunks)
    mine, theirs = refs[:count], refs[count : 2 * count]
    gate_ref, gain_ref, bias_ref, w_ref, out_ref, hold = refs[2 * count :]
    hidden, _ = w_ref.shape
    half = hidden // 2
    _, rows, width = mine[0].shape
    stride = hold.shape[1] // hidden
    core = place[2]
    total_val = jnp.zeros((rows, width), f32)
    for part in mine + theirs:
        total_val = total_val + jnp.sum(part[...], axis=0)
    mean_val = total_val * (1.0 / hidden)
    square = jnp.zeros((rows, width), f32)
    for part in mine + theirs:
        for h in range(part.shape[0]):
            centered = part[h] - mean_val
            square = square + centered * centered
    scale = lax.rsqrt(square * (1.0 / hidden) + EPS)
    for owner, parts in ((0, mine), (1, theirs)):
        index = jnp.where(core == owner, 0, half)
        for part in parts:
            for h in range(part.shape[0]):
                value = (part[h] - mean_val) * scale * gain_ref[index] + bias_ref[index]
                for lane in range(width // LANES):
                    hold[lane, pl.ds(index * stride, rows), :] = value[:, lane * LANES : (lane + 1) * LANES]
                index = index + 1
    weights = w_ref[...]
    for row in range(rows):
        for lane in range(width // LANES):
            normed = hold[lane, pl.ds(row, hidden, stride=stride), :].astype(bf16)
            mixed = lax.dot_general(normed, weights, (((0,), (0,)), ((), ())), preferred_element_type=f32)
            span = pl.ds(lane * LANES, LANES)
            out_ref[row, span, :] = (gate_ref[row, span, :] * mixed).astype(bf16)


def finish(place, mine, theirs, gate_act, gain, bias, w_out):
    rows, width, chan = gate_act.shape
    hidden = w_out.shape[0]
    step = 8
    stride = step + 8
    parts = [pl.BlockSpec((part.shape[0], step, width), lambda i, _: (0, i, 0)) for part in mine]
    spec = pl.BlockSpec((step, width, chan), lambda i, _: (i, 0, 0))
    smem = pl.BlockSpec(memory_space=pltpu.SMEM)
    return call(
        functools.partial(finish_body, [part.shape[0] for part in mine]),
        (rows // step,),
        parts * 2 + [spec, smem, smem, whole(w_out.shape)],
        spec,
        jax.ShapeDtypeStruct((rows, width, chan), bf16),
        [pltpu.VMEM((width // LANES, hidden * stride, LANES), f32)],
        (2 * rows * width * chan * hidden, rows * width * (chan * 6 + hidden * 4)),
        (place, *mine, *theirs, gate_act, gain, bias, w_out),
    )


def event_order(sizes, orders, bits):
    links, order, flying = {}, [], []
    waiting = list(range(len(sizes)))

    def send(chunk, step, time):
        bit = orders[chunk][step]
        load = sizes[chunk] / 2**step
        link = min(bit, 1)
        begin = max(time, links.get(link, 0.0))
        links[link] = begin + load * max(bit, 1)
        flying.append((links[link] + 2.0, chunk, step))

    while waiting or flying:
        for chunk in [c for c in waiting if c < 2]:
            waiting.remove(chunk)
            order.append((chunk, 0))
            send(chunk, 0, 0.0)
        flying.sort()
        time, chunk, step = flying.pop(0)
        order.append((chunk, step + 1))
        if step + 1 < bits:
            send(chunk, step + 1, time + 2.0)
        if step == 0 and waiting:
            follower = waiting.pop(0)
            order.append((follower, 0))
            send(follower, 0, time + 2.0)
    return order


def on_device(pair_act, pair_mask, in_gain, in_bias, w_proj, w_gate, out_gain, out_bias, w_out):
    width = pair_act.shape[1]
    devices = lax.axis_size("row")
    bits = (devices // 2).bit_length() - 1
    half = w_out.shape[0] // 2
    chunks = (half // 4, half // 8, half // 4, half // 4, half // 8)
    z_last, z_first = tuple(range(bits)), tuple(range(1, bits)) + (0,)
    orders = tuple(z_first if c == 1 else z_last for c in range(len(chunks)))
    index = lax.axis_index("row")
    place = jnp.stack([index, index // 2, index % 2]).astype(jnp.int32)

    def swap(values, bit):
        return lax.ppermute(values, "row", [(d, d ^ bit) for d in range(devices)])

    last = []

    def put(kernel, *operands):
        outs = kernel(*operands, tuple(last[-1:]))
        last.append(outs[0] if isinstance(outs, (list, tuple)) else outs)
        return outs

    acts = put(project, place, pair_act, pair_mask, in_gain, in_bias, w_proj, chunks, 0, 56 * 2**20)
    count = len(chunks)
    own, got = acts[:count], [swap(part, 1) for part in acts[count:]]
    held, arrived = {}, {}

    def advance(chunk, step):
        if step == 0:
            held[chunk], sent = put(triangle, place, own[chunk], got[chunk], orders[chunk])
        elif step < bits:
            held[chunk], sent = put(halve, place, held[chunk], arrived[chunk])
        else:
            held[chunk], sent = put(total, place, held[chunk], arrived[chunk])
        arrived[chunk] = swap(sent, 2 << orders[chunk][step] if step < bits else 1)

    sizes = [11.4 * size / (half // 4) for size in chunks]
    for position, (chunk, step) in enumerate(event_order(sizes, orders, bits)):
        advance(chunk, step)
        if position == 1:
            gate_act = put(gate, place, pair_act, in_gain, in_bias, w_gate, width // devices)
    mine, theirs = [held[c] for c in range(count)], [arrived[c] for c in range(count)]
    return finish(place, mine, theirs, gate_act, out_gain, out_bias, w_out)


def solution(mesh):
    return jax.shard_map(
        on_device,
        mesh=mesh,
        in_specs=(
            P(("groups", "row"), None, None),
            P(("groups", "row"), None),
            P(),
            P(),
            P(),
            P(),
            P(),
            P(),
            P(),
        ),
        out_specs=P(("groups", "row"), None, None),
        check_vma=False,
    )
```

time: 113 us -> 91.4 us (0.81)
  waiting for transfers between devices: 42.2 us -> 28.8 us
  starting transfers between devices: 37.1 us -> 24.1 us
  Pallas kernels: 26.2 us -> 35.2 us
  local copies, waits for them, and re-layouts: 6.06 us -> 2.18 us
    ppermute x24 -> x25, waiting for transfers between devices: 42.2 us -> 28.8 us  [swap(): return lax.ppermute(values, 'row', [(d, d ^ bit) for d in range(devices)])]
    ppermute x24 -> x25, starting transfers between devices: 37.1 us -> 24.1 us  [swap(): return lax.ppermute(values, 'row', [(d, d ^ bit) for d in range(devices)])]
    pallas_call x15 -> x23, Pallas kernels: 26.2 us -> 35.2 us  [call(): pl.pallas_call(run, grid_spec=pltpu.PrefetchScalarGridSpec(num_scalar_pre...]
    unnamed x18 -> x28, local copies, waits for them, and re-layouts: 4.54 us -> 2.18 us
    reshape x2 -> x0, local copies, waits for them, and re-layouts: 1.52 us -> none  [the longest x1 0.76 us: project(): bias.reshape(chan, 1)]
  transfers between devices with their start and end apart: 24 -> 25, of which waited for: 7 -> 10; matrix products, arithmetic and copies ran while one was open for 0% -> 0% of each run, Pallas kernels for 9% -> 19%
where the time goes in v2:
time: 91.4 us; the launch traced here: 91.2 us
  Pallas kernels  35.2 us (39%)
  waiting for transfers between devices  28.8 us (32%)
  starting transfers between devices  24.1 us (26%)
  local copies, waits for them, and re-layouts  2.18 us (2%)
    pallas_call x23, Pallas kernels, call(): pl.pallas_call(run, grid_spec=pltpu.PrefetchScalarGridSpec(num_scalar_pre...  35.2 us
    ppermute x25, waiting for transfers between devices, swap(): return lax.ppermute(values, 'row', [(d, d ^ bit) for d in range(devices)])  28.8 us
    ppermute x25, starting transfers between devices, swap(): return lax.ppermute(values, 'row', [(d, d ^ bit) for d in range(devices)])  24.1 us
    unnamed x28, local copies, waits for them, and re-layouts  2.18 us
  transfers between devices with their start and end apart: 25, of which 10 were waited for; matrix products, arithmetic and copies ran while one was open for 0% of the time, Pallas kernels for 19%

profile of v2, /device:TPU:0, one launch (start us, length us, event | category | flops | bytes accessed | tf_op | source)
XLA Modules:
  0.0 91.2 jit_solution(13349045595430176296)
XLA Ops:
  0.0 0.7 pad_add_fusion.refs_0_
  0.7 14.4 %shard_map.91 = (bf16[2,8,96,256]{3,2,1,0:T(8,128)(2,1)}, bf16[2,4,96,256]{3,2,1,0:T(8,128)(2,1)}, bf16[2,8,96,256]{3,2,1,0:T(8,128)(2,1)}, bf16[2,8,96,256]{3,2...) custom-call(s32[3]{0:T(128)} %pad_add_fusion.refs_0_, ...), custom_call_target="tpu_custom_call" | custom-call | flops 1610612736 | bytes 12582912 | tf_op jit(solution)/shard_map/pallas_call | solution.py:29
  15.1 0.6 collective-permute-start
  16.2 1.5 %collective-permute-done.refs_2_ = bf16[2,8,96,256]{3,2,1,0:T(8,128)(2,1)S(1)} collective-permute-done((bf16[2,8,96,256]{3,2,1,0:T(8,128)(2,1)}, bf16[2,8,96,256]{3,2,1,0:T(8,128)(2,1)S(1)}, u32[]{:S(2)}, u32[]{:S(2)}) %collective-permute-start) | collective-permute-done | bytes 786464 | tf_op jit(solution)/shard_map/ppermute | solution.py:353
  17.7 1.1 %copy-done.1 = bf16[2,8,96,256]{3,2,1,0:T(8,128)(2,1)S(1)} copy-done((bf16[2,8,96,256]{3,2,1,0:T(8,128)(2,1)S(1)}, bf16[2,8,96,256]{3,2,1,0:T(8,128)(2,1)}, u32[]{:S(2)}) %copy-start.1) | copy-done | bytes 786456
  18.9 1.5 %shard_map.92 = (f32[8,4,32,256]{3,2,1,0:T(8,128)S(1)}, bf16[8,4,32,256]{3,2,1,0:T(8,128)(2,1)S(1)}) custom-call(s32[3]{0:T(128)S(1)} %copy-done.6, bf16[2,8,96,256]{3,2,1,0:T(8,128)(2,1)S(1)} %copy-done.1, bf16[2,8,96,256]{3,2,1,0:T(8,128)(2,1)S(1)} %collective-permute-done.refs_2_, bf16[2,8,96,256]{3,2,1,0:T(8,128)(2,1)S(1)} %copy-done.1), custom_call_target="tpu_custom_call" | custom-call | flops 201326592 | bytes 3145728 | tf_op jit(solution)/shard_map/pallas_call | solution.py:29
  20.4 3.0 %collective-permute-start.1 = (bf16[8,4,32,256]{3,2,1,0:T(8,128)(2,1)S(1)}, bf16[8,4,32,256]{3,2,1,0:T(8,128)(2,1)S(1)}, u32[]{:S(2)}, u32[]{:S(2)}) collective-permute-start(bf16[8,4,32,256]{3,2,1,0:T(8,128)(2,1)S(1)} %get-tuple-element.58), channel_id=1, source_target_pairs={{0,2},{1,3},{2,0},{3,1},{4,6},{5,7},{6,4},{7,5},{8,10},{9,11},{10,... | collective-permute-start | bytes 1572872 | tf_op jit(solution)/shard_map/ppermute | solution.py:353
  23.3 1.0 %copy-done.5 = bf16[2,4,96,256]{3,2,1,0:T(8,128)(2,1)S(1)} copy-done((bf16[2,4,96,256]{3,2,1,0:T(8,128)(2,1)S(1)}, bf16[2,4,96,256]{3,2,1,0:T(8,128)(2,1)}, u32[]{:S(2)}) %copy-start.5) | copy-done | bytes 393240
  24.3 0.9 %shard_map.93 = (f32[4,4,32,256]{3,2,1,0:T(8,128)S(1)}, bf16[4,4,32,256]{3,2,1,0:T(8,128)(2,1)S(1)}) custom-call(s32[3]{0:T(128)S(1)} %copy-done.6, bf16[2,4,96,256]{3,2,1,0:T(8,128)(2,1)S(1)} %copy-done.5, bf16[2,4,96,256]{3,2,1,0:T(8,128)(2,1)S(1)} %collective-permute-done.3.refs_2_, f32[8,4,32,256]{3,2,1,0:T(8,128)S(1)} %get-tuple-element.57.refs_3_.refs_1_), custom_call_target="tpu_custom_call" | custom-call | flops 100663296 | bytes 1572864 | tf_op jit(solution)/shard_map/pallas_call | solution.py:29
  25.3 1.7 %collective-permute-start.4 = (bf16[4,4,32,256]{3,2,1,0:T(8,128)(2,1)S(1)}, bf16[4,4,32,256]{3,2,1,0:T(8,128)(2,1)S(1)}, u32[]{:S(2)}, u32[]{:S(2)}) collective-permute-start(bf16[4,4,32,256]{3,2,1,0:T(8,128)(2,1)S(1)} %get-tuple-element.64), channel_id=1, source_target_pairs={{0,4},{1,5},{2,6},{3,7},{4,0},{5,1},{6,2},{7,3},{8,12},{9,13},{10,... | collective-permute-start | bytes 786440 | tf_op jit(solution)/shard_map/ppermute | solution.py:353
  27.0 2.1 %shard_map.94.refs_3_.refs_11_ = f32[16,256,128]{2,1,0:T(8,128)S(1)} custom-call(s32[3]{0:T(128)S(1)} %copy-done.6, bf16[96,256,128]{2,1,0:T(8,128)(2,1)S(1)} %copy-done, f32[1,128]{1,0:T(1,128)S(1)} %bitcast.6, f32[1,128]{1,0:T(1,128)S(1)} %bitcast.8, bf16[128,128]{1,0:T(8,128)(2,1)S(1)} %copy-done.7, f32[4,4,32,256]{3,2,1,0:T(8,128)S(1)} %get-tuple-element.63.refs_5_.refs_1_), custom_call_target="tpu_custom_call" | custom-call | flops 134217728 | bytes 3145728 | tf_op jit(solution)/shard_map/pallas_call | solution.py:29
  29.1 4.3 %collective-permute-done.4.refs_2_ = bf16[4,4,32,256]{3,2,1,0:T(8,128)(2,1)S(1)} collective-permute-done((bf16[4,4,32,256]{3,2,1,0:T(8,128)(2,1)S(1)}, bf16[4,4,32,256]{3,2,1,0:T(8,128)(2,1)S(1)}, u32[]{:S(2)}, u32[]{:S(2)}) %collective-permute-start.4) | collective-permute-done | bytes 262176 | tf_op jit(solution)/shard_map/ppermute | solution.py:353
  33.4 0.6 shard_map.95
  34.0 1.5 %shard_map.96 = (f32[8,4,32,256]{3,2,1,0:T(8,128)S(1)}, bf16[8,4,32,256]{3,2,1,0:T(8,128)(2,1)S(1)}) custom-call(s32[3]{0:T(128)S(1)} %copy-done.6, bf16[2,8,96,256]{3,2,1,0:T(8,128)(2,1)S(1)} %copy-done.3, bf16[2,8,96,256]{3,2,1,0:T(8,128)(2,1)S(1)} %collective-permute-done.2.refs_2_, f32[4,2,32,256]{3,2,1,0:T(8,128)S(1)} %get-tuple-element.65.refs_3_.refs_1_), custom_call_target="tpu_custom_call" | custom-call | flops 201326592 | bytes 3145728 | tf_op jit(solution)/shard_map/pallas_call | solution.py:29
  36.0 0.7 shard_map.97
  36.7 1.5 %shard_map.98 = (f32[8,4,32,256]{3,2,1,0:T(8,128)S(1)}, bf16[8,4,32,256]{3,2,1,0:T(8,128)(2,1)S(1)}) custom-call(s32[3]{0:T(128)S(1)} %copy-done.6, bf16[2,8,96,256]{3,2,1,0:T(8,128)(2,1)S(1)} %copy-done.2, bf16[2,8,96,256]{3,2,1,0:T(8,128)(2,1)S(1)} %collective-permute-done.7.refs_2_, f32[8,2,32,256]{3,2,1,0:T(8,128)S(1)} %get-tuple-element.67.refs_3_.refs_1_), custom_call_target="tpu_custom_call" | custom-call | flops 201326592 | bytes 3145728 | tf_op jit(solution)/shard_map/pallas_call | solution.py:29
  38.1 1.7 %collective-permute-start.12 = (bf16[8,4,32,256]{3,2,1,0:T(8,128)(2,1)S(1)}, bf16[8,4,32,256]{3,2,1,0:T(8,128)(2,1)S(1)}, u32[]{:S(2)}, u32[]{:S(2)}) collective-permute-start(bf16[8,4,32,256]{3,2,1,0:T(8,128)(2,1)S(1)} %get-tuple-element.83), channel_id=1, source_target_pairs={{0,2},{1,3},{2,0},{3,1},{4,6},{5,7},{6,4},{7,5},{8,10},{9,11},{10,... | collective-permute-start | bytes 1572872 | tf_op jit(solution)/shard_map/ppermute | solution.py:353
  39.8 1.6 %collective-permute-start.5 = (bf16[8,2,32,256]{3,2,1,0:T(8,128)(2,1)S(1)}, bf16[8,2,32,256]{3,2,1,0:T(8,128)(2,1)S(1)}, u32[]{:S(2)}, u32[]{:S(2)}) collective-permute-start(bf16[8,2,32,256]{3,2,1,0:T(8,128)(2,1)S(1)} %get-tuple-element.68), channel_id=1, source_target_pairs={{0,4},{1,5},{2,6},{3,7},{4,0},{5,1},{6,2},{7,3},{8,12},{9,13},{10,... | collective-permute-start | bytes 786440 | tf_op jit(solution)/shard_map/ppermute | solution.py:353
  41.5 2.6 %collective-permute-start.6 = (bf16[4,2,32,256]{3,2,1,0:T(8,128)(2,1)S(1)}, bf16[4,2,32,256]{3,2,1,0:T(8,128)(2,1)S(1)}, u32[]{:S(2)}, u32[]{:S(2)}) collective-permute-start(bf16[4,2,32,256]{3,2,1,0:T(8,128)(2,1)S(1)} %get-tuple-element.69), channel_id=1, source_target_pairs={{0,8},{1,9},{2,10},{3,11},{4,12},{5,13},{6,14},{7,15},{8,0},{9,1},... | collective-permute-start | bytes 393224 | tf_op jit(solution)/shard_map/ppermute | solution.py:353
  44.0 6.5 %collective-permute-done.6.refs_2_ = bf16[4,2,32,256]{3,2,1,0:T(8,128)(2,1)S(1)} collective-permute-done((bf16[4,2,32,256]{3,2,1,0:T(8,128)(2,1)S(1)}, bf16[4,2,32,256]{3,2,1,0:T(8,128)(2,1)S(1)}, u32[]{:S(2)}, u32[]{:S(2)}) %collective-permute-start.6) | collective-permute-done | bytes 131104 | tf_op jit(solution)/shard_map/ppermute | solution.py:353
  50.5 0.6 shard_map.99
  51.4 0.6 shard_map.100
  52.0 3.2 %collective-permute-start.8 = (bf16[8,1,32,256]{3,2,1,0:T(8,128)(2,1)S(1)}, bf16[8,1,32,256]{3,2,1,0:T(8,128)(2,1)S(1)}, u32[]{:S(2)}, u32[]{:S(2)}) collective-permute-start(bf16[8,1,32,256]{3,2,1,0:T(8,128)(2,1)S(1)} %get-tuple-element.75), channel_id=1, source_target_pairs={{0,8},{1,9},{2,10},{3,11},{4,12},{5,13},{6,14},{7,15},{8,0},{9,1},... | collective-permute-start | bytes 393224 | tf_op jit(solution)/shard_map/ppermute | solution.py:353
  55.2 0.7 shard_map.101
  55.9 1.1 %collective-permute-start.13 = (bf16[8,2,32,256]{3,2,1,0:T(8,128)(2,1)S(1)}, bf16[8,2,32,256]{3,2,1,0:T(8,128)(2,1)S(1)}, u32[]{:S(2)}, u32[]{:S(2)}) collective-permute-start(bf16[8,2,32,256]{3,2,1,0:T(8,128)(2,1)S(1)} %get-tuple-element.86), channel_id=1, source_target_pairs={{0,4},{1,5},{2,6},{3,7},{4,0},{5,1},{6,2},{7,3},{8,12},{9,13},{10,... | collective-permute-start | bytes 786440 | tf_op jit(solution)/shard_map/ppermute | solution.py:353
  57.0 0.9 %shard_map.102 = (f32[4,4,32,256]{3,2,1,0:T(8,128)S(1)}, bf16[4,4,32,256]{3,2,1,0:T(8,128)(2,1)S(1)}) custom-call(s32[3]{0:T(128)S(1)} %copy-done.6, bf16[2,4,96,256]{3,2,1,0:T(8,128)(2,1)S(1)} %copy-done.4, bf16[2,4,96,256]{3,2,1,0:T(8,128)(2,1)S(1)} %collective-permute-done.9.refs_2_, f32[8,2,32,256]{3,2,1,0:T(8,128)S(1)} %get-tuple-element.79.refs_3_.refs_1_), custom_call_target="tpu_custom_call" | custom-call | flops 100663296 | bytes 1572864 | tf_op jit(solution)/shard_map/pallas_call | solution.py:29
  57.9 0.6 collective-permute-start.16
  58.5 2.3 %collective-permute-done.8.refs_2_ = bf16[8,1,32,256]{3,2,1,0:T(8,128)(2,1)S(1)} collective-permute-done((bf16[8,1,32,256]{3,2,1,0:T(8,128)(2,1)S(1)}, bf16[8,1,32,256]{3,2,1,0:T(8,128)(2,1)S(1)}, u32[]{:S(2)}, u32[]{:S(2)}) %collective-permute-start.8) | collective-permute-done | bytes 131104 | tf_op jit(solution)/shard_map/ppermute | solution.py:353
  60.8 0.6 shard_map.103
  61.4 0.7 shard_map.104
  62.1 1.8 %collective-permute-start.15 = (bf16[8,2,32,256]{3,2,1,0:T(8,128)(2,1)S(1)}, bf16[8,2,32,256]{3,2,1,0:T(8,128)(2,1)S(1)}, u32[]{:S(2)}, u32[]{:S(2)}) collective-permute-start(bf16[8,2,32,256]{3,2,1,0:T(8,128)(2,1)S(1)} %get-tuple-element.89), channel_id=1, source_target_pairs={{0,4},{1,5},{2,6},{3,7},{4,0},{5,1},{6,2},{7,3},{8,12},{9,13},{10,... | collective-permute-start | bytes 786440 | tf_op jit(solution)/shard_map/ppermute | solution.py:353
  64.4 3.8 %collective-permute-done.11.refs_2_ = bf16[4,1,32,256]{3,2,1,0:T(8,128)(2,1)S(1)} collective-permute-done((bf16[4,1,32,256]{3,2,1,0:T(8,128)(2,1)S(1)}, bf16[4,1,32,256]{3,2,1,0:T(8,128)(2,1)S(1)}, u32[]{:S(2)}, u32[]{:S(2)}) %collective-permute-start.11) | collective-permute-done | bytes 65568 | tf_op jit(solution)/shard_map/ppermute | solution.py:353
  68.2 0.6 shard_map.105
  68.8 0.6 shard_map.106
  69.4 2.7 %collective-permute-start.14 = (bf16[8,1,32,256]{3,2,1,0:T(8,128)(2,1)S(1)}, bf16[8,1,32,256]{3,2,1,0:T(8,128)(2,1)S(1)}, u32[]{:S(2)}, u32[]{:S(2)}) collective-permute-start(bf16[8,1,32,256]{3,2,1,0:T(8,128)(2,1)S(1)} %get-tuple-element.88), channel_id=1, source_target_pairs={{0,8},{1,9},{2,10},{3,11},{4,12},{5,13},{6,14},{7,15},{8,0},{9,1},... | collective-permute-start | bytes 393224 | tf_op jit(solution)/shard_map/ppermute | solution.py:353
  72.1 0.6 shard_map.107
  72.9 0.6 shard_map.108
  73.5 0.5 collective-permute-start.17
  74.0 4.9 %collective-permute-done.14.refs_2_ = bf16[8,1,32,256]{3,2,1,0:T(8,128)(2,1)S(1)} collective-permute-done((bf16[8,1,32,256]{3,2,1,0:T(8,128)(2,1)S(1)}, bf16[8,1,32,256]{3,2,1,0:T(8,128)(2,1)S(1)}, u32[]{:S(2)}, u32[]{:S(2)}) %collective-permute-start.14) | collective-permute-done | bytes 131104 | tf_op jit(solution)/shard_map/ppermute | solution.py:353
  78.9 0.6 shard_map.109
  79.5 0.6 shard_map.110
  80.1 0.7 collective-permute-start.19
  80.8 3.1 %collective-permute-done.17.refs_2_ = bf16[8,1,32,256]{3,2,1,0:T(8,128)(2,1)S(1)} collective-permute-done((bf16[8,1,32,256]{3,2,1,0:T(8,128)(2,1)S(1)}, bf16[8,1,32,256]{3,2,1,0:T(8,128)(2,1)S(1)}, u32[]{:S(2)}, u32[]{:S(2)}) %collective-permute-start.17) | collective-permute-done | bytes 131104 | tf_op jit(solution)/shard_map/ppermute | solution.py:353
  83.9 0.6 shard_map.111
  85.1 0.9 %collective-permute-done.19.refs_2_ = bf16[4,1,32,256]{3,2,1,0:T(8,128)(2,1)S(1)} collective-permute-done((bf16[4,1,32,256]{3,2,1,0:T(8,128)(2,1)S(1)}, bf16[4,1,32,256]{3,2,1,0:T(8,128)(2,1)S(1)}, u32[]{:S(2)}, u32[]{:S(2)}) %collective-permute-start.19) | collective-permute-done | bytes 65568 | tf_op jit(solution)/shard_map/ppermute | solution.py:353
  86.0 0.6 shard_map.112
  86.7 1.2 %collective-permute-done.24.refs_10_ = f32[4,16,256]{2,1,0:T(8,128)S(1)} collective-permute-done((f32[4,16,256]{2,1,0:T(8,128)S(1)}, f32[4,16,256]{2,1,0:T(8,128)S(1)}, u32[]{:S(2)}, u32[]{:S(2)}) %collective-permute-start.24) | collective-permute-done | bytes 65568 | tf_op jit(solution)/shard_map/ppermute | solution.py:353
  87.9 3.3 %shard_map.113 = bf16[16,256,128]{2,1,0:T(8,128)(2,1)} custom-call(s32[3]{0:T(128)S(1)} %copy-done.6, f32[8,16,256]{2,1,0:T(8,128)S(1)} %get-tuple-element.81.refs_3_.refs_1_, f32[4,16,256]{2,1,0:T(8,128)S(1)} %get-tuple-element.85.refs_3_.refs_2_, f32[8,16,256]{2,1,0:T(8,128)S(1)} %get-tuple-element.93.refs_3_, ...), custom_call_target="tpu_custom_call" | custom-call | flops 67108864 | bytes 4194304 | tf_op jit(solution)/shard_map/pallas_call | solution.py:29
  (54 shorter events, 2.7 us)
Async XLA Ops:
  0.0 26.9 %copy-start.10 = (f32[128]{0:T(128)S(1)}, f32[128]{0:T(128)}, u32[]{:S(2)}) copy-start(f32[128]{0:T(128)} %param.12) | copy-start | bytes 1540
  0.0 26.9 %copy-start.9 = (f32[128]{0:T(128)S(1)}, f32[128]{0:T(128)}, u32[]{:S(2)}) copy-start(f32[128]{0:T(128)} %param.11) | copy-start | bytes 1540
  0.0 26.9 %copy-start.7 = (bf16[128,128]{1,0:T(8,128)(2,1)S(1)}, bf16[128,128]{1,0:T(8,128)(2,1)}, u32[]{:S(2)}) copy-start(bf16[128,128]{1,0:T(8,128)(2,1)} %refs_4_.1) | copy-start | bytes 98308
  0.0 26.9 %copy-start = (bf16[96,256,128]{2,1,0:T(8,128)(2,1)S(1)}, bf16[96,256,128]{2,1,0:T(8,128)(2,1)}, u32[]{:S(2)}) copy-start(bf16[96,256,128]{2,1,0:T(8,128)(2,1)} %refs_1_.3) | copy-start | bytes 18874372
  0.7 17.1 %copy-start.6 = (s32[3]{0:T(128)S(1)}, s32[3]{0:T(128)}, u32[]{:S(2)}) copy-start(s32[3]{0:T(128)} %pad_add_fusion.refs_0_) | copy-start | bytes 40
  15.1 2.7 %collective-permute-start = (bf16[2,8,96,256]{3,2,1,0:T(8,128)(2,1)}, bf16[2,8,96,256]{3,2,1,0:T(8,128)(2,1)S(1)}, u32[]{:S(2)}, u32[]{:S(2)}) collective-permute-start(bf16[2,8,96,256]{3,2,1,0:T(8,128)(2,1)} %get-tuple-element.56), channel_id=1, source_target_pairs={{0,1},{1,0},{2,3},{3,2},{4,5},{5,4},{6,7},{7,6},{8,9},{9,8},{10,11... | collective-permute-start | bytes 2359304 | tf_op jit(solution)/shard_map/ppermute | solution.py:353
  15.6 18.4 %collective-permute-start.2 = (bf16[2,8,96,256]{3,2,1,0:T(8,128)(2,1)}, bf16[2,8,96,256]{3,2,1,0:T(8,128)(2,1)S(1)}, u32[]{:S(2)}, u32[]{:S(2)}) collective-permute-start(bf16[2,8,96,256]{3,2,1,0:T(8,128)(2,1)} %get-tuple-element.60), channel_id=1, source_target_pairs={{0,1},{1,0},{2,3},{3,2},{4,5},{5,4},{6,7},{7,6},{8,9},{9,8},{10,11... | collective-permute-start | bytes 2359304 | tf_op jit(solution)/shard_map/ppermute | solution.py:353
  15.7 21.0 %collective-permute-start.7 = (bf16[2,8,96,256]{3,2,1,0:T(8,128)(2,1)}, bf16[2,8,96,256]{3,2,1,0:T(8,128)(2,1)S(1)}, u32[]{:S(2)}, u32[]{:S(2)}) collective-permute-start(bf16[2,8,96,256]{3,2,1,0:T(8,128)(2,1)} %get-tuple-element.71), channel_id=1, source_target_pairs={{0,1},{1,0},{2,3},{3,2},{4,5},{5,4},{6,7},{7,6},{8,9},{9,8},{10,11... | collective-permute-start | bytes 2359304 | tf_op jit(solution)/shard_map/ppermute | solution.py:353
  16.1 7.2 %collective-permute-start.3 = (bf16[2,4,96,256]{3,2,1,0:T(8,128)(2,1)}, bf16[2,4,96,256]{3,2,1,0:T(8,128)(2,1)S(1)}, u32[]{:S(2)}, u32[]{:S(2)}) collective-permute-start(bf16[2,4,96,256]{3,2,1,0:T(8,128)(2,1)} %get-tuple-element.62), channel_id=1, source_target_pairs={{0,1},{1,0},{2,3},{3,2},{4,5},{5,4},{6,7},{7,6},{8,9},{9,8},{10,11... | collective-permute-start | bytes 1179656 | tf_op jit(solution)/shard_map/ppermute | solution.py:353
  17.7 1.1 %copy-start.1 = (bf16[2,8,96,256]{3,2,1,0:T(8,128)(2,1)S(1)}, bf16[2,8,96,256]{3,2,1,0:T(8,128)(2,1)}, u32[]{:S(2)}) copy-start(bf16[2,8,96,256]{3,2,1,0:T(8,128)(2,1)} %get-tuple-element.55.refs_1_.refs_3_) | copy-start | bytes 2359300
  20.4 15.6 %collective-permute-start.1 = (bf16[8,4,32,256]{3,2,1,0:T(8,128)(2,1)S(1)}, bf16[8,4,32,256]{3,2,1,0:T(8,128)(2,1)S(1)}, u32[]{:S(2)}, u32[]{:S(2)}) collective-permute-start(bf16[8,4,32,256]{3,2,1,0:T(8,128)(2,1)S(1)} %get-tuple-element.58), channel_id=1, source_target_pairs={{0,2},{1,3},{2,0},{3,1},{4,6},{5,7},{6,4},{7,5},{8,10},{9,11},{10,... | collective-permute-start | bytes 1572872 | tf_op jit(solution)/shard_map/ppermute | solution.py:353
  23.3 1.0 %copy-start.5 = (bf16[2,4,96,256]{3,2,1,0:T(8,128)(2,1)S(1)}, bf16[2,4,96,256]{3,2,1,0:T(8,128)(2,1)}, u32[]{:S(2)}) copy-start(bf16[2,4,96,256]{3,2,1,0:T(8,128)(2,1)} %get-tuple-element.61.refs_1_) | copy-start | bytes 1179652
  25.2 8.7 %copy-start.3 = (bf16[2,8,96,256]{3,2,1,0:T(8,128)(2,1)S(1)}, bf16[2,8,96,256]{3,2,1,0:T(8,128)(2,1)}, u32[]{:S(2)}) copy-start(bf16[2,8,96,256]{3,2,1,0:T(8,128)(2,1)} %get-tuple-element.59.refs_1_) | copy-start | bytes 2359300
  25.3 8.1 %collective-permute-start.4 = (bf16[4,4,32,256]{3,2,1,0:T(8,128)(2,1)S(1)}, bf16[4,4,32,256]{3,2,1,0:T(8,128)(2,1)S(1)}, u32[]{:S(2)}, u32[]{:S(2)}) collective-permute-start(bf16[4,4,32,256]{3,2,1,0:T(8,128)(2,1)S(1)} %get-tuple-element.64), channel_id=1, source_target_pairs={{0,4},{1,5},{2,6},{3,7},{4,0},{5,1},{6,2},{7,3},{8,12},{9,13},{10,... | collective-permute-start | bytes 786440 | tf_op jit(solution)/shard_map/ppermute | solution.py:353
  27.0 9.7 %copy-start.2 = (bf16[2,8,96,256]{3,2,1,0:T(8,128)(2,1)S(1)}, bf16[2,8,96,256]{3,2,1,0:T(8,128)(2,1)}, u32[]{:S(2)}) copy-start(bf16[2,8,96,256]{3,2,1,0:T(8,128)(2,1)} %get-tuple-element.70.refs_1_) | copy-start | bytes 2359300
  29.1 10.8 %copy-start.13 = (bf16[2,4,96,256]{3,2,1,0:T(8,128)(2,1)S(1)}, bf16[2,4,96,256]{3,2,1,0:T(8,128)(2,1)}, u32[]{:S(2)}) copy-start(bf16[2,4,96,256]{3,2,1,0:T(8,128)(2,1)} %get-tuple-element.77) | copy-start | bytes 1179652
  29.1 27.9 %copy-start.4 = (bf16[2,4,96,256]{3,2,1,0:T(8,128)(2,1)S(1)}, bf16[2,4,96,256]{3,2,1,0:T(8,128)(2,1)}, u32[]{:S(2)}) copy-start(bf16[2,4,96,256]{3,2,1,0:T(8,128)(2,1)} %get-tuple-element.76.refs_1_) | copy-start | bytes 1179652
  35.5 19.7 %collective-permute-start.10 = (bf16[8,4,32,256]{3,2,1,0:T(8,128)(2,1)S(1)}, bf16[8,4,32,256]{3,2,1,0:T(8,128)(2,1)S(1)}, u32[]{:S(2)}, u32[]{:S(2)}) collective-permute-start(bf16[8,4,32,256]{3,2,1,0:T(8,128)(2,1)S(1)} %get-tuple-element.78), channel_id=1, source_target_pairs={{0,2},{1,3},{2,0},{3,1},{4,6},{5,7},{6,4},{7,5},{8,10},{9,11},{10,... | collective-permute-start | bytes 1572872 | tf_op jit(solution)/shard_map/ppermute | solution.py:353
  38.1 23.3 %collective-permute-start.12 = (bf16[8,4,32,256]{3,2,1,0:T(8,128)(2,1)S(1)}, bf16[8,4,32,256]{3,2,1,0:T(8,128)(2,1)S(1)}, u32[]{:S(2)}, u32[]{:S(2)}) collective-permute-start(bf16[8,4,32,256]{3,2,1,0:T(8,128)(2,1)S(1)} %get-tuple-element.83), channel_id=1, source_target_pairs={{0,2},{1,3},{2,0},{3,1},{4,6},{5,7},{6,4},{7,5},{8,10},{9,11},{10,... | collective-permute-start | bytes 1572872 | tf_op jit(solution)/shard_map/ppermute | solution.py:353
  39.8 17.2 %collective-permute-start.9 = (bf16[2,4,96,256]{3,2,1,0:T(8,128)(2,1)S(1)}, bf16[2,4,96,256]{3,2,1,0:T(8,128)(2,1)S(1)}, u32[]{:S(2)}, u32[]{:S(2)}) collective-permute-start(bf16[2,4,96,256]{3,2,1,0:T(8,128)(2,1)S(1)} %copy-done.13), channel_id=1, source_target_pairs={{0,1},{1,0},{2,3},{3,2},{4,5},{5,4},{6,7},{7,6},{8,9},{9,8},{10,11... | collective-permute-start | bytes 1179656 | tf_op jit(solution)/shard_map/ppermute | solution.py:353
  39.8 11.5 %collective-permute-start.5 = (bf16[8,2,32,256]{3,2,1,0:T(8,128)(2,1)S(1)}, bf16[8,2,32,256]{3,2,1,0:T(8,128)(2,1)S(1)}, u32[]{:S(2)}, u32[]{:S(2)}) collective-permute-start(bf16[8,2,32,256]{3,2,1,0:T(8,128)(2,1)S(1)} %get-tuple-element.68), channel_id=1, source_target_pairs={{0,4},{1,5},{2,6},{3,7},{4,0},{5,1},{6,2},{7,3},{8,12},{9,13},{10,... | collective-permute-start | bytes 786440 | tf_op jit(solution)/shard_map/ppermute | solution.py:353
  41.5 9.0 %collective-permute-start.6 = (bf16[4,2,32,256]{3,2,1,0:T(8,128)(2,1)S(1)}, bf16[4,2,32,256]{3,2,1,0:T(8,128)(2,1)S(1)}, u32[]{:S(2)}, u32[]{:S(2)}) collective-permute-start(bf16[4,2,32,256]{3,2,1,0:T(8,128)(2,1)S(1)} %get-tuple-element.69), channel_id=1, source_target_pairs={{0,8},{1,9},{2,10},{3,11},{4,12},{5,13},{6,14},{7,15},{8,0},{9,1},... | collective-permute-start | bytes 393224 | tf_op jit(solution)/shard_map/ppermute | solution.py:353
  51.1 36.8 %copy-start.8 = (bf16[64,128]{1,0:T(8,128)(2,1)S(1)}, bf16[64,128]{1,0:T(8,128)(2,1)}, u32[]{:S(2)}) copy-start(bf16[64,128]{1,0:T(8,128)(2,1)} %refs_14_.1) | copy-start | bytes 49156
  51.1 36.8 %copy-start.11 = (f32[64]{0:T(128)S(1)}, f32[64]{0:T(128)}, u32[]{:S(2)}) copy-start(f32[64]{0:T(128)} %refs_12_.1) | copy-start | bytes 772
  51.1 36.8 %copy-start.12 = (f32[64]{0:T(128)S(1)}, f32[64]{0:T(128)}, u32[]{:S(2)}) copy-start(f32[64]{0:T(128)} %refs_13_.1) | copy-start | bytes 772
  52.0 8.8 %collective-permute-start.8 = (bf16[8,1,32,256]{3,2,1,0:T(8,128)(2,1)S(1)}, bf16[8,1,32,256]{3,2,1,0:T(8,128)(2,1)S(1)}, u32[]{:S(2)}, u32[]{:S(2)}) collective-permute-start(bf16[8,1,32,256]{3,2,1,0:T(8,128)(2,1)S(1)} %get-tuple-element.75), channel_id=1, source_target_pairs={{0,8},{1,9},{2,10},{3,11},{4,12},{5,13},{6,14},{7,15},{8,0},{9,1},... | collective-permute-start | bytes 393224 | tf_op jit(solution)/shard_map/ppermute | solution.py:353
  55.9 12.9 %collective-permute-start.13 = (bf16[8,2,32,256]{3,2,1,0:T(8,128)(2,1)S(1)}, bf16[8,2,32,256]{3,2,1,0:T(8,128)(2,1)S(1)}, u32[]{:S(2)}, u32[]{:S(2)}) collective-permute-start(bf16[8,2,32,256]{3,2,1,0:T(8,128)(2,1)S(1)} %get-tuple-element.86), channel_id=1, source_target_pairs={{0,4},{1,5},{2,6},{3,7},{4,0},{5,1},{6,2},{7,3},{8,12},{9,13},{10,... | collective-permute-start | bytes 786440 | tf_op jit(solution)/shard_map/ppermute | solution.py:353
  57.9 14.2 %collective-permute-start.16 = (bf16[4,4,32,256]{3,2,1,0:T(8,128)(2,1)S(1)}, bf16[4,4,32,256]{3,2,1,0:T(8,128)(2,1)S(1)}, u32[]{:S(2)}, u32[]{:S(2)}) collective-permute-start(bf16[4,4,32,256]{3,2,1,0:T(8,128)(2,1)S(1)} %get-tuple-element.90), channel_id=1, source_target_pairs={{0,2},{1,3},{2,0},{3,1},{4,6},{5,7},{6,4},{7,5},{8,10},{9,11},{10,... | collective-permute-start | bytes 786440 | tf_op jit(solution)/shard_map/ppermute | solution.py:353
  62.1 10.8 %collective-permute-start.15 = (bf16[8,2,32,256]{3,2,1,0:T(8,128)(2,1)S(1)}, bf16[8,2,32,256]{3,2,1,0:T(8,128)(2,1)S(1)}, u32[]{:S(2)}, u32[]{:S(2)}) collective-permute-start(bf16[8,2,32,256]{3,2,1,0:T(8,128)(2,1)S(1)} %get-tuple-element.89), channel_id=1, source_target_pairs={{0,4},{1,5},{2,6},{3,7},{4,0},{5,1},{6,2},{7,3},{8,12},{9,13},{10,... | collective-permute-start | bytes 786440 | tf_op jit(solution)/shard_map/ppermute | solution.py:353
  63.9 4.3 %collective-permute-start.11 = (bf16[4,1,32,256]{3,2,1,0:T(8,128)(2,1)S(1)}, bf16[4,1,32,256]{3,2,1,0:T(8,128)(2,1)S(1)}, u32[]{:S(2)}, u32[]{:S(2)}) collective-permute-start(bf16[4,1,32,256]{3,2,1,0:T(8,128)(2,1)S(1)} %get-tuple-element.82), channel_id=1, source_target_pairs={{0,2},{1,3},{2,0},{3,1},{4,6},{5,7},{6,4},{7,5},{8,10},{9,11},{10,... | collective-permute-start | bytes 196616 | tf_op jit(solution)/shard_map/ppermute | solution.py:353
  69.4 9.5 %collective-permute-start.14 = (bf16[8,1,32,256]{3,2,1,0:T(8,128)(2,1)S(1)}, bf16[8,1,32,256]{3,2,1,0:T(8,128)(2,1)S(1)}, u32[]{:S(2)}, u32[]{:S(2)}) collective-permute-start(bf16[8,1,32,256]{3,2,1,0:T(8,128)(2,1)S(1)} %get-tuple-element.88), channel_id=1, source_target_pairs={{0,8},{1,9},{2,10},{3,11},{4,12},{5,13},{6,14},{7,15},{8,0},{9,1},... | collective-permute-start | bytes 393224 | tf_op jit(solution)/shard_map/ppermute | solution.py:353
  72.7 6.8 %collective-permute-start.18 = (bf16[4,2,32,256]{3,2,1,0:T(8,128)(2,1)S(1)}, bf16[4,2,32,256]{3,2,1,0:T(8,128)(2,1)S(1)}, u32[]{:S(2)}, u32[]{:S(2)}) collective-permute-start(bf16[4,2,32,256]{3,2,1,0:T(8,128)(2,1)S(1)} %get-tuple-element.95), channel_id=1, source_target_pairs={{0,4},{1,5},{2,6},{3,7},{4,0},{5,1},{6,2},{7,3},{8,12},{9,13},{10,... | collective-permute-start | bytes 393224 | tf_op jit(solution)/shard_map/ppermute | solution.py:353
  73.5 10.4 %collective-permute-start.17 = (bf16[8,1,32,256]{3,2,1,0:T(8,128)(2,1)S(1)}, bf16[8,1,32,256]{3,2,1,0:T(8,128)(2,1)S(1)}, u32[]{:S(2)}, u32[]{:S(2)}) collective-permute-start(bf16[8,1,32,256]{3,2,1,0:T(8,128)(2,1)S(1)} %get-tuple-element.94), channel_id=1, source_target_pairs={{0,8},{1,9},{2,10},{3,11},{4,12},{5,13},{6,14},{7,15},{8,0},{9,1},... | collective-permute-start | bytes 393224 | tf_op jit(solution)/shard_map/ppermute | solution.py:353
  74.0 12.6 %collective-permute-start.20 = (f32[8,16,256]{2,1,0:T(8,128)S(1)}, f32[8,16,256]{2,1,0:T(8,128)S(1)}, u32[]{:S(2)}, u32[]{:S(2)}) collective-permute-start(f32[8,16,256]{2,1,0:T(8,128)S(1)} %get-tuple-element.100), channel_id=1, source_target_pairs={{0,1},{1,0},{2,3},{3,2},{4,5},{5,4},{6,7},{7,6},{8,9},{9,8},{10,11... | collective-permute-start | bytes 393224 | tf_op jit(solution)/shard_map/ppermute | solution.py:353
  80.1 5.9 %collective-permute-start.19 = (bf16[4,1,32,256]{3,2,1,0:T(8,128)(2,1)S(1)}, bf16[4,1,32,256]{3,2,1,0:T(8,128)(2,1)S(1)}, u32[]{:S(2)}, u32[]{:S(2)}) collective-permute-start(bf16[4,1,32,256]{3,2,1,0:T(8,128)(2,1)S(1)} %get-tuple-element.98), channel_id=1, source_target_pairs={{0,8},{1,9},{2,10},{3,11},{4,12},{5,13},{6,14},{7,15},{8,0},{9,1},... | collective-permute-start | bytes 196616 | tf_op jit(solution)/shard_map/ppermute | solution.py:353
  80.8 5.9 %collective-permute-start.22 = (f32[8,16,256]{2,1,0:T(8,128)S(1)}, f32[8,16,256]{2,1,0:T(8,128)S(1)}, u32[]{:S(2)}, u32[]{:S(2)}) collective-permute-start(f32[8,16,256]{2,1,0:T(8,128)S(1)} %get-tuple-element.102), channel_id=1, source_target_pairs={{0,1},{1,0},{2,3},{3,2},{4,5},{5,4},{6,7},{7,6},{8,9},{9,8},{10,11... | collective-permute-start | bytes 393224 | tf_op jit(solution)/shard_map/ppermute | solution.py:353
  84.5 3.4 %collective-permute-start.23 = (f32[8,16,256]{2,1,0:T(8,128)S(1)}, f32[8,16,256]{2,1,0:T(8,128)S(1)}, u32[]{:S(2)}, u32[]{:S(2)}) collective-permute-start(f32[8,16,256]{2,1,0:T(8,128)S(1)} %get-tuple-element.103), channel_id=1, source_target_pairs={{0,1},{1,0},{2,3},{3,2},{4,5},{5,4},{6,7},{7,6},{8,9},{9,8},{10,11... | collective-permute-start | bytes 393224 | tf_op jit(solution)/shard_map/ppermute | solution.py:353
  84.6 2.1 %collective-permute-start.21 = (f32[4,16,256]{2,1,0:T(8,128)S(1)}, f32[4,16,256]{2,1,0:T(8,128)S(1)}, u32[]{:S(2)}, u32[]{:S(2)}) collective-permute-start(f32[4,16,256]{2,1,0:T(8,128)S(1)} %get-tuple-element.101), channel_id=1, source_target_pairs={{0,1},{1,0},{2,3},{3,2},{4,5},{5,4},{6,7},{7,6},{8,9},{9,8},{10,11... | collective-permute-start | bytes 196616 | tf_op jit(solution)/shard_map/ppermute | solution.py:353
  86.6 1.3 %collective-permute-start.24 = (f32[4,16,256]{2,1,0:T(8,128)S(1)}, f32[4,16,256]{2,1,0:T(8,128)S(1)}, u32[]{:S(2)}, u32[]{:S(2)}) collective-permute-start(f32[4,16,256]{2,1,0:T(8,128)S(1)} %get-tuple-element.104), channel_id=1, source_target_pairs={{0,1},{1,0},{2,3},{3,2},{4,5},{5,4},{6,7},{7,6},{8,9},{9,8},{10,11... | collective-permute-start | bytes 196616 | tf_op jit(solution)/shard_map/ppermute | solution.py:353

commit v3 on v2

v3 whole, which is shorter than its diff:
```python
import functools

import jax
import jax.numpy as jnp
from jax import lax
from jax.experimental import pallas as pl
from jax.experimental.pallas import tpu as pltpu
from jax.sharding import PartitionSpec as P

f32 = jnp.float32
bf16 = jnp.bfloat16
LANES = 128
EPS = 1e-05
VMEM_BYTES = 12 << 20
PROJECT_ROWS = 16
IN_PLACE = pl.BlockSpec(memory_space=pltpu.VMEM)


def whole(shape):
    return pl.BlockSpec(shape, lambda *_: (0,) * len(shape))


def corner(shape):
    return pl.BlockSpec((1,) * (len(shape) - 2) + (16, LANES), lambda *_: (0,) * len(shape))


def call(body, grid, in_specs, out_specs, out_shape, scratch, cost, operands, after=(), vmem=VMEM_BYTES):
    count = len(operands)
    extra = len(after)

    def run(*refs):
        return body(*refs[:count], *refs[count + extra :])

    return pl.pallas_call(
        run,
        grid=grid,
        in_specs=list(in_specs) + [corner(array.shape) for array in after],
        out_specs=out_specs,
        out_shape=out_shape,
        scratch_shapes=scratch,
        compiler_params=pltpu.CompilerParams(vmem_limit_bytes=vmem),
        cost_estimate=pl.CostEstimate(flops=cost[0], bytes_accessed=cost[1], transcendentals=0),
    )(*operands, *after)


def norm_columns(tile, gain, bias):
    count = tile.shape[0]
    mean_val = jnp.sum(tile, axis=0, keepdims=True) * (1.0 / count)
    centered = tile - mean_val
    variance = jnp.sum(centered * centered, axis=0, keepdims=True) * (1.0 / count)
    return (centered * lax.rsqrt(variance + EPS) * gain + bias).astype(bf16)


def gather_weights(w_ref, wt_ref):
    hidden = w_ref.shape[1] // 4
    turned = w_ref[...].astype(f32).T * 0.5
    for value in range(2):
        for side in range(2):
            source, target = (2 * side + value) * hidden, (2 * value + side) * hidden
            wt_ref[target : target + hidden, :] = turned[source : source + hidden].astype(bf16)


def turn_affine(gain_ref, bias_ref, affine_ref):
    chan = gain_ref.shape[1]
    affine_ref[0] = jnp.broadcast_to(gain_ref[...], (LANES, chan)).T
    affine_ref[1] = jnp.broadcast_to(bias_ref[...], (LANES, chan)).T


def normed_row(x_ref, affine_ref, k):
    parts = [
        norm_columns(x_ref[k, low : low + LANES, :].T.astype(f32), affine_ref[0], affine_ref[1])
        for low in range(0, x_ref.shape[1], LANES)
    ]
    return jnp.concatenate(parts, axis=1)


def project_body(chunks, stride, all_ref, all_mask, all_gain, all_bias, all_w, *rest):
    count = len(chunks)
    outs, rest = (rest[:count], rest[count : 2 * count]), rest[2 * count :]
    window_ref, hold, wt_ref, affine_ref, x_buf, mask_ref, gain_ref, bias_ref, w_ref, x_sem, sems = rest
    _, rows, width, _ = x_buf.shape
    size = sum(chunks)
    step, steps = pl.program_id(0), all_ref.shape[0] // rows

    def fetch(number):
        slot = number % 2
        block = all_ref.at[pl.ds(number * rows, rows)]
        return pltpu.make_async_copy(block, x_buf.at[slot], x_sem.at[slot])

    window = pltpu.make_async_copy(all_ref.at[pl.ds(0, window_ref.shape[0])], window_ref, sems.at[4])

    @pl.when(step == 0)
    def _():
        pairs = ((all_w, w_ref), (all_gain, gain_ref), (all_bias, bias_ref), (all_mask, mask_ref))
        copies = [pltpu.make_async_copy(source, target, sems.at[n]) for n, (source, target) in enumerate(pairs)]
        fetch(0).start()
        for copy in copies:
            copy.start()
        window.start()
        for copy in copies:
            copy.wait()
        gather_weights(w_ref, wt_ref)
        turn_affine(gain_ref, bias_ref, affine_ref)

    @pl.when(step + 1 < steps)
    def _():
        fetch(step + 1).start()

    @pl.when(step + 1 == steps)
    def _():
        window.wait()

    weights = wt_ref[...]
    fetch(step).wait()
    x_ref = x_buf.at[step % 2]
    for k in range(rows):
        proj = jnp.dot(weights, normed_row(x_ref, affine_ref, k), preferred_element_type=f32)
        keep = mask_ref[pl.ds(step * rows + k, 1), :].astype(f32)
        act = (jnp.tanh(proj[: 4 * size]) + 1.0) * proj[4 * size :] * keep
        for lane in range(width // LANES):
            hold[lane, pl.ds(k * stride, 4 * size), :] = act[:, lane * LANES : (lane + 1) * LANES]
    span = pl.ds(pl.multiple_of(step * rows, rows), rows)
    for owner in range(2):
        base = jnp.where(lax.axis_index("row") % 2 == owner, 0, size)
        offset = 0
        for out, count in zip(outs[owner], chunks):
            for side in range(2):
                for h in range(count):
                    for lane in range(width // LANES):
                        start = base + 2 * side * size + offset + h
                        tile = hold[lane, pl.ds(start, rows, stride=stride), :]
                        out[side, h, span, lane * LANES : (lane + 1) * LANES] = tile.astype(bf16)
            offset += count


def project(x, mask, gain, bias, w_proj, chunks, window, vmem, after):
    depth, width, chan = x.shape
    rows, size = PROJECT_ROWS, sum(chunks)
    stride = 4 * size + 4
    return call(
        functools.partial(project_body, chunks, stride),
        (depth // rows,),
        [pl.BlockSpec(memory_space=pltpu.HBM)] * 5,
        [IN_PLACE] * (2 * len(chunks) + 1),
        [pltpu.VMEM((2, size, depth, width), bf16) for size in chunks] * 2 + [pltpu.VMEM((window, width, chan), bf16)],
        [
            pltpu.VMEM((width // LANES, rows * stride, LANES), f32),
            pltpu.VMEM((8 * size, chan), bf16),
            pltpu.VMEM((2, chan, LANES), f32),
            pltpu.VMEM((2, rows, width, chan), bf16),
            pltpu.VMEM((depth, width), mask.dtype),
            pltpu.VMEM((1, chan), f32),
            pltpu.VMEM((1, chan), f32),
            pltpu.VMEM(w_proj.shape, bf16),
            pltpu.SemaphoreType.DMA((2,)),
            pltpu.SemaphoreType.DMA((5,)),
        ],
        (2 * depth * width * chan * 8 * size, 4 * depth * width * chan),
        (x, mask, gain.reshape(1, chan), bias.reshape(1, chan), w_proj),
        after,
        vmem,
    )


def gate_body(x_ref, gain_ref, bias_ref, w_ref, out_ref, affine_ref):
    turn_affine(gain_ref, bias_ref, affine_ref)
    weights = w_ref[...]
    for k in range(x_ref.shape[0]):
        normed = normed_row(x_ref, affine_ref, k)
        proj = lax.dot_general(normed, weights, (((0,), (0,)), ((), ())), preferred_element_type=f32)
        out_ref[k] = 0.5 * jnp.tanh(0.5 * proj) + 0.5


def gate(x, gain, bias, w_gate, after):
    rows, width, chan = x.shape
    return call(
        gate_body,
        (1,),
        [IN_PLACE] * 4,
        IN_PLACE,
        pltpu.VMEM(x.shape, f32),
        [pltpu.VMEM((2, chan, LANES), f32)],
        (2 * rows * width * chan * chan, 6 * rows * width * chan),
        (x, gain.reshape(1, chan), bias.reshape(1, chan), w_gate),
        after,
    )


def triangle_body(order, own_ref, got_ref, keep_ref, send_ref, hold):
    count, slots, block, _ = keep_ref.shape
    device = lax.axis_index("row")
    for h in range(count):
        left = jnp.concatenate([own_ref[0, h], got_ref[0, h]], axis=0)
        right = jnp.concatenate([own_ref[1, h], got_ref[1, h]], axis=0)
        hold[h % 4] = lax.dot_general(left, right, (((0,), (0,)), ((), ())), preferred_element_type=f32)
        for slot in range(2 * slots):
            mask = 0
            for digit, bit in enumerate(reversed(order)):
                mask |= (slot >> digit & 1) << bit
            rows = pl.ds(pl.multiple_of((device ^ mask) // 2 * block, block), block)
            if slot < slots:
                keep_ref[h, slot] = hold[h % 4, rows, :]
            else:
                send_ref[h, slot - slots] = hold[h % 4, rows, :].astype(bf16)


def triangle(own, got, order, after):
    _, size, depth, width = own.shape
    slots = 2 ** (len(order) - 1)
    shape = (size, slots, width // (2 * slots), width)
    return call(
        functools.partial(triangle_body, order),
        (1,),
        [IN_PLACE] * 2,
        [IN_PLACE] * 2,
        [pltpu.VMEM(shape, f32), pltpu.VMEM(shape, bf16)],
        [pltpu.VMEM((4, width, width), f32)],
        (4 * size * depth * width * width, 8 * size * depth * width + 3 * size * width * width),
        (own, got),
        after,
    )


def halve_body(held_ref, got_ref, keep_ref, send_ref):
    slots = keep_ref.shape[1]
    keep_ref[...] = held_ref[:, :slots] + got_ref[:, :slots].astype(f32)
    send_ref[...] = (held_ref[:, slots:] + got_ref[:, slots:].astype(f32)).astype(bf16)


def halve(held, got, after):
    count, slots, block, width = held.shape
    shape = (count, slots // 2, block, width)
    return call(
        halve_body,
        (1,),
        [IN_PLACE] * 2,
        [IN_PLACE] * 2,
        [pltpu.VMEM(shape, f32), pltpu.VMEM(shape, bf16)],
        [],
        (held.size, held.size * 9),
        (held, got),
        after,
    )


def total_body(held_ref, got_ref, mine_ref, theirs_ref, hold):
    hold[...] = held_ref[:, 0] + got_ref[:, 0].astype(f32)
    rows = mine_ref.shape[1]
    core = lax.axis_index("row") % 2
    mine_ref[...] = hold[:, pl.ds(pl.multiple_of(core * rows, rows), rows), :]
    theirs_ref[...] = hold[:, pl.ds(pl.multiple_of((1 - core) * rows, rows), rows), :]


def total(held, got, after):
    count, _, block, width = held.shape
    shape = pltpu.VMEM((count, block // 2, width), f32)
    return call(
        total_body,
        (1,),
        [IN_PLACE] * 2,
        [IN_PLACE] * 2,
        [shape, shape],
        [pltpu.VMEM((count, block, width), f32)],
        (held.size, held.size * 10),
        (held, got),
        after,
    )


def finish_body(chunks, *refs):
    count = len(chunks)
    mine, theirs = refs[:count], refs[count : 2 * count]
    gate_ref, gain_ref, bias_ref, w_ref, out_ref, hold = refs[2 * count :]
    hidden, _ = w_ref.shape
    half = hidden // 2
    rows, width, _ = gate_ref.shape
    stride = hold.shape[1] // hidden
    core = lax.axis_index("row") % 2

    @pl.when(pl.program_id(0) == 0)
    def _():
        sums = []
        first = 0
        for chunk, size in enumerate(chunks):
            for part in range(2):
                for h in range(size):
                    index = jnp.where(core == part, 0, half) + first + h
                    sums.append((index, (mine, theirs)[part][chunk][h]))
            first += size
        mean_val = sum(value for _, value in sums) * (1.0 / hidden)
        square = sum((value - mean_val) * (value - mean_val) for _, value in sums)
        scale = lax.rsqrt(square * (1.0 / hidden) + EPS)
        for index, value in sums:
            value = (value - mean_val) * scale * gain_ref[index] + bias_ref[index]
            for lane in range(width // LANES):
                hold[lane, pl.ds(index * stride, rows), :] = value[:, lane * LANES : (lane + 1) * LANES]

    weights = w_ref[...]
    for near in range(out_ref.shape[0]):
        row = pl.program_id(0) * out_ref.shape[0] + near
        for lane in range(width // LANES):
            normed = hold[lane, pl.ds(row, hidden, stride=stride), :].astype(bf16)
            mixed = lax.dot_general(normed, weights, (((0,), (0,)), ((), ())), preferred_element_type=f32)
            span = pl.ds(lane * LANES, LANES)
            out_ref[near, span, :] = (gate_ref[row, span, :] * mixed).astype(bf16)


def finish(mine, theirs, gate_act, gain, bias, w_out, chunks):
    rows, width, chan = gate_act.shape
    hidden = w_out.shape[0]
    step = 4
    stride = rows + 4
    smem = pl.BlockSpec(memory_space=pltpu.SMEM)
    return call(
        functools.partial(finish_body, chunks),
        (rows // step,),
        [IN_PLACE] * (2 * len(mine) + 1) + [smem, smem, IN_PLACE],
        pl.BlockSpec((step, width, chan), lambda i: (i, 0, 0)),
        jax.ShapeDtypeStruct((rows, width, chan), bf16),
        [pltpu.VMEM((width // LANES, hidden * stride, LANES), f32)],
        (2 * rows * width * chan * hidden, rows * width * (chan * 6 + hidden * 4)),
        (*mine, *theirs, gate_act, gain, bias, w_out),
    )


def in_turn(orders):
    events, turn = [], 0
    for chunk, order in enumerate(orders):
        late = order[0] != 1
        for step in range(len(order) + 1):
            if late:
                time = step + (step == len(order))
            else:
                time = turn + step if step else max(turn - 1, 0)
            events.append((time, step == 0, late and step > 0, step, chunk))
        turn += not late
    return [(chunk, step) for *_, step, chunk in sorted(events)]


def on_device(pair_act, pair_mask, in_gain, in_bias, w_proj, w_gate, out_gain, out_bias, w_out):
    width = pair_act.shape[1]
    devices = lax.axis_size("row")
    bits = devices.bit_length() - 1
    unit = w_out.shape[0] // 32
    z_last, z_first = tuple(range(1, bits)), tuple(range(2, bits)) + (1,)
    plan = ((4, z_last), (2, z_first), (4, z_last), (3, z_last), (2, z_last), (1, z_last))
    chunks, orders = tuple(size * unit for size, _ in plan), tuple(order for _, order in plan)
    count = len(chunks)

    def swap(values, bit):
        return lax.ppermute(values, "row", [(d, d ^ 1 << bit) for d in range(devices)])

    last = []

    def put(kernel, *operands):
        outs = kernel(*operands, tuple(last[-1:]))
        last.append(outs[0] if isinstance(outs, (list, tuple)) else outs)
        return outs

    vmem = (61 << 20) - pair_act.shape[0] * width * w_out.shape[0] * 4
    acts = put(
        project, pair_act, pair_mask, in_gain, in_bias, w_proj, chunks, width // devices, vmem
    )
    own, got = acts[:count], [swap(part, 0) for part in acts[count:-1]]
    held, arrived = {}, {}

    def advance(chunk, step):
        order = orders[chunk]
        if step == 0:
            held[chunk], sent = put(triangle, own[chunk], got[chunk], order)
        elif step < len(order):
            held[chunk], sent = put(halve, held[chunk], arrived[chunk])
        else:
            held[chunk], sent = put(total, held[chunk], arrived[chunk])
        arrived[chunk] = swap(sent, order[step] if step < len(order) else 0)

    sequence = in_turn(orders)
    for position, (chunk, step) in enumerate(sequence):
        with jax.named_scope(f"chunk{chunk}_step{step}"):
            advance(chunk, step)
        if position == 1:
            gate_act = put(gate, acts[-1], in_gain, in_bias, w_gate)
    mine, theirs = [held[c] for c in range(count)], [arrived[c] for c in range(count)]
    return finish(mine, theirs, gate_act, out_gain, out_bias, w_out, chunks)


def solution(mesh):
    return jax.shard_map(
        on_device,
        mesh=mesh,
        in_specs=(
            P(("groups", "row"), None, None),
            P(("groups", "row"), None),
            P(),
            P(),
            P(),
            P(),
            P(),
            P(),
            P(),
        ),
        out_specs=P(("groups", "row"), None, None),
        check_vma=False,
    )
```

time: 91.4 us -> 78.1 us (0.85)
  Pallas kernels: 35.2 us -> 19.2 us
  starting transfers between devices: 24.1 us -> 33.2 us
  waiting for transfers between devices: 28.8 us -> 25.2 us
  local copies, waits for them, and re-layouts: 2.18 us -> 0.03 us
    pallas_call x23 -> x27, Pallas kernels: 35.2 us -> 19.2 us  [call(): pl.pallas_call(run, grid=grid, in_specs=list(in_specs) + [corner(array.sh...]
    ppermute x25 -> x30, starting transfers between devices: 24.1 us -> 33.2 us  [swap(): lax.ppermute(values, 'row', [(d, d ^ 1 << bit) for d in range(devices)])]
    ppermute x25 -> x30, waiting for transfers between devices: 28.8 us -> 25.2 us  [swap(): lax.ppermute(values, 'row', [(d, d ^ 1 << bit) for d in range(devices)])]
    unnamed x28 -> x12, local copies, waits for them, and re-layouts: 2.18 us -> 0.03 us
  transfers between devices with their start and end apart: 25 -> 30, of which waited for: 10 -> 11; matrix products, arithmetic and copies ran while one was open for 0% -> 0% of each run, Pallas kernels for 19% -> 6%
where the time goes in v3:
time: 78.1 us; the launch traced here: 77.9 us
  starting transfers between devices  33.2 us (43%)
  waiting for transfers between devices  25.2 us (32%)
  Pallas kernels  19.2 us (25%)
    ppermute x30, starting transfers between devices, swap(): lax.ppermute(values, 'row', [(d, d ^ 1 << bit) for d in range(devices)])  33.2 us
    ppermute x30, waiting for transfers between devices, swap(): lax.ppermute(values, 'row', [(d, d ^ 1 << bit) for d in range(devices)])  25.2 us
    pallas_call x27, Pallas kernels, call(): pl.pallas_call(run, grid=grid, in_specs=list(in_specs) + [corner(array.sh...  19.2 us
  transfers between devices with their start and end apart: 30, of which 11 were waited for; matrix products, arithmetic and copies ran while one was open for 0% of the time, Pallas kernels for 6%

profile of v3, /device:TPU:0, one launch (start us, length us, event | category | flops | bytes accessed | tf_op | source)
XLA Modules:
  0.0 77.9 jit_solution(15250067816035303177)
XLA Ops:
  0.0 11.2 %shard_map.91 = (bf16[2,8,96,256]{3,2,1,0:T(8,128)(2,1)S(1)}, bf16[2,4,96,256]{3,2,1,0:T(8,128)(2,1)S(1)}, bf16[2,8,96,256]{3,2,1,0:T(8,128)(2,1)S(1)}, bf16[2,6...) custom-call(bf16[96,256,128]{2,1,0:T(8,128)(2,1)} %refs_0_.1, ...), custom_call_target="tpu_custom_call" | custom-call | flops 1610612736 | bytes 12582912 | tf_op jit(solution)/shard_map/pallas_call | solution.py:34
  11.2 0.5 collective-permute-start
  11.7 0.1 collective-permute-start.2
  11.8 0.4 collective-permute-start.3
  12.2 0.1 collective-permute-start.6
  12.3 1.3 %collective-permute-done.refs_1_ = bf16[2,8,96,256]{3,2,1,0:T(8,128)(2,1)S(1)} collective-permute-done((bf16[2,8,96,256]{3,2,1,0:T(8,128)(2,1)S(1)}, bf16[2,8,96,256]{3,2,1,0:T(8,128)(2,1)S(1)}, u32[]{:S(2)}, u32[]{:S(2)}) %collective-permute-start) | collective-permute-done | bytes 786464 | tf_op jit(solution)/shard_map/ppermute | solution.py:351
  13.6 0.6 chunk0_step0.1
  14.2 3.0 %collective-permute-start.1 = (bf16[8,4,32,256]{3,2,1,0:T(8,128)(2,1)S(1)}, bf16[8,4,32,256]{3,2,1,0:T(8,128)(2,1)S(1)}, u32[]{:S(2)}, u32[]{:S(2)}) collective-permute-start(bf16[8,4,32,256]{3,2,1,0:T(8,128)(2,1)S(1)} %get-tuple-element.69), channel_id=1, source_target_pairs={{0,2},{1,3},{2,0},{3,1},{4,6},{5,7},{6,4},{7,5},{8,10},{9,11},{10,... | collective-permute-start | bytes 1572872 | tf_op jit(solution)/shard_map/chunk0_step0/ppermute | solution.py:351
  17.1 0.4 chunk1_step0.1
  17.6 1.3 %shard_map.92.refs_2_.refs_12_ = f32[16,256,128]{2,1,0:T(8,128)S(1)} custom-call(bf16[16,256,128]{2,1,0:T(8,128)(2,1)S(1)} %get-tuple-element.72.refs_0_, f32[1,128]{1,0:T(1,128)S(1)} %bitcast.3, f32[1,128]{1,0:T(1,128)S(1)} %bitcast.5, bf16[128,128]{1,0:T(8,128)(2,1)S(1)} %copy-done, f32[4,4,32,256]{3,2,1,0:T(8,128)S(1)} %get-tuple-element.75.refs_4_.refs_0_), custom_call_target="tpu_custom_call" | custom-call | flops 134217728 | bytes 3145728 | tf_op jit(solution)/shard_map/pallas_call | solution.py:34
  18.9 0.6 chunk2_step0.1
  19.5 1.1 %collective-permute-start.5 = (bf16[8,4,32,256]{3,2,1,0:T(8,128)(2,1)S(1)}, bf16[8,4,32,256]{3,2,1,0:T(8,128)(2,1)S(1)}, u32[]{:S(2)}, u32[]{:S(2)}) collective-permute-start(bf16[8,4,32,256]{3,2,1,0:T(8,128)(2,1)S(1)} %get-tuple-element.79), channel_id=1, source_target_pairs={{0,2},{1,3},{2,0},{3,1},{4,6},{5,7},{6,4},{7,5},{8,10},{9,11},{10,... | collective-permute-start | bytes 1572872 | tf_op jit(solution)/shard_map/chunk2_step0/ppermute | solution.py:351
  20.6 1.6 %collective-permute-start.7 = (bf16[4,4,32,256]{3,2,1,0:T(8,128)(2,1)S(1)}, bf16[4,4,32,256]{3,2,1,0:T(8,128)(2,1)S(1)}, u32[]{:S(2)}, u32[]{:S(2)}) collective-permute-start(bf16[4,4,32,256]{3,2,1,0:T(8,128)(2,1)S(1)} %get-tuple-element.82), channel_id=1, source_target_pairs={{0,4},{1,5},{2,6},{3,7},{4,0},{5,1},{6,2},{7,3},{8,12},{9,13},{10,... | collective-permute-start | bytes 786440 | tf_op jit(solution)/shard_map/chunk1_step0/ppermute | solution.py:351
  22.2 7.7 %collective-permute-done.1.refs_1_ = bf16[8,4,32,256]{3,2,1,0:T(8,128)(2,1)S(1)} collective-permute-done((bf16[8,4,32,256]{3,2,1,0:T(8,128)(2,1)S(1)}, bf16[8,4,32,256]{3,2,1,0:T(8,128)(2,1)S(1)}, u32[]{:S(2)}, u32[]{:S(2)}) %collective-permute-start.1) | collective-permute-done | bytes 524320 | tf_op jit(solution)/shard_map/chunk0_step0/ppermute | solution.py:351
  29.8 0.1 chunk0_step1.1
  29.9 2.2 %collective-permute-start.4 = (bf16[8,2,32,256]{3,2,1,0:T(8,128)(2,1)S(1)}, bf16[8,2,32,256]{3,2,1,0:T(8,128)(2,1)S(1)}, u32[]{:S(2)}, u32[]{:S(2)}) collective-permute-start(bf16[8,2,32,256]{3,2,1,0:T(8,128)(2,1)S(1)} %get-tuple-element.78), channel_id=1, source_target_pairs={{0,4},{1,5},{2,6},{3,7},{4,0},{5,1},{6,2},{7,3},{8,12},{9,13},{10,... | collective-permute-start | bytes 786440 | tf_op jit(solution)/shard_map/chunk0_step1/ppermute | solution.py:351
  32.2 0.5 chunk3_step0.1
  32.7 1.6 %collective-permute-start.10 = (bf16[6,4,32,256]{3,2,1,0:T(8,128)(2,1)S(1)}, bf16[6,4,32,256]{3,2,1,0:T(8,128)(2,1)S(1)}, u32[]{:S(2)}, u32[]{:S(2)}) collective-permute-start(bf16[6,4,32,256]{3,2,1,0:T(8,128)(2,1)S(1)} %get-tuple-element.89), channel_id=1, source_target_pairs={{0,2},{1,3},{2,0},{3,1},{4,6},{5,7},{6,4},{7,5},{8,10},{9,11},{10,... | collective-permute-start | bytes 1179656 | tf_op jit(solution)/shard_map/chunk3_step0/ppermute | solution.py:351
  34.3 2.6 %collective-permute-start.12 = (bf16[4,2,32,256]{3,2,1,0:T(8,128)(2,1)S(1)}, bf16[4,2,32,256]{3,2,1,0:T(8,128)(2,1)S(1)}, u32[]{:S(2)}, u32[]{:S(2)}) collective-permute-start(bf16[4,2,32,256]{3,2,1,0:T(8,128)(2,1)S(1)} %get-tuple-element.92), channel_id=1, source_target_pairs={{0,8},{1,9},{2,10},{3,11},{4,12},{5,13},{6,14},{7,15},{8,0},{9,1},... | collective-permute-start | bytes 393224 | tf_op jit(solution)/shard_map/chunk1_step1/ppermute | solution.py:351
  36.9 4.2 %collective-permute-done.5.refs_1_ = bf16[8,4,32,256]{3,2,1,0:T(8,128)(2,1)S(1)} collective-permute-done((bf16[8,4,32,256]{3,2,1,0:T(8,128)(2,1)S(1)}, bf16[8,4,32,256]{3,2,1,0:T(8,128)(2,1)S(1)}, u32[]{:S(2)}, u32[]{:S(2)}) %collective-permute-start.5) | collective-permute-done | bytes 524320 | tf_op jit(solution)/shard_map/chunk2_step0/ppermute | solution.py:351
  41.1 0.1 chunk2_step1.1
  41.2 2.2 %collective-permute-start.9 = (bf16[8,2,32,256]{3,2,1,0:T(8,128)(2,1)S(1)}, bf16[8,2,32,256]{3,2,1,0:T(8,128)(2,1)S(1)}, u32[]{:S(2)}, u32[]{:S(2)}) collective-permute-start(bf16[8,2,32,256]{3,2,1,0:T(8,128)(2,1)S(1)} %get-tuple-element.88), channel_id=1, source_target_pairs={{0,4},{1,5},{2,6},{3,7},{4,0},{5,1},{6,2},{7,3},{8,12},{9,13},{10,... | collective-permute-start | bytes 786440 | tf_op jit(solution)/shard_map/chunk2_step1/ppermute | solution.py:351
  43.5 0.4 chunk4_step0.1
  43.9 1.6 %collective-permute-start.16 = (bf16[4,4,32,256]{3,2,1,0:T(8,128)(2,1)S(1)}, bf16[4,4,32,256]{3,2,1,0:T(8,128)(2,1)S(1)}, u32[]{:S(2)}, u32[]{:S(2)}) collective-permute-start(bf16[4,4,32,256]{3,2,1,0:T(8,128)(2,1)S(1)} %get-tuple-element.101), channel_id=1, source_target_pairs={{0,2},{1,3},{2,0},{3,1},{4,6},{5,7},{6,4},{7,5},{8,10},{9,11},{10,... | collective-permute-start | bytes 786440 | tf_op jit(solution)/shard_map/chunk4_step0/ppermute | solution.py:351
  45.5 2.6 %collective-permute-start.8 = (bf16[8,1,32,256]{3,2,1,0:T(8,128)(2,1)S(1)}, bf16[8,1,32,256]{3,2,1,0:T(8,128)(2,1)S(1)}, u32[]{:S(2)}, u32[]{:S(2)}) collective-permute-start(bf16[8,1,32,256]{3,2,1,0:T(8,128)(2,1)S(1)} %get-tuple-element.87), channel_id=1, source_target_pairs={{0,8},{1,9},{2,10},{3,11},{4,12},{5,13},{6,14},{7,15},{8,0},{9,1},... | collective-permute-start | bytes 393224 | tf_op jit(solution)/shard_map/chunk0_step2/ppermute | solution.py:351
  48.1 1.4 %collective-permute-done.10.refs_1_ = bf16[6,4,32,256]{3,2,1,0:T(8,128)(2,1)S(1)} collective-permute-done((bf16[6,4,32,256]{3,2,1,0:T(8,128)(2,1)S(1)}, bf16[6,4,32,256]{3,2,1,0:T(8,128)(2,1)S(1)}, u32[]{:S(2)}, u32[]{:S(2)}) %collective-permute-start.10) | collective-permute-done | bytes 393248 | tf_op jit(solution)/shard_map/chunk3_step0/ppermute | solution.py:351
  49.5 0.1 chunk3_step1.1
  49.6 2.2 %collective-permute-start.15 = (bf16[6,2,32,256]{3,2,1,0:T(8,128)(2,1)S(1)}, bf16[6,2,32,256]{3,2,1,0:T(8,128)(2,1)S(1)}, u32[]{:S(2)}, u32[]{:S(2)}) collective-permute-start(bf16[6,2,32,256]{3,2,1,0:T(8,128)(2,1)S(1)} %get-tuple-element.100), channel_id=1, source_target_pairs={{0,4},{1,5},{2,6},{3,7},{4,0},{5,1},{6,2},{7,3},{8,12},{9,13},{10,... | collective-permute-start | bytes 589832 | tf_op jit(solution)/shard_map/chunk3_step1/ppermute | solution.py:351
  51.8 2.7 %collective-permute-start.14 = (bf16[8,1,32,256]{3,2,1,0:T(8,128)(2,1)S(1)}, bf16[8,1,32,256]{3,2,1,0:T(8,128)(2,1)S(1)}, u32[]{:S(2)}, u32[]{:S(2)}) collective-permute-start(bf16[8,1,32,256]{3,2,1,0:T(8,128)(2,1)S(1)} %get-tuple-element.99), channel_id=1, source_target_pairs={{0,8},{1,9},{2,10},{3,11},{4,12},{5,13},{6,14},{7,15},{8,0},{9,1},... | collective-permute-start | bytes 393224 | tf_op jit(solution)/shard_map/chunk2_step2/ppermute | solution.py:351
  54.5 0.9 %collective-permute-done.8.refs_1_ = bf16[8,1,32,256]{3,2,1,0:T(8,128)(2,1)S(1)} collective-permute-done((bf16[8,1,32,256]{3,2,1,0:T(8,128)(2,1)S(1)}, bf16[8,1,32,256]{3,2,1,0:T(8,128)(2,1)S(1)}, u32[]{:S(2)}, u32[]{:S(2)}) %collective-permute-start.8) | collective-permute-done | bytes 131104 | tf_op jit(solution)/shard_map/chunk0_step2/ppermute | solution.py:351
  55.4 0.1 chunk0_step3.1
  55.5 0.3 chunk5_step0.1
  55.8 0.7 collective-permute-start.20
  56.5 0.5 collective-permute-start.19
  57.0 1.1 %collective-permute-start.13 = (bf16[4,1,32,256]{3,2,1,0:T(8,128)(2,1)S(1)}, bf16[4,1,32,256]{3,2,1,0:T(8,128)(2,1)S(1)}, u32[]{:S(2)}, u32[]{:S(2)}) collective-permute-start(bf16[4,1,32,256]{3,2,1,0:T(8,128)(2,1)S(1)} %get-tuple-element.98), channel_id=1, source_target_pairs={{0,2},{1,3},{2,0},{3,1},{4,6},{5,7},{6,4},{7,5},{8,10},{9,11},{10,... | collective-permute-start | bytes 196616 | tf_op jit(solution)/shard_map/chunk1_step2/ppermute | solution.py:351
  58.1 3.0 %collective-permute-done.15.refs_1_ = bf16[6,2,32,256]{3,2,1,0:T(8,128)(2,1)S(1)} collective-permute-done((bf16[6,2,32,256]{3,2,1,0:T(8,128)(2,1)S(1)}, bf16[6,2,32,256]{3,2,1,0:T(8,128)(2,1)S(1)}, u32[]{:S(2)}, u32[]{:S(2)}) %collective-permute-start.15) | collective-permute-done | bytes 196640 | tf_op jit(solution)/shard_map/chunk3_step1/ppermute | solution.py:351
  61.1 1.9 %collective-permute-start.18 = (bf16[6,1,32,256]{3,2,1,0:T(8,128)(2,1)S(1)}, bf16[6,1,32,256]{3,2,1,0:T(8,128)(2,1)S(1)}, u32[]{:S(2)}, u32[]{:S(2)}) collective-permute-start(bf16[6,1,32,256]{3,2,1,0:T(8,128)(2,1)S(1)} %get-tuple-element.109), channel_id=1, source_target_pairs={{0,8},{1,9},{2,10},{3,11},{4,12},{5,13},{6,14},{7,15},{8,0},{9,1},... | collective-permute-start | bytes 294920 | tf_op jit(solution)/shard_map/chunk3_step2/ppermute | solution.py:351
  63.2 2.5 %collective-permute-start.22 = (bf16[2,2,32,256]{3,2,1,0:T(8,128)(2,1)S(1)}, bf16[2,2,32,256]{3,2,1,0:T(8,128)(2,1)S(1)}, u32[]{:S(2)}, u32[]{:S(2)}) collective-permute-start(bf16[2,2,32,256]{3,2,1,0:T(8,128)(2,1)S(1)} %get-tuple-element.116), channel_id=1, source_target_pairs={{0,4},{1,5},{2,6},{3,7},{4,0},{5,1},{6,2},{7,3},{8,12},{9,13},{10,... | collective-permute-start | bytes 196616 | tf_op jit(solution)/shard_map/chunk5_step1/ppermute | solution.py:351
  65.7 0.4 collective-permute-start.21
  66.2 0.2 collective-permute-start.26
  66.4 1.5 %collective-permute-done.18.refs_1_ = bf16[6,1,32,256]{3,2,1,0:T(8,128)(2,1)S(1)} collective-permute-done((bf16[6,1,32,256]{3,2,1,0:T(8,128)(2,1)S(1)}, bf16[6,1,32,256]{3,2,1,0:T(8,128)(2,1)S(1)}, u32[]{:S(2)}, u32[]{:S(2)}) %collective-permute-start.18) | collective-permute-done | bytes 98336 | tf_op jit(solution)/shard_map/chunk3_step2/ppermute | solution.py:351
  67.9 0.2 collective-permute-done.22.refs_1_
  68.1 1.0 %collective-permute-start.23 = (bf16[2,1,32,256]{3,2,1,0:T(8,128)(2,1)S(1)}, bf16[2,1,32,256]{3,2,1,0:T(8,128)(2,1)S(1)}, u32[]{:S(2)}, u32[]{:S(2)}) collective-permute-start(bf16[2,1,32,256]{3,2,1,0:T(8,128)(2,1)S(1)} %get-tuple-element.119), channel_id=1, source_target_pairs={{0,8},{1,9},{2,10},{3,11},{4,12},{5,13},{6,14},{7,15},{8,0},{9,1},... | collective-permute-start | bytes 98312 | tf_op jit(solution)/shard_map/chunk5_step2/ppermute | solution.py:351
  69.1 3.1 %collective-permute-done.21.refs_1_ = bf16[4,1,32,256]{3,2,1,0:T(8,128)(2,1)S(1)} collective-permute-done((bf16[4,1,32,256]{3,2,1,0:T(8,128)(2,1)S(1)}, bf16[4,1,32,256]{3,2,1,0:T(8,128)(2,1)S(1)}, u32[]{:S(2)}, u32[]{:S(2)}) %collective-permute-start.21) | collective-permute-done | bytes 65568 | tf_op jit(solution)/shard_map/chunk4_step2/ppermute | solution.py:351
  72.2 1.0 %collective-permute-done.23.refs_1_ = bf16[2,1,32,256]{3,2,1,0:T(8,128)(2,1)S(1)} collective-permute-done((bf16[2,1,32,256]{3,2,1,0:T(8,128)(2,1)S(1)}, bf16[2,1,32,256]{3,2,1,0:T(8,128)(2,1)S(1)}, u32[]{:S(2)}, u32[]{:S(2)}) %collective-permute-start.23) | collective-permute-done | bytes 32800 | tf_op jit(solution)/shard_map/chunk5_step2/ppermute | solution.py:351
  73.2 0.6 collective-permute-start.29
  73.8 0.9 %collective-permute-done.29.refs_11_ = f32[2,16,256]{2,1,0:T(8,128)S(1)} collective-permute-done((f32[2,16,256]{2,1,0:T(8,128)S(1)}, f32[2,16,256]{2,1,0:T(8,128)S(1)}, u32[]{:S(2)}, u32[]{:S(2)}) %collective-permute-start.29) | collective-permute-done | bytes 32800 | tf_op jit(solution)/shard_map/chunk5_step3/ppermute | solution.py:351
  74.7 3.2 %shard_map.93 = bf16[16,256,128]{2,1,0:T(8,128)(2,1)} custom-call(f32[8,16,256]{2,1,0:T(8,128)S(1)} %get-tuple-element.97.refs_2_.refs_0_, f32[4,16,256]{2,1,0:T(8,128)S(1)} %get-tuple-element.108.refs_2_.refs_1_, f32[8,16,256]{2,1,0:T(8,128)S(1)} %get-tuple-element.107.refs_2_, f32[6,16,256]{2,1,0:T(8,128)S(1)} %get-tuple-element.114.refs_2_.refs_3_, ...), custom_call_target="tpu_custom_call" | custom-call | flops 67108864 | bytes 4194304 | tf_op jit(solution)/shard_map/pallas_call | solution.py:34
  (51 shorter events, 0.6 us)
Async XLA Ops:
  0.0 17.5 %copy-start.3 = (f32[128]{0:T(128)S(1)}, f32[128]{0:T(128)}, u32[]{:S(2)}) copy-start(f32[128]{0:T(128)} %param.12) | copy-start | bytes 1540
  0.0 17.5 %copy-start.2 = (f32[128]{0:T(128)S(1)}, f32[128]{0:T(128)}, u32[]{:S(2)}) copy-start(f32[128]{0:T(128)} %param.11) | copy-start | bytes 1540
  0.0 17.5 %copy-start = (bf16[128,128]{1,0:T(8,128)(2,1)S(1)}, bf16[128,128]{1,0:T(8,128)(2,1)}, u32[]{:S(2)}) copy-start(bf16[128,128]{1,0:T(8,128)(2,1)} %refs_3_.1) | copy-start | bytes 98308
  11.2 2.4 %collective-permute-start = (bf16[2,8,96,256]{3,2,1,0:T(8,128)(2,1)S(1)}, bf16[2,8,96,256]{3,2,1,0:T(8,128)(2,1)S(1)}, u32[]{:S(2)}, u32[]{:S(2)}) collective-permute-start(bf16[2,8,96,256]{3,2,1,0:T(8,128)(2,1)S(1)} %get-tuple-element.67), channel_id=1, source_target_pairs={{0,1},{1,0},{2,3},{3,2},{4,5},{5,4},{6,7},{7,6},{8,9},{9,8},{10,11... | collective-permute-start | bytes 2359304 | tf_op jit(solution)/shard_map/ppermute | solution.py:351
  11.7 7.2 %collective-permute-start.2 = (bf16[2,8,96,256]{3,2,1,0:T(8,128)(2,1)S(1)}, bf16[2,8,96,256]{3,2,1,0:T(8,128)(2,1)S(1)}, u32[]{:S(2)}, u32[]{:S(2)}) collective-permute-start(bf16[2,8,96,256]{3,2,1,0:T(8,128)(2,1)S(1)} %get-tuple-element.71), channel_id=1, source_target_pairs={{0,1},{1,0},{2,3},{3,2},{4,5},{5,4},{6,7},{7,6},{8,9},{9,8},{10,11... | collective-permute-start | bytes 2359304 | tf_op jit(solution)/shard_map/ppermute | solution.py:351
  11.8 5.4 %collective-permute-start.3 = (bf16[2,4,96,256]{3,2,1,0:T(8,128)(2,1)S(1)}, bf16[2,4,96,256]{3,2,1,0:T(8,128)(2,1)S(1)}, u32[]{:S(2)}, u32[]{:S(2)}) collective-permute-start(bf16[2,4,96,256]{3,2,1,0:T(8,128)(2,1)S(1)} %get-tuple-element.74), channel_id=1, source_target_pairs={{0,1},{1,0},{2,3},{3,2},{4,5},{5,4},{6,7},{7,6},{8,9},{9,8},{10,11... | collective-permute-start | bytes 1179656 | tf_op jit(solution)/shard_map/ppermute | solution.py:351
  12.2 20.0 %collective-permute-start.6 = (bf16[2,6,96,256]{3,2,1,0:T(8,128)(2,1)S(1)}, bf16[2,6,96,256]{3,2,1,0:T(8,128)(2,1)S(1)}, u32[]{:S(2)}, u32[]{:S(2)}) collective-permute-start(bf16[2,6,96,256]{3,2,1,0:T(8,128)(2,1)S(1)} %get-tuple-element.81), channel_id=1, source_target_pairs={{0,1},{1,0},{2,3},{3,2},{4,5},{5,4},{6,7},{7,6},{8,9},{9,8},{10,11... | collective-permute-start | bytes 1769480 | tf_op jit(solution)/shard_map/ppermute | solution.py:351
  14.2 15.7 %collective-permute-start.1 = (bf16[8,4,32,256]{3,2,1,0:T(8,128)(2,1)S(1)}, bf16[8,4,32,256]{3,2,1,0:T(8,128)(2,1)S(1)}, u32[]{:S(2)}, u32[]{:S(2)}) collective-permute-start(bf16[8,4,32,256]{3,2,1,0:T(8,128)(2,1)S(1)} %get-tuple-element.69), channel_id=1, source_target_pairs={{0,2},{1,3},{2,0},{3,1},{4,6},{5,7},{6,4},{7,5},{8,10},{9,11},{10,... | collective-permute-start | bytes 1572872 | tf_op jit(solution)/shard_map/chunk0_step0/ppermute | solution.py:351
  19.5 21.6 %collective-permute-start.5 = (bf16[8,4,32,256]{3,2,1,0:T(8,128)(2,1)S(1)}, bf16[8,4,32,256]{3,2,1,0:T(8,128)(2,1)S(1)}, u32[]{:S(2)}, u32[]{:S(2)}) collective-permute-start(bf16[8,4,32,256]{3,2,1,0:T(8,128)(2,1)S(1)} %get-tuple-element.79), channel_id=1, source_target_pairs={{0,2},{1,3},{2,0},{3,1},{4,6},{5,7},{6,4},{7,5},{8,10},{9,11},{10,... | collective-permute-start | bytes 1572872 | tf_op jit(solution)/shard_map/chunk2_step0/ppermute | solution.py:351
  20.6 11.6 %collective-permute-start.7 = (bf16[4,4,32,256]{3,2,1,0:T(8,128)(2,1)S(1)}, bf16[4,4,32,256]{3,2,1,0:T(8,128)(2,1)S(1)}, u32[]{:S(2)}, u32[]{:S(2)}) collective-permute-start(bf16[4,4,32,256]{3,2,1,0:T(8,128)(2,1)S(1)} %get-tuple-element.82), channel_id=1, source_target_pairs={{0,4},{1,5},{2,6},{3,7},{4,0},{5,1},{6,2},{7,3},{8,12},{9,13},{10,... | collective-permute-start | bytes 786440 | tf_op jit(solution)/shard_map/chunk1_step0/ppermute | solution.py:351
  22.2 21.3 %collective-permute-start.11 = (bf16[2,4,96,256]{3,2,1,0:T(8,128)(2,1)S(1)}, bf16[2,4,96,256]{3,2,1,0:T(8,128)(2,1)S(1)}, u32[]{:S(2)}, u32[]{:S(2)}) collective-permute-start(bf16[2,4,96,256]{3,2,1,0:T(8,128)(2,1)S(1)} %get-tuple-element.91), channel_id=1, source_target_pairs={{0,1},{1,0},{2,3},{3,2},{4,5},{5,4},{6,7},{7,6},{8,9},{9,8},{10,11... | collective-permute-start | bytes 1179656 | tf_op jit(solution)/shard_map/ppermute | solution.py:351
  29.9 13.5 %collective-permute-start.4 = (bf16[8,2,32,256]{3,2,1,0:T(8,128)(2,1)S(1)}, bf16[8,2,32,256]{3,2,1,0:T(8,128)(2,1)S(1)}, u32[]{:S(2)}, u32[]{:S(2)}) collective-permute-start(bf16[8,2,32,256]{3,2,1,0:T(8,128)(2,1)S(1)} %get-tuple-element.78), channel_id=1, source_target_pairs={{0,4},{1,5},{2,6},{3,7},{4,0},{5,1},{6,2},{7,3},{8,12},{9,13},{10,... | collective-permute-start | bytes 786440 | tf_op jit(solution)/shard_map/chunk0_step1/ppermute | solution.py:351
  32.7 16.8 %collective-permute-start.10 = (bf16[6,4,32,256]{3,2,1,0:T(8,128)(2,1)S(1)}, bf16[6,4,32,256]{3,2,1,0:T(8,128)(2,1)S(1)}, u32[]{:S(2)}, u32[]{:S(2)}) collective-permute-start(bf16[6,4,32,256]{3,2,1,0:T(8,128)(2,1)S(1)} %get-tuple-element.89), channel_id=1, source_target_pairs={{0,2},{1,3},{2,0},{3,1},{4,6},{5,7},{6,4},{7,5},{8,10},{9,11},{10,... | collective-permute-start | bytes 1179656 | tf_op jit(solution)/shard_map/chunk3_step0/ppermute | solution.py:351
  34.3 9.2 %collective-permute-start.12 = (bf16[4,2,32,256]{3,2,1,0:T(8,128)(2,1)S(1)}, bf16[4,2,32,256]{3,2,1,0:T(8,128)(2,1)S(1)}, u32[]{:S(2)}, u32[]{:S(2)}) collective-permute-start(bf16[4,2,32,256]{3,2,1,0:T(8,128)(2,1)S(1)} %get-tuple-element.92), channel_id=1, source_target_pairs={{0,8},{1,9},{2,10},{3,11},{4,12},{5,13},{6,14},{7,15},{8,0},{9,1},... | collective-permute-start | bytes 393224 | tf_op jit(solution)/shard_map/chunk1_step1/ppermute | solution.py:351
  41.2 33.5 %copy-start.1 = (bf16[64,128]{1,0:T(8,128)(2,1)S(1)}, bf16[64,128]{1,0:T(8,128)(2,1)}, u32[]{:S(2)}) copy-start(bf16[64,128]{1,0:T(8,128)(2,1)} %refs_15_.1) | copy-start | bytes 49156
  41.2 33.5 %copy-start.4 = (f32[64]{0:T(128)S(1)}, f32[64]{0:T(128)}, u32[]{:S(2)}) copy-start(f32[64]{0:T(128)} %refs_13_.1) | copy-start | bytes 772
  41.2 33.5 %copy-start.5 = (f32[64]{0:T(128)S(1)}, f32[64]{0:T(128)}, u32[]{:S(2)}) copy-start(f32[64]{0:T(128)} %refs_14_.1) | copy-start | bytes 772
  41.2 10.6 %collective-permute-start.9 = (bf16[8,2,32,256]{3,2,1,0:T(8,128)(2,1)S(1)}, bf16[8,2,32,256]{3,2,1,0:T(8,128)(2,1)S(1)}, u32[]{:S(2)}, u32[]{:S(2)}) collective-permute-start(bf16[8,2,32,256]{3,2,1,0:T(8,128)(2,1)S(1)} %get-tuple-element.88), channel_id=1, source_target_pairs={{0,4},{1,5},{2,6},{3,7},{4,0},{5,1},{6,2},{7,3},{8,12},{9,13},{10,... | collective-permute-start | bytes 786440 | tf_op jit(solution)/shard_map/chunk2_step1/ppermute | solution.py:351
  43.9 12.6 %collective-permute-start.16 = (bf16[4,4,32,256]{3,2,1,0:T(8,128)(2,1)S(1)}, bf16[4,4,32,256]{3,2,1,0:T(8,128)(2,1)S(1)}, u32[]{:S(2)}, u32[]{:S(2)}) collective-permute-start(bf16[4,4,32,256]{3,2,1,0:T(8,128)(2,1)S(1)} %get-tuple-element.101), channel_id=1, source_target_pairs={{0,2},{1,3},{2,0},{3,1},{4,6},{5,7},{6,4},{7,5},{8,10},{9,11},{10,... | collective-permute-start | bytes 786440 | tf_op jit(solution)/shard_map/chunk4_step0/ppermute | solution.py:351
  45.5 10.0 %collective-permute-start.17 = (bf16[2,2,96,256]{3,2,1,0:T(8,128)(2,1)S(1)}, bf16[2,2,96,256]{3,2,1,0:T(8,128)(2,1)S(1)}, u32[]{:S(2)}, u32[]{:S(2)}) collective-permute-start(bf16[2,2,96,256]{3,2,1,0:T(8,128)(2,1)S(1)} %get-tuple-element.103), channel_id=1, source_target_pairs={{0,1},{1,0},{2,3},{3,2},{4,5},{5,4},{6,7},{7,6},{8,9},{9,8},{10,11... | collective-permute-start | bytes 589832 | tf_op jit(solution)/shard_map/ppermute | solution.py:351
  45.5 9.9 %collective-permute-start.8 = (bf16[8,1,32,256]{3,2,1,0:T(8,128)(2,1)S(1)}, bf16[8,1,32,256]{3,2,1,0:T(8,128)(2,1)S(1)}, u32[]{:S(2)}, u32[]{:S(2)}) collective-permute-start(bf16[8,1,32,256]{3,2,1,0:T(8,128)(2,1)S(1)} %get-tuple-element.87), channel_id=1, source_target_pairs={{0,8},{1,9},{2,10},{3,11},{4,12},{5,13},{6,14},{7,15},{8,0},{9,1},... | collective-permute-start | bytes 393224 | tf_op jit(solution)/shard_map/chunk0_step2/ppermute | solution.py:351
  49.6 11.5 %collective-permute-start.15 = (bf16[6,2,32,256]{3,2,1,0:T(8,128)(2,1)S(1)}, bf16[6,2,32,256]{3,2,1,0:T(8,128)(2,1)S(1)}, u32[]{:S(2)}, u32[]{:S(2)}) collective-permute-start(bf16[6,2,32,256]{3,2,1,0:T(8,128)(2,1)S(1)} %get-tuple-element.100), channel_id=1, source_target_pairs={{0,4},{1,5},{2,6},{3,7},{4,0},{5,1},{6,2},{7,3},{8,12},{9,13},{10,... | collective-permute-start | bytes 589832 | tf_op jit(solution)/shard_map/chunk3_step1/ppermute | solution.py:351
  51.8 11.2 %collective-permute-start.14 = (bf16[8,1,32,256]{3,2,1,0:T(8,128)(2,1)S(1)}, bf16[8,1,32,256]{3,2,1,0:T(8,128)(2,1)S(1)}, u32[]{:S(2)}, u32[]{:S(2)}) collective-permute-start(bf16[8,1,32,256]{3,2,1,0:T(8,128)(2,1)S(1)} %get-tuple-element.99), channel_id=1, source_target_pairs={{0,8},{1,9},{2,10},{3,11},{4,12},{5,13},{6,14},{7,15},{8,0},{9,1},... | collective-permute-start | bytes 393224 | tf_op jit(solution)/shard_map/chunk2_step2/ppermute | solution.py:351
  55.8 7.3 %collective-permute-start.20 = (bf16[2,4,32,256]{3,2,1,0:T(8,128)(2,1)S(1)}, bf16[2,4,32,256]{3,2,1,0:T(8,128)(2,1)S(1)}, u32[]{:S(2)}, u32[]{:S(2)}) collective-permute-start(bf16[2,4,32,256]{3,2,1,0:T(8,128)(2,1)S(1)} %get-tuple-element.111), channel_id=1, source_target_pairs={{0,2},{1,3},{2,0},{3,1},{4,6},{5,7},{6,4},{7,5},{8,10},{9,11},{10,... | collective-permute-start | bytes 393224 | tf_op jit(solution)/shard_map/chunk5_step0/ppermute | solution.py:351
  56.5 9.2 %collective-permute-start.19 = (bf16[4,2,32,256]{3,2,1,0:T(8,128)(2,1)S(1)}, bf16[4,2,32,256]{3,2,1,0:T(8,128)(2,1)S(1)}, u32[]{:S(2)}, u32[]{:S(2)}) collective-permute-start(bf16[4,2,32,256]{3,2,1,0:T(8,128)(2,1)S(1)} %get-tuple-element.110), channel_id=1, source_target_pairs={{0,4},{1,5},{2,6},{3,7},{4,0},{5,1},{6,2},{7,3},{8,12},{9,13},{10,... | collective-permute-start | bytes 393224 | tf_op jit(solution)/shard_map/chunk4_step1/ppermute | solution.py:351
  57.0 6.1 %collective-permute-start.13 = (bf16[4,1,32,256]{3,2,1,0:T(8,128)(2,1)S(1)}, bf16[4,1,32,256]{3,2,1,0:T(8,128)(2,1)S(1)}, u32[]{:S(2)}, u32[]{:S(2)}) collective-permute-start(bf16[4,1,32,256]{3,2,1,0:T(8,128)(2,1)S(1)} %get-tuple-element.98), channel_id=1, source_target_pairs={{0,2},{1,3},{2,0},{3,1},{4,6},{5,7},{6,4},{7,5},{8,10},{9,11},{10,... | collective-permute-start | bytes 196616 | tf_op jit(solution)/shard_map/chunk1_step2/ppermute | solution.py:351
  61.1 6.7 %collective-permute-start.18 = (bf16[6,1,32,256]{3,2,1,0:T(8,128)(2,1)S(1)}, bf16[6,1,32,256]{3,2,1,0:T(8,128)(2,1)S(1)}, u32[]{:S(2)}, u32[]{:S(2)}) collective-permute-start(bf16[6,1,32,256]{3,2,1,0:T(8,128)(2,1)S(1)} %get-tuple-element.109), channel_id=1, source_target_pairs={{0,8},{1,9},{2,10},{3,11},{4,12},{5,13},{6,14},{7,15},{8,0},{9,1},... | collective-permute-start | bytes 294920 | tf_op jit(solution)/shard_map/chunk3_step2/ppermute | solution.py:351
  63.2 5.0 %collective-permute-start.22 = (bf16[2,2,32,256]{3,2,1,0:T(8,128)(2,1)S(1)}, bf16[2,2,32,256]{3,2,1,0:T(8,128)(2,1)S(1)}, u32[]{:S(2)}, u32[]{:S(2)}) collective-permute-start(bf16[2,2,32,256]{3,2,1,0:T(8,128)(2,1)S(1)} %get-tuple-element.116), channel_id=1, source_target_pairs={{0,4},{1,5},{2,6},{3,7},{4,0},{5,1},{6,2},{7,3},{8,12},{9,13},{10,... | collective-permute-start | bytes 196616 | tf_op jit(solution)/shard_map/chunk5_step1/ppermute | solution.py:351
  65.7 7.5 %collective-permute-start.24 = (f32[8,16,256]{2,1,0:T(8,128)S(1)}, f32[8,16,256]{2,1,0:T(8,128)S(1)}, u32[]{:S(2)}, u32[]{:S(2)}) collective-permute-start(f32[8,16,256]{2,1,0:T(8,128)S(1)} %get-tuple-element.121), channel_id=1, source_target_pairs={{0,1},{1,0},{2,3},{3,2},{4,5},{5,4},{6,7},{7,6},{8,9},{9,8},{10,11... | collective-permute-start | bytes 393224 | tf_op jit(solution)/shard_map/chunk0_step3/ppermute | solution.py:351
  65.7 6.4 %collective-permute-start.21 = (bf16[4,1,32,256]{3,2,1,0:T(8,128)(2,1)S(1)}, bf16[4,1,32,256]{3,2,1,0:T(8,128)(2,1)S(1)}, u32[]{:S(2)}, u32[]{:S(2)}) collective-permute-start(bf16[4,1,32,256]{3,2,1,0:T(8,128)(2,1)S(1)} %get-tuple-element.115), channel_id=1, source_target_pairs={{0,8},{1,9},{2,10},{3,11},{4,12},{5,13},{6,14},{7,15},{8,0},{9,1},... | collective-permute-start | bytes 196616 | tf_op jit(solution)/shard_map/chunk4_step2/ppermute | solution.py:351
  66.2 7.6 %collective-permute-start.26 = (f32[8,16,256]{2,1,0:T(8,128)S(1)}, f32[8,16,256]{2,1,0:T(8,128)S(1)}, u32[]{:S(2)}, u32[]{:S(2)}) collective-permute-start(f32[8,16,256]{2,1,0:T(8,128)S(1)} %get-tuple-element.123), channel_id=1, source_target_pairs={{0,1},{1,0},{2,3},{3,2},{4,5},{5,4},{6,7},{7,6},{8,9},{9,8},{10,11... | collective-permute-start | bytes 393224 | tf_op jit(solution)/shard_map/chunk2_step3/ppermute | solution.py:351
  68.1 5.0 %collective-permute-start.23 = (bf16[2,1,32,256]{3,2,1,0:T(8,128)(2,1)S(1)}, bf16[2,1,32,256]{3,2,1,0:T(8,128)(2,1)S(1)}, u32[]{:S(2)}, u32[]{:S(2)}) collective-permute-start(bf16[2,1,32,256]{3,2,1,0:T(8,128)(2,1)S(1)} %get-tuple-element.119), channel_id=1, source_target_pairs={{0,8},{1,9},{2,10},{3,11},{4,12},{5,13},{6,14},{7,15},{8,0},{9,1},... | collective-permute-start | bytes 98312 | tf_op jit(solution)/shard_map/chunk5_step2/ppermute | solution.py:351
  69.1 5.6 %collective-permute-start.27 = (f32[6,16,256]{2,1,0:T(8,128)S(1)}, f32[6,16,256]{2,1,0:T(8,128)S(1)}, u32[]{:S(2)}, u32[]{:S(2)}) collective-permute-start(f32[6,16,256]{2,1,0:T(8,128)S(1)} %get-tuple-element.124), channel_id=1, source_target_pairs={{0,1},{1,0},{2,3},{3,2},{4,5},{5,4},{6,7},{7,6},{8,9},{9,8},{10,11... | collective-permute-start | bytes 294920 | tf_op jit(solution)/shard_map/chunk3_step3/ppermute | solution.py:351
  72.2 1.6 %collective-permute-start.25 = (f32[4,16,256]{2,1,0:T(8,128)S(1)}, f32[4,16,256]{2,1,0:T(8,128)S(1)}, u32[]{:S(2)}, u32[]{:S(2)}) collective-permute-start(f32[4,16,256]{2,1,0:T(8,128)S(1)} %get-tuple-element.122), channel_id=1, source_target_pairs={{0,1},{1,0},{2,3},{3,2},{4,5},{5,4},{6,7},{7,6},{8,9},{9,8},{10,11... | collective-permute-start | bytes 196616 | tf_op jit(solution)/shard_map/chunk1_step3/ppermute | solution.py:351
  73.2 1.5 %collective-permute-start.28 = (f32[4,16,256]{2,1,0:T(8,128)S(1)}, f32[4,16,256]{2,1,0:T(8,128)S(1)}, u32[]{:S(2)}, u32[]{:S(2)}) collective-permute-start(f32[4,16,256]{2,1,0:T(8,128)S(1)} %get-tuple-element.125), channel_id=1, source_target_pairs={{0,1},{1,0},{2,3},{3,2},{4,5},{5,4},{6,7},{7,6},{8,9},{9,8},{10,11... | collective-permute-start | bytes 196616 | tf_op jit(solution)/shard_map/chunk4_step3/ppermute | solution.py:351
  73.2 1.4 %collective-permute-start.29 = (f32[2,16,256]{2,1,0:T(8,128)S(1)}, f32[2,16,256]{2,1,0:T(8,128)S(1)}, u32[]{:S(2)}, u32[]{:S(2)}) collective-permute-start(f32[2,16,256]{2,1,0:T(8,128)S(1)} %get-tuple-element.126), channel_id=1, source_target_pairs={{0,1},{1,0},{2,3},{3,2},{4,5},{5,4},{6,7},{7,6},{8,9},{9,8},{10,11... | collective-permute-start | bytes 98312 | tf_op jit(solution)/shard_map/chunk5_step3/ppermute | solution.py:351

commit v4 on v3

--- a/solution.py
+++ b/solution.py
@@ -269,55 +269,65 @@
 
 def finish_body(chunks, *refs):
     count = len(chunks)
-    mine, theirs = refs[:count], refs[count : 2 * count]
-    gate_ref, gain_ref, bias_ref, w_ref, out_ref, hold = refs[2 * count :]
-    hidden, _ = w_ref.shape
+    parts = refs[:count], refs[count : 2 * count]
+    gate_ref, gain_ref, bias_ref, w_ref, all_ref, hold, wide_ref, out_ref, sems = refs[2 * count :]
+    hidden, chan = w_ref.shape
     half = hidden // 2
     rows, width, _ = gate_ref.shape
     stride = hold.shape[1] // hidden
-    core = lax.axis_index("row") % 2
-
-    @pl.when(pl.program_id(0) == 0)
-    def _():
-        sums = []
-        first = 0
-        for chunk, size in enumerate(chunks):
-            for part in range(2):
-                for h in range(size):
-                    index = jnp.where(core == part, 0, half) + first + h
-                    sums.append((index, (mine, theirs)[part][chunk][h]))
-            first += size
-        mean_val = sum(value for _, value in sums) * (1.0 / hidden)
-        square = sum((value - mean_val) * (value - mean_val) for _, value in sums)
-        scale = lax.rsqrt(square * (1.0 / hidden) + EPS)
-        for index, value in sums:
-            value = (value - mean_val) * scale * gain_ref[index] + bias_ref[index]
-            for lane in range(width // LANES):
-                hold[lane, pl.ds(index * stride, rows), :] = value[:, lane * LANES : (lane + 1) * LANES]
-
-    weights = w_ref[...]
-    for near in range(out_ref.shape[0]):
-        row = pl.program_id(0) * out_ref.shape[0] + near
+
+    values = [part[h] for side in parts for part in side for h in range(part.shape[0])]
+    mean_val = sum(values) * (1.0 / hidden)
+    square = sum((value - mean_val) * (value - mean_val) for value in values)
+    scale = lax.rsqrt(square * (1.0 / hidden) + EPS)
+    base = lax.axis_index("row") % 2 * half
+    for place, value in enumerate(values):
+        index = base + place if place < half else place - base
+        value = (value - mean_val) * scale * gain_ref[index] + bias_ref[index]
         for lane in range(width // LANES):
-            normed = hold[lane, pl.ds(row, hidden, stride=stride), :].astype(bf16)
+            hold[lane, place * stride : place * stride + rows, :] = value[:, lane * LANES : (lane + 1) * LANES]
+    wide_ref[...] = jnp.zeros_like(wide_ref)
+    for place, start in ((0, base), (half, half - base)):
+        block = w_ref[pl.ds(pl.multiple_of(start, half), half), :]
+        wide_ref[place : place + half, :chan] = block
+        wide_ref[hidden + place : hidden + place + half, chan:] = block
+
+    weights = wide_ref[...]
+    copies = []
+    for row in range(0, rows, 2):
+        for lane in range(width // LANES):
+            pair = [hold[lane, pl.ds(row + n, hidden, stride=stride), :].astype(bf16) for n in range(2)]
+            normed = jnp.concatenate(pair, axis=0)
             mixed = lax.dot_general(normed, weights, (((0,), (0,)), ((), ())), preferred_element_type=f32)
             span = pl.ds(lane * LANES, LANES)
-            out_ref[near, span, :] = (gate_ref[row, span, :] * mixed).astype(bf16)
+            for n in range(2):
+                value = gate_ref[row + n, span, :] * mixed[:, n * chan : (n + 1) * chan]
+                out_ref[row + n, span, :] = value.astype(bf16)
+        if row % 4 == 2:
+            block = pl.ds(row - 2, 4)
+            copies.append(pltpu.make_async_copy(out_ref.at[block], all_ref.at[block], sems.at[row // 4]))
+            copies[-1].start()
+    for copy in copies:
+        copy.wait()
 
 
 def finish(mine, theirs, gate_act, gain, bias, w_out, chunks):
     rows, width, chan = gate_act.shape
     hidden = w_out.shape[0]
-    step = 4
-    stride = rows + 4
+    stride = rows + 8
     smem = pl.BlockSpec(memory_space=pltpu.SMEM)
     return call(
         functools.partial(finish_body, chunks),
-        (rows // step,),
+        (1,),
         [IN_PLACE] * (2 * len(mine) + 1) + [smem, smem, IN_PLACE],
-        pl.BlockSpec((step, width, chan), lambda i: (i, 0, 0)),
+        pl.BlockSpec(memory_space=pltpu.HBM),
         jax.ShapeDtypeStruct((rows, width, chan), bf16),
-        [pltpu.VMEM((width // LANES, hidden * stride, LANES), f32)],
+        [
+            pltpu.VMEM((width // LANES, hidden * stride, LANES), f32),
+            pltpu.VMEM((2 * hidden, 2 * chan), bf16),
+            pltpu.VMEM((rows, width, chan), bf16),
+            pltpu.SemaphoreType.DMA((rows // 4,)),
+        ],
         (2 * rows * width * chan * hidden, rows * width * (chan * 6 + hidden * 4)),
         (*mine, *theirs, gate_act, gain, bias, w_out),
     )
@@ -329,7 +339,7 @@
         late = order[0] != 1
         for step in range(len(order) + 1):
             if late:
-                time = step + (step == len(order))
+                time = step + 2 * (step == len(order))
             else:
                 time = turn + step if step else max(turn - 1, 0)
             events.append((time, step == 0, late and step > 0, step, chunk))
@@ -343,7 +353,7 @@
     bits = devices.bit_length() - 1
     unit = w_out.shape[0] // 32
     z_last, z_first = tuple(range(1, bits)), tuple(range(2, bits)) + (1,)
-    plan = ((4, z_last), (2, z_first), (4, z_last), (3, z_last), (2, z_last), (1, z_last))
+    plan = ((4, z_last), (3, z_first), (4, z_last), (3, z_last), (2, z_last))
     chunks, orders = tuple(size * unit for size, _ in plan), tuple(order for _, order in plan)
     count = len(chunks)
 

time: 78.1 us -> 72.2 us (0.924)
  starting transfers between devices: 33.2 us -> 30.8 us
  waiting for transfers between devices: 25.2 us -> 23.1 us
  Pallas kernels: 19.2 us -> 17.8 us
    ppermute x30 -> x25, starting transfers between devices: 33.2 us -> 30.8 us  [swap(): lax.ppermute(values, 'row', [(d, d ^ 1 << bit) for d in range(devices)])]
    ppermute x30 -> x25, waiting for transfers between devices: 25.2 us -> 23.1 us  [swap(): lax.ppermute(values, 'row', [(d, d ^ 1 << bit) for d in range(devices)])]
    pallas_call x27 -> x23, Pallas kernels: 19.2 us -> 17.8 us  [call(): pl.pallas_call(run, grid=grid, in_specs=list(in_specs) + [corner(array.sh...]
  transfers between devices with their start and end apart: 30 -> 25, of which waited for: 11 -> 11; matrix products, arithmetic and copies ran while one was open for 0% -> 0% of each run, Pallas kernels for 6% -> 6%
where the time goes in v4:
time: 72.2 us; the launch traced here: 72 us
  starting transfers between devices  30.8 us (43%)
  waiting for transfers between devices  23.1 us (32%)
  Pallas kernels  17.8 us (25%)
    ppermute x25, starting transfers between devices, swap(): lax.ppermute(values, 'row', [(d, d ^ 1 << bit) for d in range(devices)])  30.8 us
    ppermute x25, waiting for transfers between devices, swap(): lax.ppermute(values, 'row', [(d, d ^ 1 << bit) for d in range(devices)])  23.1 us
    pallas_call x23, Pallas kernels, call(): pl.pallas_call(run, grid=grid, in_specs=list(in_specs) + [corner(array.sh...  17.8 us
  transfers between devices with their start and end apart: 25, of which 11 were waited for; matrix products, arithmetic and copies ran while one was open for 0% of the time, Pallas kernels for 6%

profile of v4, /device:TPU:0, one launch (start us, length us, event | category | flops | bytes accessed | tf_op | source)
XLA Modules:
  0.0 72.0 jit_solution(12779744491182025729)
XLA Ops:
  0.0 11.0 %shard_map.91 = (bf16[2,8,96,256]{3,2,1,0:T(8,128)(2,1)S(1)}, bf16[2,6,96,256]{3,2,1,0:T(8,128)(2,1)S(1)}, bf16[2,8,96,256]{3,2,1,0:T(8,128)(2,1)S(1)}, bf16[2,6...) custom-call(bf16[96,256,128]{2,1,0:T(8,128)(2,1)} %refs_0_.1, ...), custom_call_target="tpu_custom_call" | custom-call | flops 1610612736 | bytes 12582912 | tf_op jit(solution)/shard_map/pallas_call | solution.py:34
  11.0 0.5 collective-permute-start
  11.5 0.1 collective-permute-start.2
  11.6 0.4 collective-permute-start.3
  12.1 0.1 collective-permute-start.6
  12.1 1.3 %collective-permute-done.refs_1_ = bf16[2,8,96,256]{3,2,1,0:T(8,128)(2,1)S(1)} collective-permute-done((bf16[2,8,96,256]{3,2,1,0:T(8,128)(2,1)S(1)}, bf16[2,8,96,256]{3,2,1,0:T(8,128)(2,1)S(1)}, u32[]{:S(2)}, u32[]{:S(2)}) %collective-permute-start) | collective-permute-done | bytes 786464 | tf_op jit(solution)/shard_map/ppermute | solution.py:361
  13.5 0.6 chunk0_step0.1
  14.0 2.9 %collective-permute-start.1 = (bf16[8,4,32,256]{3,2,1,0:T(8,128)(2,1)S(1)}, bf16[8,4,32,256]{3,2,1,0:T(8,128)(2,1)S(1)}, u32[]{:S(2)}, u32[]{:S(2)}) collective-permute-start(bf16[8,4,32,256]{3,2,1,0:T(8,128)(2,1)S(1)} %get-tuple-element.59), channel_id=1, source_target_pairs={{0,2},{1,3},{2,0},{3,1},{4,6},{5,7},{6,4},{7,5},{8,10},{9,11},{10,... | collective-permute-start | bytes 1572872 | tf_op jit(solution)/shard_map/chunk0_step0/ppermute | solution.py:361
  17.0 0.5 chunk1_step0.1
  17.5 1.7 %collective-permute-start.7 = (bf16[6,4,32,256]{3,2,1,0:T(8,128)(2,1)S(1)}, bf16[6,4,32,256]{3,2,1,0:T(8,128)(2,1)S(1)}, u32[]{:S(2)}, u32[]{:S(2)}) collective-permute-start(bf16[6,4,32,256]{3,2,1,0:T(8,128)(2,1)S(1)} %get-tuple-element.72), channel_id=1, source_target_pairs={{0,4},{1,5},{2,6},{3,7},{4,0},{5,1},{6,2},{7,3},{8,12},{9,13},{10,... | collective-permute-start | bytes 1179656 | tf_op jit(solution)/shard_map/chunk1_step0/ppermute | solution.py:361
  19.1 1.3 %shard_map.92.refs_2_.refs_10_ = f32[16,256,128]{2,1,0:T(8,128)S(1)} custom-call(bf16[16,256,128]{2,1,0:T(8,128)(2,1)S(1)} %get-tuple-element.62.refs_0_, f32[1,128]{1,0:T(1,128)S(1)} %bitcast.3, f32[1,128]{1,0:T(1,128)S(1)} %bitcast.5, bf16[128,128]{1,0:T(8,128)(2,1)S(1)} %copy-done, f32[6,4,32,256]{3,2,1,0:T(8,128)S(1)} %get-tuple-element.65.refs_4_.refs_0_), custom_call_target="tpu_custom_call" | custom-call | flops 134217728 | bytes 3145728 | tf_op jit(solution)/shard_map/pallas_call | solution.py:34
  20.4 0.6 chunk2_step0.1
  21.0 1.4 %collective-permute-start.5 = (bf16[8,4,32,256]{3,2,1,0:T(8,128)(2,1)S(1)}, bf16[8,4,32,256]{3,2,1,0:T(8,128)(2,1)S(1)}, u32[]{:S(2)}, u32[]{:S(2)}) collective-permute-start(bf16[8,4,32,256]{3,2,1,0:T(8,128)(2,1)S(1)} %get-tuple-element.69), channel_id=1, source_target_pairs={{0,2},{1,3},{2,0},{3,1},{4,6},{5,7},{6,4},{7,5},{8,10},{9,11},{10,... | collective-permute-start | bytes 1572872 | tf_op jit(solution)/shard_map/chunk2_step0/ppermute | solution.py:361
  22.4 7.3 %collective-permute-done.1.refs_1_ = bf16[8,4,32,256]{3,2,1,0:T(8,128)(2,1)S(1)} collective-permute-done((bf16[8,4,32,256]{3,2,1,0:T(8,128)(2,1)S(1)}, bf16[8,4,32,256]{3,2,1,0:T(8,128)(2,1)S(1)}, u32[]{:S(2)}, u32[]{:S(2)}) %collective-permute-start.1) | collective-permute-done | bytes 524320 | tf_op jit(solution)/shard_map/chunk0_step0/ppermute | solution.py:361
  29.7 0.1 chunk0_step1.1
  29.8 2.2 %collective-permute-start.4 = (bf16[8,2,32,256]{3,2,1,0:T(8,128)(2,1)S(1)}, bf16[8,2,32,256]{3,2,1,0:T(8,128)(2,1)S(1)}, u32[]{:S(2)}, u32[]{:S(2)}) collective-permute-start(bf16[8,2,32,256]{3,2,1,0:T(8,128)(2,1)S(1)} %get-tuple-element.68), channel_id=1, source_target_pairs={{0,4},{1,5},{2,6},{3,7},{4,0},{5,1},{6,2},{7,3},{8,12},{9,13},{10,... | collective-permute-start | bytes 786440 | tf_op jit(solution)/shard_map/chunk0_step1/ppermute | solution.py:361
  32.0 0.1 chunk1_step1.1
  32.1 0.5 chunk3_step0.1
  32.6 1.6 %collective-permute-start.10 = (bf16[6,4,32,256]{3,2,1,0:T(8,128)(2,1)S(1)}, bf16[6,4,32,256]{3,2,1,0:T(8,128)(2,1)S(1)}, u32[]{:S(2)}, u32[]{:S(2)}) collective-permute-start(bf16[6,4,32,256]{3,2,1,0:T(8,128)(2,1)S(1)} %get-tuple-element.79), channel_id=1, source_target_pairs={{0,2},{1,3},{2,0},{3,1},{4,6},{5,7},{6,4},{7,5},{8,10},{9,11},{10,... | collective-permute-start | bytes 1179656 | tf_op jit(solution)/shard_map/chunk3_step0/ppermute | solution.py:361
  34.2 2.6 %collective-permute-start.12 = (bf16[6,2,32,256]{3,2,1,0:T(8,128)(2,1)S(1)}, bf16[6,2,32,256]{3,2,1,0:T(8,128)(2,1)S(1)}, u32[]{:S(2)}, u32[]{:S(2)}) collective-permute-start(bf16[6,2,32,256]{3,2,1,0:T(8,128)(2,1)S(1)} %get-tuple-element.82), channel_id=1, source_target_pairs={{0,8},{1,9},{2,10},{3,11},{4,12},{5,13},{6,14},{7,15},{8,0},{9,1},... | collective-permute-start | bytes 589832 | tf_op jit(solution)/shard_map/chunk1_step1/ppermute | solution.py:361
  36.8 4.2 %collective-permute-done.5.refs_1_ = bf16[8,4,32,256]{3,2,1,0:T(8,128)(2,1)S(1)} collective-permute-done((bf16[8,4,32,256]{3,2,1,0:T(8,128)(2,1)S(1)}, bf16[8,4,32,256]{3,2,1,0:T(8,128)(2,1)S(1)}, u32[]{:S(2)}, u32[]{:S(2)}) %collective-permute-start.5) | collective-permute-done | bytes 524320 | tf_op jit(solution)/shard_map/chunk2_step0/ppermute | solution.py:361
  40.9 0.1 chunk2_step1.1
  41.1 2.2 %collective-permute-start.9 = (bf16[8,2,32,256]{3,2,1,0:T(8,128)(2,1)S(1)}, bf16[8,2,32,256]{3,2,1,0:T(8,128)(2,1)S(1)}, u32[]{:S(2)}, u32[]{:S(2)}) collective-permute-start(bf16[8,2,32,256]{3,2,1,0:T(8,128)(2,1)S(1)} %get-tuple-element.78), channel_id=1, source_target_pairs={{0,4},{1,5},{2,6},{3,7},{4,0},{5,1},{6,2},{7,3},{8,12},{9,13},{10,... | collective-permute-start | bytes 786440 | tf_op jit(solution)/shard_map/chunk2_step1/ppermute | solution.py:361
  43.3 0.9 %collective-permute-done.12.refs_1_ = bf16[6,2,32,256]{3,2,1,0:T(8,128)(2,1)S(1)} collective-permute-done((bf16[6,2,32,256]{3,2,1,0:T(8,128)(2,1)S(1)}, bf16[6,2,32,256]{3,2,1,0:T(8,128)(2,1)S(1)}, u32[]{:S(2)}, u32[]{:S(2)}) %collective-permute-start.12) | collective-permute-done | bytes 196640 | tf_op jit(solution)/shard_map/chunk1_step1/ppermute | solution.py:361
  44.2 0.4 chunk4_step0.1
  44.6 0.7 %collective-permute-start.15 = (bf16[4,4,32,256]{3,2,1,0:T(8,128)(2,1)S(1)}, bf16[4,4,32,256]{3,2,1,0:T(8,128)(2,1)S(1)}, u32[]{:S(2)}, u32[]{:S(2)}) collective-permute-start(bf16[4,4,32,256]{3,2,1,0:T(8,128)(2,1)S(1)} %get-tuple-element.90), channel_id=1, source_target_pairs={{0,2},{1,3},{2,0},{3,1},{4,6},{5,7},{6,4},{7,5},{8,10},{9,11},{10,... | collective-permute-start | bytes 786440 | tf_op jit(solution)/shard_map/chunk4_step0/ppermute | solution.py:361
  45.4 2.6 %collective-permute-start.8 = (bf16[8,1,32,256]{3,2,1,0:T(8,128)(2,1)S(1)}, bf16[8,1,32,256]{3,2,1,0:T(8,128)(2,1)S(1)}, u32[]{:S(2)}, u32[]{:S(2)}) collective-permute-start(bf16[8,1,32,256]{3,2,1,0:T(8,128)(2,1)S(1)} %get-tuple-element.77), channel_id=1, source_target_pairs={{0,8},{1,9},{2,10},{3,11},{4,12},{5,13},{6,14},{7,15},{8,0},{9,1},... | collective-permute-start | bytes 393224 | tf_op jit(solution)/shard_map/chunk0_step2/ppermute | solution.py:361
  47.9 1.4 %collective-permute-done.10.refs_1_ = bf16[6,4,32,256]{3,2,1,0:T(8,128)(2,1)S(1)} collective-permute-done((bf16[6,4,32,256]{3,2,1,0:T(8,128)(2,1)S(1)}, bf16[6,4,32,256]{3,2,1,0:T(8,128)(2,1)S(1)}, u32[]{:S(2)}, u32[]{:S(2)}) %collective-permute-start.10) | collective-permute-done | bytes 393248 | tf_op jit(solution)/shard_map/chunk3_step0/ppermute | solution.py:361
  49.3 0.1 chunk3_step1.1
  49.4 2.2 %collective-permute-start.14 = (bf16[6,2,32,256]{3,2,1,0:T(8,128)(2,1)S(1)}, bf16[6,2,32,256]{3,2,1,0:T(8,128)(2,1)S(1)}, u32[]{:S(2)}, u32[]{:S(2)}) collective-permute-start(bf16[6,2,32,256]{3,2,1,0:T(8,128)(2,1)S(1)} %get-tuple-element.89), channel_id=1, source_target_pairs={{0,4},{1,5},{2,6},{3,7},{4,0},{5,1},{6,2},{7,3},{8,12},{9,13},{10,... | collective-permute-start | bytes 589832 | tf_op jit(solution)/shard_map/chunk3_step1/ppermute | solution.py:361
  51.6 0.3 collective-permute-done.9.refs_1_
  52.0 2.3 %collective-permute-start.18 = (bf16[8,1,32,256]{3,2,1,0:T(8,128)(2,1)S(1)}, bf16[8,1,32,256]{3,2,1,0:T(8,128)(2,1)S(1)}, u32[]{:S(2)}, u32[]{:S(2)}) collective-permute-start(bf16[8,1,32,256]{3,2,1,0:T(8,128)(2,1)S(1)} %get-tuple-element.95), channel_id=1, source_target_pairs={{0,8},{1,9},{2,10},{3,11},{4,12},{5,13},{6,14},{7,15},{8,0},{9,1},... | collective-permute-start | bytes 393224 | tf_op jit(solution)/shard_map/chunk2_step2/ppermute | solution.py:361
  54.3 0.1 chunk0_step3.1
  54.4 0.1 collective-permute-done.15.refs_1_
  54.5 1.9 %collective-permute-start.17 = (bf16[4,2,32,256]{3,2,1,0:T(8,128)(2,1)S(1)}, bf16[4,2,32,256]{3,2,1,0:T(8,128)(2,1)S(1)}, u32[]{:S(2)}, u32[]{:S(2)}) collective-permute-start(bf16[4,2,32,256]{3,2,1,0:T(8,128)(2,1)S(1)} %get-tuple-element.94), channel_id=1, source_target_pairs={{0,4},{1,5},{2,6},{3,7},{4,0},{5,1},{6,2},{7,3},{8,12},{9,13},{10,... | collective-permute-start | bytes 393224 | tf_op jit(solution)/shard_map/chunk4_step1/ppermute | solution.py:361
  56.4 3.3 %collective-permute-done.14.refs_1_ = bf16[6,2,32,256]{3,2,1,0:T(8,128)(2,1)S(1)} collective-permute-done((bf16[6,2,32,256]{3,2,1,0:T(8,128)(2,1)S(1)}, bf16[6,2,32,256]{3,2,1,0:T(8,128)(2,1)S(1)}, u32[]{:S(2)}, u32[]{:S(2)}) %collective-permute-start.14) | collective-permute-done | bytes 196640 | tf_op jit(solution)/shard_map/chunk3_step1/ppermute | solution.py:361
  59.7 1.6 %collective-permute-start.16 = (bf16[6,1,32,256]{3,2,1,0:T(8,128)(2,1)S(1)}, bf16[6,1,32,256]{3,2,1,0:T(8,128)(2,1)S(1)}, u32[]{:S(2)}, u32[]{:S(2)}) collective-permute-start(bf16[6,1,32,256]{3,2,1,0:T(8,128)(2,1)S(1)} %get-tuple-element.93), channel_id=1, source_target_pairs={{0,8},{1,9},{2,10},{3,11},{4,12},{5,13},{6,14},{7,15},{8,0},{9,1},... | collective-permute-start | bytes 294920 | tf_op jit(solution)/shard_map/chunk3_step2/ppermute | solution.py:361
  61.3 1.2 %collective-permute-start.13 = (bf16[6,1,32,256]{3,2,1,0:T(8,128)(2,1)S(1)}, bf16[6,1,32,256]{3,2,1,0:T(8,128)(2,1)S(1)}, u32[]{:S(2)}, u32[]{:S(2)}) collective-permute-start(bf16[6,1,32,256]{3,2,1,0:T(8,128)(2,1)S(1)} %get-tuple-element.88), channel_id=1, source_target_pairs={{0,2},{1,3},{2,0},{3,1},{4,6},{5,7},{6,4},{7,5},{8,10},{9,11},{10,... | collective-permute-start | bytes 294920 | tf_op jit(solution)/shard_map/chunk1_step2/ppermute | solution.py:361
  62.6 0.1 chunk2_step3.1
  62.6 0.1 collective-permute-done.17.refs_1_
  62.8 1.4 %collective-permute-start.19 = (bf16[4,1,32,256]{3,2,1,0:T(8,128)(2,1)S(1)}, bf16[4,1,32,256]{3,2,1,0:T(8,128)(2,1)S(1)}, u32[]{:S(2)}, u32[]{:S(2)}) collective-permute-start(bf16[4,1,32,256]{3,2,1,0:T(8,128)(2,1)S(1)} %get-tuple-element.100), channel_id=1, source_target_pairs={{0,8},{1,9},{2,10},{3,11},{4,12},{5,13},{6,14},{7,15},{8,0},{9,1},... | collective-permute-start | bytes 196616 | tf_op jit(solution)/shard_map/chunk4_step2/ppermute | solution.py:361
  64.2 0.5 collective-permute-start.22
  64.7 3.0 %collective-permute-done.16.refs_1_ = bf16[6,1,32,256]{3,2,1,0:T(8,128)(2,1)S(1)} collective-permute-done((bf16[6,1,32,256]{3,2,1,0:T(8,128)(2,1)S(1)}, bf16[6,1,32,256]{3,2,1,0:T(8,128)(2,1)S(1)}, u32[]{:S(2)}, u32[]{:S(2)}) %collective-permute-start.16) | collective-permute-done | bytes 98336 | tf_op jit(solution)/shard_map/chunk3_step2/ppermute | solution.py:361
  67.8 0.1 collective-permute-start.21
  67.9 0.5 collective-permute-start.23
  68.5 0.1 collective-permute-start.24
  68.6 1.2 %collective-permute-done.24.refs_9_ = f32[4,16,256]{2,1,0:T(8,128)S(1)} collective-permute-done((f32[4,16,256]{2,1,0:T(8,128)S(1)}, f32[4,16,256]{2,1,0:T(8,128)S(1)}, u32[]{:S(2)}, u32[]{:S(2)}) %collective-permute-start.24) | collective-permute-done | bytes 65568 | tf_op jit(solution)/shard_map/chunk4_step3/ppermute | solution.py:361
  69.8 2.2 %shard_map.93 = bf16[16,256,128]{2,1,0:T(8,128)(2,1)} custom-call(f32[8,16,256]{2,1,0:T(8,128)S(1)} %get-tuple-element.87.refs_2_.refs_0_, f32[6,16,256]{2,1,0:T(8,128)S(1)} %get-tuple-element.99.refs_2_.refs_1_, f32[8,16,256]{2,1,0:T(8,128)S(1)} %get-tuple-element.96.refs_2_, f32[6,16,256]{2,1,0:T(8,128)S(1)} %get-tuple-element.98.refs_2_.refs_3_, ...), custom_call_target="tpu_custom_call" | custom-call | flops 67108864 | bytes 4194304 | tf_op jit(solution)/shard_map/pallas_call | solution.py:34
  (37 shorter events, 0.4 us)
Async XLA Ops:
  0.0 19.1 %copy-start.3 = (f32[128]{0:T(128)S(1)}, f32[128]{0:T(128)}, u32[]{:S(2)}) copy-start(f32[128]{0:T(128)} %param.12) | copy-start | bytes 1540
  0.0 19.1 %copy-start.2 = (f32[128]{0:T(128)S(1)}, f32[128]{0:T(128)}, u32[]{:S(2)}) copy-start(f32[128]{0:T(128)} %param.11) | copy-start | bytes 1540
  0.0 19.1 %copy-start = (bf16[128,128]{1,0:T(8,128)(2,1)S(1)}, bf16[128,128]{1,0:T(8,128)(2,1)}, u32[]{:S(2)}) copy-start(bf16[128,128]{1,0:T(8,128)(2,1)} %refs_3_.1) | copy-start | bytes 98308
  11.0 2.5 %collective-permute-start = (bf16[2,8,96,256]{3,2,1,0:T(8,128)(2,1)S(1)}, bf16[2,8,96,256]{3,2,1,0:T(8,128)(2,1)S(1)}, u32[]{:S(2)}, u32[]{:S(2)}) collective-permute-start(bf16[2,8,96,256]{3,2,1,0:T(8,128)(2,1)S(1)} %get-tuple-element.57), channel_id=1, source_target_pairs={{0,1},{1,0},{2,3},{3,2},{4,5},{5,4},{6,7},{7,6},{8,9},{9,8},{10,11... | collective-permute-start | bytes 2359304 | tf_op jit(solution)/shard_map/ppermute | solution.py:361
  11.5 8.9 %collective-permute-start.2 = (bf16[2,8,96,256]{3,2,1,0:T(8,128)(2,1)S(1)}, bf16[2,8,96,256]{3,2,1,0:T(8,128)(2,1)S(1)}, u32[]{:S(2)}, u32[]{:S(2)}) collective-permute-start(bf16[2,8,96,256]{3,2,1,0:T(8,128)(2,1)S(1)} %get-tuple-element.61), channel_id=1, source_target_pairs={{0,1},{1,0},{2,3},{3,2},{4,5},{5,4},{6,7},{7,6},{8,9},{9,8},{10,11... | collective-permute-start | bytes 2359304 | tf_op jit(solution)/shard_map/ppermute | solution.py:361
  11.6 5.3 %collective-permute-start.3 = (bf16[2,6,96,256]{3,2,1,0:T(8,128)(2,1)S(1)}, bf16[2,6,96,256]{3,2,1,0:T(8,128)(2,1)S(1)}, u32[]{:S(2)}, u32[]{:S(2)}) collective-permute-start(bf16[2,6,96,256]{3,2,1,0:T(8,128)(2,1)S(1)} %get-tuple-element.64), channel_id=1, source_target_pairs={{0,1},{1,0},{2,3},{3,2},{4,5},{5,4},{6,7},{7,6},{8,9},{9,8},{10,11... | collective-permute-start | bytes 1769480 | tf_op jit(solution)/shard_map/ppermute | solution.py:361
  12.1 20.0 %collective-permute-start.6 = (bf16[2,6,96,256]{3,2,1,0:T(8,128)(2,1)S(1)}, bf16[2,6,96,256]{3,2,1,0:T(8,128)(2,1)S(1)}, u32[]{:S(2)}, u32[]{:S(2)}) collective-permute-start(bf16[2,6,96,256]{3,2,1,0:T(8,128)(2,1)S(1)} %get-tuple-element.71), channel_id=1, source_target_pairs={{0,1},{1,0},{2,3},{3,2},{4,5},{5,4},{6,7},{7,6},{8,9},{9,8},{10,11... | collective-permute-start | bytes 1769480 | tf_op jit(solution)/shard_map/ppermute | solution.py:361
  14.0 15.6 %collective-permute-start.1 = (bf16[8,4,32,256]{3,2,1,0:T(8,128)(2,1)S(1)}, bf16[8,4,32,256]{3,2,1,0:T(8,128)(2,1)S(1)}, u32[]{:S(2)}, u32[]{:S(2)}) collective-permute-start(bf16[8,4,32,256]{3,2,1,0:T(8,128)(2,1)S(1)} %get-tuple-element.59), channel_id=1, source_target_pairs={{0,2},{1,3},{2,0},{3,1},{4,6},{5,7},{6,4},{7,5},{8,10},{9,11},{10,... | collective-permute-start | bytes 1572872 | tf_op jit(solution)/shard_map/chunk0_step0/ppermute | solution.py:361
  17.5 14.5 %collective-permute-start.7 = (bf16[6,4,32,256]{3,2,1,0:T(8,128)(2,1)S(1)}, bf16[6,4,32,256]{3,2,1,0:T(8,128)(2,1)S(1)}, u32[]{:S(2)}, u32[]{:S(2)}) collective-permute-start(bf16[6,4,32,256]{3,2,1,0:T(8,128)(2,1)S(1)} %get-tuple-element.72), channel_id=1, source_target_pairs={{0,4},{1,5},{2,6},{3,7},{4,0},{5,1},{6,2},{7,3},{8,12},{9,13},{10,... | collective-permute-start | bytes 1179656 | tf_op jit(solution)/shard_map/chunk1_step0/ppermute | solution.py:361
  21.0 19.9 %collective-permute-start.5 = (bf16[8,4,32,256]{3,2,1,0:T(8,128)(2,1)S(1)}, bf16[8,4,32,256]{3,2,1,0:T(8,128)(2,1)S(1)}, u32[]{:S(2)}, u32[]{:S(2)}) collective-permute-start(bf16[8,4,32,256]{3,2,1,0:T(8,128)(2,1)S(1)} %get-tuple-element.69), channel_id=1, source_target_pairs={{0,2},{1,3},{2,0},{3,1},{4,6},{5,7},{6,4},{7,5},{8,10},{9,11},{10,... | collective-permute-start | bytes 1572872 | tf_op jit(solution)/shard_map/chunk2_step0/ppermute | solution.py:361
  22.4 21.8 %collective-permute-start.11 = (bf16[2,4,96,256]{3,2,1,0:T(8,128)(2,1)S(1)}, bf16[2,4,96,256]{3,2,1,0:T(8,128)(2,1)S(1)}, u32[]{:S(2)}, u32[]{:S(2)}) collective-permute-start(bf16[2,4,96,256]{3,2,1,0:T(8,128)(2,1)S(1)} %get-tuple-element.81), channel_id=1, source_target_pairs={{0,1},{1,0},{2,3},{3,2},{4,5},{5,4},{6,7},{7,6},{8,9},{9,8},{10,11... | collective-permute-start | bytes 1179656 | tf_op jit(solution)/shard_map/ppermute | solution.py:361
  29.8 13.4 %collective-permute-start.4 = (bf16[8,2,32,256]{3,2,1,0:T(8,128)(2,1)S(1)}, bf16[8,2,32,256]{3,2,1,0:T(8,128)(2,1)S(1)}, u32[]{:S(2)}, u32[]{:S(2)}) collective-permute-start(bf16[8,2,32,256]{3,2,1,0:T(8,128)(2,1)S(1)} %get-tuple-element.68), channel_id=1, source_target_pairs={{0,4},{1,5},{2,6},{3,7},{4,0},{5,1},{6,2},{7,3},{8,12},{9,13},{10,... | collective-permute-start | bytes 786440 | tf_op jit(solution)/shard_map/chunk0_step1/ppermute | solution.py:361
  32.6 16.8 %collective-permute-start.10 = (bf16[6,4,32,256]{3,2,1,0:T(8,128)(2,1)S(1)}, bf16[6,4,32,256]{3,2,1,0:T(8,128)(2,1)S(1)}, u32[]{:S(2)}, u32[]{:S(2)}) collective-permute-start(bf16[6,4,32,256]{3,2,1,0:T(8,128)(2,1)S(1)} %get-tuple-element.79), channel_id=1, source_target_pairs={{0,2},{1,3},{2,0},{3,1},{4,6},{5,7},{6,4},{7,5},{8,10},{9,11},{10,... | collective-permute-start | bytes 1179656 | tf_op jit(solution)/shard_map/chunk3_step0/ppermute | solution.py:361
  34.2 10.0 %collective-permute-start.12 = (bf16[6,2,32,256]{3,2,1,0:T(8,128)(2,1)S(1)}, bf16[6,2,32,256]{3,2,1,0:T(8,128)(2,1)S(1)}, u32[]{:S(2)}, u32[]{:S(2)}) collective-permute-start(bf16[6,2,32,256]{3,2,1,0:T(8,128)(2,1)S(1)} %get-tuple-element.82), channel_id=1, source_target_pairs={{0,8},{1,9},{2,10},{3,11},{4,12},{5,13},{6,14},{7,15},{8,0},{9,1},... | collective-permute-start | bytes 589832 | tf_op jit(solution)/shard_map/chunk1_step1/ppermute | solution.py:361
  40.9 28.9 %copy-start.1 = (bf16[64,128]{1,0:T(8,128)(2,1)S(1)}, bf16[64,128]{1,0:T(8,128)(2,1)}, u32[]{:S(2)}) copy-start(bf16[64,128]{1,0:T(8,128)(2,1)} %refs_13_.1) | copy-start | bytes 49156
  40.9 28.9 %copy-start.4 = (f32[64]{0:T(128)S(1)}, f32[64]{0:T(128)}, u32[]{:S(2)}) copy-start(f32[64]{0:T(128)} %refs_11_.1) | copy-start | bytes 772
  40.9 28.9 %copy-start.5 = (f32[64]{0:T(128)S(1)}, f32[64]{0:T(128)}, u32[]{:S(2)}) copy-start(f32[64]{0:T(128)} %refs_12_.1) | copy-start | bytes 772
  41.1 10.9 %collective-permute-start.9 = (bf16[8,2,32,256]{3,2,1,0:T(8,128)(2,1)S(1)}, bf16[8,2,32,256]{3,2,1,0:T(8,128)(2,1)S(1)}, u32[]{:S(2)}, u32[]{:S(2)}) collective-permute-start(bf16[8,2,32,256]{3,2,1,0:T(8,128)(2,1)S(1)} %get-tuple-element.78), channel_id=1, source_target_pairs={{0,4},{1,5},{2,6},{3,7},{4,0},{5,1},{6,2},{7,3},{8,12},{9,13},{10,... | collective-permute-start | bytes 786440 | tf_op jit(solution)/shard_map/chunk2_step1/ppermute | solution.py:361
  44.6 9.9 %collective-permute-start.15 = (bf16[4,4,32,256]{3,2,1,0:T(8,128)(2,1)S(1)}, bf16[4,4,32,256]{3,2,1,0:T(8,128)(2,1)S(1)}, u32[]{:S(2)}, u32[]{:S(2)}) collective-permute-start(bf16[4,4,32,256]{3,2,1,0:T(8,128)(2,1)S(1)} %get-tuple-element.90), channel_id=1, source_target_pairs={{0,2},{1,3},{2,0},{3,1},{4,6},{5,7},{6,4},{7,5},{8,10},{9,11},{10,... | collective-permute-start | bytes 786440 | tf_op jit(solution)/shard_map/chunk4_step0/ppermute | solution.py:361
  45.4 9.0 %collective-permute-start.8 = (bf16[8,1,32,256]{3,2,1,0:T(8,128)(2,1)S(1)}, bf16[8,1,32,256]{3,2,1,0:T(8,128)(2,1)S(1)}, u32[]{:S(2)}, u32[]{:S(2)}) collective-permute-start(bf16[8,1,32,256]{3,2,1,0:T(8,128)(2,1)S(1)} %get-tuple-element.77), channel_id=1, source_target_pairs={{0,8},{1,9},{2,10},{3,11},{4,12},{5,13},{6,14},{7,15},{8,0},{9,1},... | collective-permute-start | bytes 393224 | tf_op jit(solution)/shard_map/chunk0_step2/ppermute | solution.py:361
  49.4 10.2 %collective-permute-start.14 = (bf16[6,2,32,256]{3,2,1,0:T(8,128)(2,1)S(1)}, bf16[6,2,32,256]{3,2,1,0:T(8,128)(2,1)S(1)}, u32[]{:S(2)}, u32[]{:S(2)}) collective-permute-start(bf16[6,2,32,256]{3,2,1,0:T(8,128)(2,1)S(1)} %get-tuple-element.89), channel_id=1, source_target_pairs={{0,4},{1,5},{2,6},{3,7},{4,0},{5,1},{6,2},{7,3},{8,12},{9,13},{10,... | collective-permute-start | bytes 589832 | tf_op jit(solution)/shard_map/chunk3_step1/ppermute | solution.py:361
  52.0 10.6 %collective-permute-start.18 = (bf16[8,1,32,256]{3,2,1,0:T(8,128)(2,1)S(1)}, bf16[8,1,32,256]{3,2,1,0:T(8,128)(2,1)S(1)}, u32[]{:S(2)}, u32[]{:S(2)}) collective-permute-start(bf16[8,1,32,256]{3,2,1,0:T(8,128)(2,1)S(1)} %get-tuple-element.95), channel_id=1, source_target_pairs={{0,8},{1,9},{2,10},{3,11},{4,12},{5,13},{6,14},{7,15},{8,0},{9,1},... | collective-permute-start | bytes 393224 | tf_op jit(solution)/shard_map/chunk2_step2/ppermute | solution.py:361
  54.5 8.2 %collective-permute-start.17 = (bf16[4,2,32,256]{3,2,1,0:T(8,128)(2,1)S(1)}, bf16[4,2,32,256]{3,2,1,0:T(8,128)(2,1)S(1)}, u32[]{:S(2)}, u32[]{:S(2)}) collective-permute-start(bf16[4,2,32,256]{3,2,1,0:T(8,128)(2,1)S(1)} %get-tuple-element.94), channel_id=1, source_target_pairs={{0,4},{1,5},{2,6},{3,7},{4,0},{5,1},{6,2},{7,3},{8,12},{9,13},{10,... | collective-permute-start | bytes 393224 | tf_op jit(solution)/shard_map/chunk4_step1/ppermute | solution.py:361
  59.7 8.0 %collective-permute-start.16 = (bf16[6,1,32,256]{3,2,1,0:T(8,128)(2,1)S(1)}, bf16[6,1,32,256]{3,2,1,0:T(8,128)(2,1)S(1)}, u32[]{:S(2)}, u32[]{:S(2)}) collective-permute-start(bf16[6,1,32,256]{3,2,1,0:T(8,128)(2,1)S(1)} %get-tuple-element.93), channel_id=1, source_target_pairs={{0,8},{1,9},{2,10},{3,11},{4,12},{5,13},{6,14},{7,15},{8,0},{9,1},... | collective-permute-start | bytes 294920 | tf_op jit(solution)/shard_map/chunk3_step2/ppermute | solution.py:361
  61.3 6.4 %collective-permute-start.13 = (bf16[6,1,32,256]{3,2,1,0:T(8,128)(2,1)S(1)}, bf16[6,1,32,256]{3,2,1,0:T(8,128)(2,1)S(1)}, u32[]{:S(2)}, u32[]{:S(2)}) collective-permute-start(bf16[6,1,32,256]{3,2,1,0:T(8,128)(2,1)S(1)} %get-tuple-element.88), channel_id=1, source_target_pairs={{0,2},{1,3},{2,0},{3,1},{4,6},{5,7},{6,4},{7,5},{8,10},{9,11},{10,... | collective-permute-start | bytes 294920 | tf_op jit(solution)/shard_map/chunk1_step2/ppermute | solution.py:361
  62.8 5.7 %collective-permute-start.19 = (bf16[4,1,32,256]{3,2,1,0:T(8,128)(2,1)S(1)}, bf16[4,1,32,256]{3,2,1,0:T(8,128)(2,1)S(1)}, u32[]{:S(2)}, u32[]{:S(2)}) collective-permute-start(bf16[4,1,32,256]{3,2,1,0:T(8,128)(2,1)S(1)} %get-tuple-element.100), channel_id=1, source_target_pairs={{0,8},{1,9},{2,10},{3,11},{4,12},{5,13},{6,14},{7,15},{8,0},{9,1},... | collective-permute-start | bytes 196616 | tf_op jit(solution)/shard_map/chunk4_step2/ppermute | solution.py:361
  64.2 4.4 %collective-permute-start.20 = (f32[8,16,256]{2,1,0:T(8,128)S(1)}, f32[8,16,256]{2,1,0:T(8,128)S(1)}, u32[]{:S(2)}, u32[]{:S(2)}) collective-permute-start(f32[8,16,256]{2,1,0:T(8,128)S(1)} %get-tuple-element.102), channel_id=1, source_target_pairs={{0,1},{1,0},{2,3},{3,2},{4,5},{5,4},{6,7},{7,6},{8,9},{9,8},{10,11... | collective-permute-start | bytes 393224 | tf_op jit(solution)/shard_map/chunk0_step3/ppermute | solution.py:361
  64.2 4.4 %collective-permute-start.22 = (f32[8,16,256]{2,1,0:T(8,128)S(1)}, f32[8,16,256]{2,1,0:T(8,128)S(1)}, u32[]{:S(2)}, u32[]{:S(2)}) collective-permute-start(f32[8,16,256]{2,1,0:T(8,128)S(1)} %get-tuple-element.104), channel_id=1, source_target_pairs={{0,1},{1,0},{2,3},{3,2},{4,5},{5,4},{6,7},{7,6},{8,9},{9,8},{10,11... | collective-permute-start | bytes 393224 | tf_op jit(solution)/shard_map/chunk2_step3/ppermute | solution.py:361
  67.8 2.0 %collective-permute-start.21 = (f32[6,16,256]{2,1,0:T(8,128)S(1)}, f32[6,16,256]{2,1,0:T(8,128)S(1)}, u32[]{:S(2)}, u32[]{:S(2)}) collective-permute-start(f32[6,16,256]{2,1,0:T(8,128)S(1)} %get-tuple-element.103), channel_id=1, source_target_pairs={{0,1},{1,0},{2,3},{3,2},{4,5},{5,4},{6,7},{7,6},{8,9},{9,8},{10,11... | collective-permute-start | bytes 294920 | tf_op jit(solution)/shard_map/chunk1_step3/ppermute | solution.py:361
  67.9 1.9 %collective-permute-start.23 = (f32[6,16,256]{2,1,0:T(8,128)S(1)}, f32[6,16,256]{2,1,0:T(8,128)S(1)}, u32[]{:S(2)}, u32[]{:S(2)}) collective-permute-start(f32[6,16,256]{2,1,0:T(8,128)S(1)} %get-tuple-element.105), channel_id=1, source_target_pairs={{0,1},{1,0},{2,3},{3,2},{4,5},{5,4},{6,7},{7,6},{8,9},{9,8},{10,11... | collective-permute-start | bytes 294920 | tf_op jit(solution)/shard_map/chunk3_step3/ppermute | solution.py:361
  68.5 1.3 %collective-permute-start.24 = (f32[4,16,256]{2,1,0:T(8,128)S(1)}, f32[4,16,256]{2,1,0:T(8,128)S(1)}, u32[]{:S(2)}, u32[]{:S(2)}) collective-permute-start(f32[4,16,256]{2,1,0:T(8,128)S(1)} %get-tuple-element.106), channel_id=1, source_target_pairs={{0,1},{1,0},{2,3},{3,2},{4,5},{5,4},{6,7},{7,6},{8,9},{9,8},{10,11... | collective-permute-start | bytes 196616 | tf_op jit(solution)/shard_map/chunk4_step3/ppermute | solution.py:361

commit v5 on v4

--- a/solution.py
+++ b/solution.py
@@ -144,7 +144,7 @@
         [IN_PLACE] * (2 * len(chunks) + 1),
         [pltpu.VMEM((2, size, depth, width), bf16) for size in chunks] * 2 + [pltpu.VMEM((window, width, chan), bf16)],
         [
-            pltpu.VMEM((width // LANES, rows * stride, LANES), f32),
+            pltpu.VMEM((width // LANES, (rows + 1) * stride, LANES), f32),
             pltpu.VMEM((8 * size, chan), bf16),
             pltpu.VMEM((2, chan, LANES), f32),
             pltpu.VMEM((2, rows, width, chan), bf16),
@@ -323,7 +323,7 @@
         pl.BlockSpec(memory_space=pltpu.HBM),
         jax.ShapeDtypeStruct((rows, width, chan), bf16),
         [
-            pltpu.VMEM((width // LANES, hidden * stride, LANES), f32),
+            pltpu.VMEM((width // LANES, (hidden + 1) * stride, LANES), f32),
             pltpu.VMEM((2 * hidden, 2 * chan), bf16),
             pltpu.VMEM((rows, width, chan), bf16),
             pltpu.SemaphoreType.DMA((rows // 4,)),

time: 72.2 us -> 72.2 us (level)
  transfers between devices with their start and end apart: 25 -> 25, of which waited for: 11 -> 12; matrix products, arithmetic and copies ran while one was open for 0% -> 0% of each run, Pallas kernels for 6% -> 6%
where the time goes in v5:
time: 72.2 us; the launch traced here: 72 us
  starting transfers between devices  30.8 us (43%)
  waiting for transfers between devices  23.1 us (32%)
  Pallas kernels  17.8 us (25%)
    ppermute x25, starting transfers between devices, swap(): lax.ppermute(values, 'row', [(d, d ^ 1 << bit) for d in range(devices)])  30.8 us
    ppermute x25, waiting for transfers between devices, swap(): lax.ppermute(values, 'row', [(d, d ^ 1 << bit) for d in range(devices)])  23.1 us
    pallas_call x23, Pallas kernels, call(): pl.pallas_call(run, grid=grid, in_specs=list(in_specs) + [corner(array.sh...  17.8 us
  transfers between devices with their start and end apart: 25, of which 12 were waited for; matrix products, arithmetic and copies ran while one was open for 0% of the time, Pallas kernels for 6%

profile of v5, /device:TPU:0, one launch (start us, length us, event | category | flops | bytes accessed | tf_op | source)
XLA Modules:
  0.0 72.0 jit_solution(1481471649731631435)
XLA Ops:
  0.0 11.0 %shard_map.91 = (bf16[2,8,96,256]{3,2,1,0:T(8,128)(2,1)S(1)}, bf16[2,6,96,256]{3,2,1,0:T(8,128)(2,1)S(1)}, bf16[2,8,96,256]{3,2,1,0:T(8,128)(2,1)S(1)}, bf16[2,6...) custom-call(bf16[96,256,128]{2,1,0:T(8,128)(2,1)} %refs_0_.1, ...), custom_call_target="tpu_custom_call" | custom-call | flops 1610612736 | bytes 12582912 | tf_op jit(solution)/shard_map/pallas_call | solution.py:34
  11.0 0.6 collective-permute-start
  11.6 0.1 collective-permute-start.2
  11.7 0.4 collective-permute-start.3
  12.1 0.1 collective-permute-start.6
  12.2 1.3 %collective-permute-done.refs_1_ = bf16[2,8,96,256]{3,2,1,0:T(8,128)(2,1)S(1)} collective-permute-done((bf16[2,8,96,256]{3,2,1,0:T(8,128)(2,1)S(1)}, bf16[2,8,96,256]{3,2,1,0:T(8,128)(2,1)S(1)}, u32[]{:S(2)}, u32[]{:S(2)}) %collective-permute-start) | collective-permute-done | bytes 786464 | tf_op jit(solution)/shard_map/ppermute | solution.py:361
  13.5 0.6 chunk0_step0.1
  14.1 2.9 %collective-permute-start.1 = (bf16[8,4,32,256]{3,2,1,0:T(8,128)(2,1)S(1)}, bf16[8,4,32,256]{3,2,1,0:T(8,128)(2,1)S(1)}, u32[]{:S(2)}, u32[]{:S(2)}) collective-permute-start(bf16[8,4,32,256]{3,2,1,0:T(8,128)(2,1)S(1)} %get-tuple-element.59), channel_id=1, source_target_pairs={{0,2},{1,3},{2,0},{3,1},{4,6},{5,7},{6,4},{7,5},{8,10},{9,11},{10,... | collective-permute-start | bytes 1572872 | tf_op jit(solution)/shard_map/chunk0_step0/ppermute | solution.py:361
  17.0 0.5 chunk1_step0.1
  17.5 1.6 %collective-permute-start.7 = (bf16[6,4,32,256]{3,2,1,0:T(8,128)(2,1)S(1)}, bf16[6,4,32,256]{3,2,1,0:T(8,128)(2,1)S(1)}, u32[]{:S(2)}, u32[]{:S(2)}) collective-permute-start(bf16[6,4,32,256]{3,2,1,0:T(8,128)(2,1)S(1)} %get-tuple-element.72), channel_id=1, source_target_pairs={{0,4},{1,5},{2,6},{3,7},{4,0},{5,1},{6,2},{7,3},{8,12},{9,13},{10,... | collective-permute-start | bytes 1179656 | tf_op jit(solution)/shard_map/chunk1_step0/ppermute | solution.py:361
  19.1 1.3 %shard_map.92.refs_2_.refs_10_ = f32[16,256,128]{2,1,0:T(8,128)S(1)} custom-call(bf16[16,256,128]{2,1,0:T(8,128)(2,1)S(1)} %get-tuple-element.62.refs_0_, f32[1,128]{1,0:T(1,128)S(1)} %bitcast.3, f32[1,128]{1,0:T(1,128)S(1)} %bitcast.5, bf16[128,128]{1,0:T(8,128)(2,1)S(1)} %copy-done, f32[6,4,32,256]{3,2,1,0:T(8,128)S(1)} %get-tuple-element.65.refs_4_.refs_0_), custom_call_target="tpu_custom_call" | custom-call | flops 134217728 | bytes 3145728 | tf_op jit(solution)/shard_map/pallas_call | solution.py:34
  20.5 0.6 chunk2_step0.1
  21.0 1.4 %collective-permute-start.5 = (bf16[8,4,32,256]{3,2,1,0:T(8,128)(2,1)S(1)}, bf16[8,4,32,256]{3,2,1,0:T(8,128)(2,1)S(1)}, u32[]{:S(2)}, u32[]{:S(2)}) collective-permute-start(bf16[8,4,32,256]{3,2,1,0:T(8,128)(2,1)S(1)} %get-tuple-element.69), channel_id=1, source_target_pairs={{0,2},{1,3},{2,0},{3,1},{4,6},{5,7},{6,4},{7,5},{8,10},{9,11},{10,... | collective-permute-start | bytes 1572872 | tf_op jit(solution)/shard_map/chunk2_step0/ppermute | solution.py:361
  22.4 7.3 %collective-permute-done.1.refs_1_ = bf16[8,4,32,256]{3,2,1,0:T(8,128)(2,1)S(1)} collective-permute-done((bf16[8,4,32,256]{3,2,1,0:T(8,128)(2,1)S(1)}, bf16[8,4,32,256]{3,2,1,0:T(8,128)(2,1)S(1)}, u32[]{:S(2)}, u32[]{:S(2)}) %collective-permute-start.1) | collective-permute-done | bytes 524320 | tf_op jit(solution)/shard_map/chunk0_step0/ppermute | solution.py:361
  29.7 0.1 chunk0_step1.1
  29.8 2.2 %collective-permute-start.4 = (bf16[8,2,32,256]{3,2,1,0:T(8,128)(2,1)S(1)}, bf16[8,2,32,256]{3,2,1,0:T(8,128)(2,1)S(1)}, u32[]{:S(2)}, u32[]{:S(2)}) collective-permute-start(bf16[8,2,32,256]{3,2,1,0:T(8,128)(2,1)S(1)} %get-tuple-element.68), channel_id=1, source_target_pairs={{0,4},{1,5},{2,6},{3,7},{4,0},{5,1},{6,2},{7,3},{8,12},{9,13},{10,... | collective-permute-start | bytes 786440 | tf_op jit(solution)/shard_map/chunk0_step1/ppermute | solution.py:361
  32.0 0.1 chunk1_step1.1
  32.1 0.5 chunk3_step0.1
  32.6 1.6 %collective-permute-start.10 = (bf16[6,4,32,256]{3,2,1,0:T(8,128)(2,1)S(1)}, bf16[6,4,32,256]{3,2,1,0:T(8,128)(2,1)S(1)}, u32[]{:S(2)}, u32[]{:S(2)}) collective-permute-start(bf16[6,4,32,256]{3,2,1,0:T(8,128)(2,1)S(1)} %get-tuple-element.79), channel_id=1, source_target_pairs={{0,2},{1,3},{2,0},{3,1},{4,6},{5,7},{6,4},{7,5},{8,10},{9,11},{10,... | collective-permute-start | bytes 1179656 | tf_op jit(solution)/shard_map/chunk3_step0/ppermute | solution.py:361
  34.2 2.6 %collective-permute-start.12 = (bf16[6,2,32,256]{3,2,1,0:T(8,128)(2,1)S(1)}, bf16[6,2,32,256]{3,2,1,0:T(8,128)(2,1)S(1)}, u32[]{:S(2)}, u32[]{:S(2)}) collective-permute-start(bf16[6,2,32,256]{3,2,1,0:T(8,128)(2,1)S(1)} %get-tuple-element.82), channel_id=1, source_target_pairs={{0,8},{1,9},{2,10},{3,11},{4,12},{5,13},{6,14},{7,15},{8,0},{9,1},... | collective-permute-start | bytes 589832 | tf_op jit(solution)/shard_map/chunk1_step1/ppermute | solution.py:361
  36.8 4.2 %collective-permute-done.5.refs_1_ = bf16[8,4,32,256]{3,2,1,0:T(8,128)(2,1)S(1)} collective-permute-done((bf16[8,4,32,256]{3,2,1,0:T(8,128)(2,1)S(1)}, bf16[8,4,32,256]{3,2,1,0:T(8,128)(2,1)S(1)}, u32[]{:S(2)}, u32[]{:S(2)}) %collective-permute-start.5) | collective-permute-done | bytes 524320 | tf_op jit(solution)/shard_map/chunk2_step0/ppermute | solution.py:361
  41.0 0.1 chunk2_step1.1
  41.1 2.2 %collective-permute-start.9 = (bf16[8,2,32,256]{3,2,1,0:T(8,128)(2,1)S(1)}, bf16[8,2,32,256]{3,2,1,0:T(8,128)(2,1)S(1)}, u32[]{:S(2)}, u32[]{:S(2)}) collective-permute-start(bf16[8,2,32,256]{3,2,1,0:T(8,128)(2,1)S(1)} %get-tuple-element.78), channel_id=1, source_target_pairs={{0,4},{1,5},{2,6},{3,7},{4,0},{5,1},{6,2},{7,3},{8,12},{9,13},{10,... | collective-permute-start | bytes 786440 | tf_op jit(solution)/shard_map/chunk2_step1/ppermute | solution.py:361
  43.3 0.9 %collective-permute-done.12.refs_1_ = bf16[6,2,32,256]{3,2,1,0:T(8,128)(2,1)S(1)} collective-permute-done((bf16[6,2,32,256]{3,2,1,0:T(8,128)(2,1)S(1)}, bf16[6,2,32,256]{3,2,1,0:T(8,128)(2,1)S(1)}, u32[]{:S(2)}, u32[]{:S(2)}) %collective-permute-start.12) | collective-permute-done | bytes 196640 | tf_op jit(solution)/shard_map/chunk1_step1/ppermute | solution.py:361
  44.2 0.4 chunk4_step0.1
  44.6 0.7 %collective-permute-start.15 = (bf16[4,4,32,256]{3,2,1,0:T(8,128)(2,1)S(1)}, bf16[4,4,32,256]{3,2,1,0:T(8,128)(2,1)S(1)}, u32[]{:S(2)}, u32[]{:S(2)}) collective-permute-start(bf16[4,4,32,256]{3,2,1,0:T(8,128)(2,1)S(1)} %get-tuple-element.90), channel_id=1, source_target_pairs={{0,2},{1,3},{2,0},{3,1},{4,6},{5,7},{6,4},{7,5},{8,10},{9,11},{10,... | collective-permute-start | bytes 786440 | tf_op jit(solution)/shard_map/chunk4_step0/ppermute | solution.py:361
  45.4 2.6 %collective-permute-start.8 = (bf16[8,1,32,256]{3,2,1,0:T(8,128)(2,1)S(1)}, bf16[8,1,32,256]{3,2,1,0:T(8,128)(2,1)S(1)}, u32[]{:S(2)}, u32[]{:S(2)}) collective-permute-start(bf16[8,1,32,256]{3,2,1,0:T(8,128)(2,1)S(1)} %get-tuple-element.77), channel_id=1, source_target_pairs={{0,8},{1,9},{2,10},{3,11},{4,12},{5,13},{6,14},{7,15},{8,0},{9,1},... | collective-permute-start | bytes 393224 | tf_op jit(solution)/shard_map/chunk0_step2/ppermute | solution.py:361
  48.0 1.4 %collective-permute-done.10.refs_1_ = bf16[6,4,32,256]{3,2,1,0:T(8,128)(2,1)S(1)} collective-permute-done((bf16[6,4,32,256]{3,2,1,0:T(8,128)(2,1)S(1)}, bf16[6,4,32,256]{3,2,1,0:T(8,128)(2,1)S(1)}, u32[]{:S(2)}, u32[]{:S(2)}) %collective-permute-start.10) | collective-permute-done | bytes 393248 | tf_op jit(solution)/shard_map/chunk3_step0/ppermute | solution.py:361
  49.4 0.1 chunk3_step1.1
  49.4 2.2 %collective-permute-start.14 = (bf16[6,2,32,256]{3,2,1,0:T(8,128)(2,1)S(1)}, bf16[6,2,32,256]{3,2,1,0:T(8,128)(2,1)S(1)}, u32[]{:S(2)}, u32[]{:S(2)}) collective-permute-start(bf16[6,2,32,256]{3,2,1,0:T(8,128)(2,1)S(1)} %get-tuple-element.89), channel_id=1, source_target_pairs={{0,4},{1,5},{2,6},{3,7},{4,0},{5,1},{6,2},{7,3},{8,12},{9,13},{10,... | collective-permute-start | bytes 589832 | tf_op jit(solution)/shard_map/chunk3_step1/ppermute | solution.py:361
  51.6 0.3 collective-permute-done.9.refs_1_
  52.0 2.3 %collective-permute-start.18 = (bf16[8,1,32,256]{3,2,1,0:T(8,128)(2,1)S(1)}, bf16[8,1,32,256]{3,2,1,0:T(8,128)(2,1)S(1)}, u32[]{:S(2)}, u32[]{:S(2)}) collective-permute-start(bf16[8,1,32,256]{3,2,1,0:T(8,128)(2,1)S(1)} %get-tuple-element.95), channel_id=1, source_target_pairs={{0,8},{1,9},{2,10},{3,11},{4,12},{5,13},{6,14},{7,15},{8,0},{9,1},... | collective-permute-start | bytes 393224 | tf_op jit(solution)/shard_map/chunk2_step2/ppermute | solution.py:361
  54.4 0.1 collective-permute-done.15.refs_1_
  54.6 1.9 %collective-permute-start.17 = (bf16[4,2,32,256]{3,2,1,0:T(8,128)(2,1)S(1)}, bf16[4,2,32,256]{3,2,1,0:T(8,128)(2,1)S(1)}, u32[]{:S(2)}, u32[]{:S(2)}) collective-permute-start(bf16[4,2,32,256]{3,2,1,0:T(8,128)(2,1)S(1)} %get-tuple-element.94), channel_id=1, source_target_pairs={{0,4},{1,5},{2,6},{3,7},{4,0},{5,1},{6,2},{7,3},{8,12},{9,13},{10,... | collective-permute-start | bytes 393224 | tf_op jit(solution)/shard_map/chunk4_step1/ppermute | solution.py:361
  56.4 3.3 %collective-permute-done.14.refs_1_ = bf16[6,2,32,256]{3,2,1,0:T(8,128)(2,1)S(1)} collective-permute-done((bf16[6,2,32,256]{3,2,1,0:T(8,128)(2,1)S(1)}, bf16[6,2,32,256]{3,2,1,0:T(8,128)(2,1)S(1)}, u32[]{:S(2)}, u32[]{:S(2)}) %collective-permute-start.14) | collective-permute-done | bytes 196640 | tf_op jit(solution)/shard_map/chunk3_step1/ppermute | solution.py:361
  59.7 1.6 %collective-permute-start.16 = (bf16[6,1,32,256]{3,2,1,0:T(8,128)(2,1)S(1)}, bf16[6,1,32,256]{3,2,1,0:T(8,128)(2,1)S(1)}, u32[]{:S(2)}, u32[]{:S(2)}) collective-permute-start(bf16[6,1,32,256]{3,2,1,0:T(8,128)(2,1)S(1)} %get-tuple-element.93), channel_id=1, source_target_pairs={{0,8},{1,9},{2,10},{3,11},{4,12},{5,13},{6,14},{7,15},{8,0},{9,1},... | collective-permute-start | bytes 294920 | tf_op jit(solution)/shard_map/chunk3_step2/ppermute | solution.py:361
  61.4 1.2 %collective-permute-start.13 = (bf16[6,1,32,256]{3,2,1,0:T(8,128)(2,1)S(1)}, bf16[6,1,32,256]{3,2,1,0:T(8,128)(2,1)S(1)}, u32[]{:S(2)}, u32[]{:S(2)}) collective-permute-start(bf16[6,1,32,256]{3,2,1,0:T(8,128)(2,1)S(1)} %get-tuple-element.88), channel_id=1, source_target_pairs={{0,2},{1,3},{2,0},{3,1},{4,6},{5,7},{6,4},{7,5},{8,10},{9,11},{10,... | collective-permute-start | bytes 294920 | tf_op jit(solution)/shard_map/chunk1_step2/ppermute | solution.py:361
  62.6 0.1 chunk2_step3.1
  62.7 0.1 collective-permute-done.17.refs_1_
  62.8 1.4 %collective-permute-start.19 = (bf16[4,1,32,256]{3,2,1,0:T(8,128)(2,1)S(1)}, bf16[4,1,32,256]{3,2,1,0:T(8,128)(2,1)S(1)}, u32[]{:S(2)}, u32[]{:S(2)}) collective-permute-start(bf16[4,1,32,256]{3,2,1,0:T(8,128)(2,1)S(1)} %get-tuple-element.100), channel_id=1, source_target_pairs={{0,8},{1,9},{2,10},{3,11},{4,12},{5,13},{6,14},{7,15},{8,0},{9,1},... | collective-permute-start | bytes 196616 | tf_op jit(solution)/shard_map/chunk4_step2/ppermute | solution.py:361
  64.2 0.5 collective-permute-start.22
  64.8 2.9 %collective-permute-done.16.refs_1_ = bf16[6,1,32,256]{3,2,1,0:T(8,128)(2,1)S(1)} collective-permute-done((bf16[6,1,32,256]{3,2,1,0:T(8,128)(2,1)S(1)}, bf16[6,1,32,256]{3,2,1,0:T(8,128)(2,1)S(1)}, u32[]{:S(2)}, u32[]{:S(2)}) %collective-permute-start.16) | collective-permute-done | bytes 98336 | tf_op jit(solution)/shard_map/chunk3_step2/ppermute | solution.py:361
  67.8 0.1 collective-permute-start.21
  67.8 0.5 collective-permute-start.23
  68.3 0.1 collective-permute-done.19.refs_1_
  68.5 0.1 collective-permute-start.24
  68.6 1.2 %collective-permute-done.24.refs_9_ = f32[4,16,256]{2,1,0:T(8,128)S(1)} collective-permute-done((f32[4,16,256]{2,1,0:T(8,128)S(1)}, f32[4,16,256]{2,1,0:T(8,128)S(1)}, u32[]{:S(2)}, u32[]{:S(2)}) %collective-permute-start.24) | collective-permute-done | bytes 65568 | tf_op jit(solution)/shard_map/chunk4_step3/ppermute | solution.py:361
  69.8 2.2 %shard_map.93 = bf16[16,256,128]{2,1,0:T(8,128)(2,1)} custom-call(f32[8,16,256]{2,1,0:T(8,128)S(1)} %get-tuple-element.87.refs_2_.refs_0_, f32[6,16,256]{2,1,0:T(8,128)S(1)} %get-tuple-element.99.refs_2_.refs_1_, f32[8,16,256]{2,1,0:T(8,128)S(1)} %get-tuple-element.96.refs_2_, f32[6,16,256]{2,1,0:T(8,128)S(1)} %get-tuple-element.98.refs_2_.refs_3_, ...), custom_call_target="tpu_custom_call" | custom-call | flops 67108864 | bytes 4194304 | tf_op jit(solution)/shard_map/pallas_call | solution.py:34
  (37 shorter events, 0.5 us)
Async XLA Ops:
  0.0 19.1 %copy-start.3 = (f32[128]{0:T(128)S(1)}, f32[128]{0:T(128)}, u32[]{:S(2)}) copy-start(f32[128]{0:T(128)} %param.12) | copy-start | bytes 1540
  0.0 19.1 %copy-start.2 = (f32[128]{0:T(128)S(1)}, f32[128]{0:T(128)}, u32[]{:S(2)}) copy-start(f32[128]{0:T(128)} %param.11) | copy-start | bytes 1540
  0.0 19.1 %copy-start = (bf16[128,128]{1,0:T(8,128)(2,1)S(1)}, bf16[128,128]{1,0:T(8,128)(2,1)}, u32[]{:S(2)}) copy-start(bf16[128,128]{1,0:T(8,128)(2,1)} %refs_3_.1) | copy-start | bytes 98308
  11.0 2.5 %collective-permute-start = (bf16[2,8,96,256]{3,2,1,0:T(8,128)(2,1)S(1)}, bf16[2,8,96,256]{3,2,1,0:T(8,128)(2,1)S(1)}, u32[]{:S(2)}, u32[]{:S(2)}) collective-permute-start(bf16[2,8,96,256]{3,2,1,0:T(8,128)(2,1)S(1)} %get-tuple-element.57), channel_id=1, source_target_pairs={{0,1},{1,0},{2,3},{3,2},{4,5},{5,4},{6,7},{7,6},{8,9},{9,8},{10,11... | collective-permute-start | bytes 2359304 | tf_op jit(solution)/shard_map/ppermute | solution.py:361
  11.6 8.9 %collective-permute-start.2 = (bf16[2,8,96,256]{3,2,1,0:T(8,128)(2,1)S(1)}, bf16[2,8,96,256]{3,2,1,0:T(8,128)(2,1)S(1)}, u32[]{:S(2)}, u32[]{:S(2)}) collective-permute-start(bf16[2,8,96,256]{3,2,1,0:T(8,128)(2,1)S(1)} %get-tuple-element.61), channel_id=1, source_target_pairs={{0,1},{1,0},{2,3},{3,2},{4,5},{5,4},{6,7},{7,6},{8,9},{9,8},{10,11... | collective-permute-start | bytes 2359304 | tf_op jit(solution)/shard_map/ppermute | solution.py:361
  11.7 5.4 %collective-permute-start.3 = (bf16[2,6,96,256]{3,2,1,0:T(8,128)(2,1)S(1)}, bf16[2,6,96,256]{3,2,1,0:T(8,128)(2,1)S(1)}, u32[]{:S(2)}, u32[]{:S(2)}) collective-permute-start(bf16[2,6,96,256]{3,2,1,0:T(8,128)(2,1)S(1)} %get-tuple-element.64), channel_id=1, source_target_pairs={{0,1},{1,0},{2,3},{3,2},{4,5},{5,4},{6,7},{7,6},{8,9},{9,8},{10,11... | collective-permute-start | bytes 1769480 | tf_op jit(solution)/shard_map/ppermute | solution.py:361
  12.1 20.0 %collective-permute-start.6 = (bf16[2,6,96,256]{3,2,1,0:T(8,128)(2,1)S(1)}, bf16[2,6,96,256]{3,2,1,0:T(8,128)(2,1)S(1)}, u32[]{:S(2)}, u32[]{:S(2)}) collective-permute-start(bf16[2,6,96,256]{3,2,1,0:T(8,128)(2,1)S(1)} %get-tuple-element.71), channel_id=1, source_target_pairs={{0,1},{1,0},{2,3},{3,2},{4,5},{5,4},{6,7},{7,6},{8,9},{9,8},{10,11... | collective-permute-start | bytes 1769480 | tf_op jit(solution)/shard_map/ppermute | solution.py:361
  14.1 15.6 %collective-permute-start.1 = (bf16[8,4,32,256]{3,2,1,0:T(8,128)(2,1)S(1)}, bf16[8,4,32,256]{3,2,1,0:T(8,128)(2,1)S(1)}, u32[]{:S(2)}, u32[]{:S(2)}) collective-permute-start(bf16[8,4,32,256]{3,2,1,0:T(8,128)(2,1)S(1)} %get-tuple-element.59), channel_id=1, source_target_pairs={{0,2},{1,3},{2,0},{3,1},{4,6},{5,7},{6,4},{7,5},{8,10},{9,11},{10,... | collective-permute-start | bytes 1572872 | tf_op jit(solution)/shard_map/chunk0_step0/ppermute | solution.py:361
  17.5 14.5 %collective-permute-start.7 = (bf16[6,4,32,256]{3,2,1,0:T(8,128)(2,1)S(1)}, bf16[6,4,32,256]{3,2,1,0:T(8,128)(2,1)S(1)}, u32[]{:S(2)}, u32[]{:S(2)}) collective-permute-start(bf16[6,4,32,256]{3,2,1,0:T(8,128)(2,1)S(1)} %get-tuple-element.72), channel_id=1, source_target_pairs={{0,4},{1,5},{2,6},{3,7},{4,0},{5,1},{6,2},{7,3},{8,12},{9,13},{10,... | collective-permute-start | bytes 1179656 | tf_op jit(solution)/shard_map/chunk1_step0/ppermute | solution.py:361
  21.0 19.9 %collective-permute-start.5 = (bf16[8,4,32,256]{3,2,1,0:T(8,128)(2,1)S(1)}, bf16[8,4,32,256]{3,2,1,0:T(8,128)(2,1)S(1)}, u32[]{:S(2)}, u32[]{:S(2)}) collective-permute-start(bf16[8,4,32,256]{3,2,1,0:T(8,128)(2,1)S(1)} %get-tuple-element.69), channel_id=1, source_target_pairs={{0,2},{1,3},{2,0},{3,1},{4,6},{5,7},{6,4},{7,5},{8,10},{9,11},{10,... | collective-permute-start | bytes 1572872 | tf_op jit(solution)/shard_map/chunk2_step0/ppermute | solution.py:361
  22.4 21.8 %collective-permute-start.11 = (bf16[2,4,96,256]{3,2,1,0:T(8,128)(2,1)S(1)}, bf16[2,4,96,256]{3,2,1,0:T(8,128)(2,1)S(1)}, u32[]{:S(2)}, u32[]{:S(2)}) collective-permute-start(bf16[2,4,96,256]{3,2,1,0:T(8,128)(2,1)S(1)} %get-tuple-element.81), channel_id=1, source_target_pairs={{0,1},{1,0},{2,3},{3,2},{4,5},{5,4},{6,7},{7,6},{8,9},{9,8},{10,11... | collective-permute-start | bytes 1179656 | tf_op jit(solution)/shard_map/ppermute | solution.py:361
  29.8 13.4 %collective-permute-start.4 = (bf16[8,2,32,256]{3,2,1,0:T(8,128)(2,1)S(1)}, bf16[8,2,32,256]{3,2,1,0:T(8,128)(2,1)S(1)}, u32[]{:S(2)}, u32[]{:S(2)}) collective-permute-start(bf16[8,2,32,256]{3,2,1,0:T(8,128)(2,1)S(1)} %get-tuple-element.68), channel_id=1, source_target_pairs={{0,4},{1,5},{2,6},{3,7},{4,0},{5,1},{6,2},{7,3},{8,12},{9,13},{10,... | collective-permute-start | bytes 786440 | tf_op jit(solution)/shard_map/chunk0_step1/ppermute | solution.py:361
  32.6 16.8 %collective-permute-start.10 = (bf16[6,4,32,256]{3,2,1,0:T(8,128)(2,1)S(1)}, bf16[6,4,32,256]{3,2,1,0:T(8,128)(2,1)S(1)}, u32[]{:S(2)}, u32[]{:S(2)}) collective-permute-start(bf16[6,4,32,256]{3,2,1,0:T(8,128)(2,1)S(1)} %get-tuple-element.79), channel_id=1, source_target_pairs={{0,2},{1,3},{2,0},{3,1},{4,6},{5,7},{6,4},{7,5},{8,10},{9,11},{10,... | collective-permute-start | bytes 1179656 | tf_op jit(solution)/shard_map/chunk3_step0/ppermute | solution.py:361
  34.2 10.0 %collective-permute-start.12 = (bf16[6,2,32,256]{3,2,1,0:T(8,128)(2,1)S(1)}, bf16[6,2,32,256]{3,2,1,0:T(8,128)(2,1)S(1)}, u32[]{:S(2)}, u32[]{:S(2)}) collective-permute-start(bf16[6,2,32,256]{3,2,1,0:T(8,128)(2,1)S(1)} %get-tuple-element.82), channel_id=1, source_target_pairs={{0,8},{1,9},{2,10},{3,11},{4,12},{5,13},{6,14},{7,15},{8,0},{9,1},... | collective-permute-start | bytes 589832 | tf_op jit(solution)/shard_map/chunk1_step1/ppermute | solution.py:361
  41.0 28.9 %copy-start.1 = (bf16[64,128]{1,0:T(8,128)(2,1)S(1)}, bf16[64,128]{1,0:T(8,128)(2,1)}, u32[]{:S(2)}) copy-start(bf16[64,128]{1,0:T(8,128)(2,1)} %refs_13_.1) | copy-start | bytes 49156
  41.0 28.9 %copy-start.4 = (f32[64]{0:T(128)S(1)}, f32[64]{0:T(128)}, u32[]{:S(2)}) copy-start(f32[64]{0:T(128)} %refs_11_.1) | copy-start | bytes 772
  41.0 28.9 %copy-start.5 = (f32[64]{0:T(128)S(1)}, f32[64]{0:T(128)}, u32[]{:S(2)}) copy-start(f32[64]{0:T(128)} %refs_12_.1) | copy-start | bytes 772
  41.1 10.9 %collective-permute-start.9 = (bf16[8,2,32,256]{3,2,1,0:T(8,128)(2,1)S(1)}, bf16[8,2,32,256]{3,2,1,0:T(8,128)(2,1)S(1)}, u32[]{:S(2)}, u32[]{:S(2)}) collective-permute-start(bf16[8,2,32,256]{3,2,1,0:T(8,128)(2,1)S(1)} %get-tuple-element.78), channel_id=1, source_target_pairs={{0,4},{1,5},{2,6},{3,7},{4,0},{5,1},{6,2},{7,3},{8,12},{9,13},{10,... | collective-permute-start | bytes 786440 | tf_op jit(solution)/shard_map/chunk2_step1/ppermute | solution.py:361
  44.6 9.9 %collective-permute-start.15 = (bf16[4,4,32,256]{3,2,1,0:T(8,128)(2,1)S(1)}, bf16[4,4,32,256]{3,2,1,0:T(8,128)(2,1)S(1)}, u32[]{:S(2)}, u32[]{:S(2)}) collective-permute-start(bf16[4,4,32,256]{3,2,1,0:T(8,128)(2,1)S(1)} %get-tuple-element.90), channel_id=1, source_target_pairs={{0,2},{1,3},{2,0},{3,1},{4,6},{5,7},{6,4},{7,5},{8,10},{9,11},{10,... | collective-permute-start | bytes 786440 | tf_op jit(solution)/shard_map/chunk4_step0/ppermute | solution.py:361
  45.4 9.0 %collective-permute-start.8 = (bf16[8,1,32,256]{3,2,1,0:T(8,128)(2,1)S(1)}, bf16[8,1,32,256]{3,2,1,0:T(8,128)(2,1)S(1)}, u32[]{:S(2)}, u32[]{:S(2)}) collective-permute-start(bf16[8,1,32,256]{3,2,1,0:T(8,128)(2,1)S(1)} %get-tuple-element.77), channel_id=1, source_target_pairs={{0,8},{1,9},{2,10},{3,11},{4,12},{5,13},{6,14},{7,15},{8,0},{9,1},... | collective-permute-start | bytes 393224 | tf_op jit(solution)/shard_map/chunk0_step2/ppermute | solution.py:361
  49.4 10.2 %collective-permute-start.14 = (bf16[6,2,32,256]{3,2,1,0:T(8,128)(2,1)S(1)}, bf16[6,2,32,256]{3,2,1,0:T(8,128)(2,1)S(1)}, u32[]{:S(2)}, u32[]{:S(2)}) collective-permute-start(bf16[6,2,32,256]{3,2,1,0:T(8,128)(2,1)S(1)} %get-tuple-element.89), channel_id=1, source_target_pairs={{0,4},{1,5},{2,6},{3,7},{4,0},{5,1},{6,2},{7,3},{8,12},{9,13},{10,... | collective-permute-start | bytes 589832 | tf_op jit(solution)/shard_map/chunk3_step1/ppermute | solution.py:361
  52.0 10.6 %collective-permute-start.18 = (bf16[8,1,32,256]{3,2,1,0:T(8,128)(2,1)S(1)}, bf16[8,1,32,256]{3,2,1,0:T(8,128)(2,1)S(1)}, u32[]{:S(2)}, u32[]{:S(2)}) collective-permute-start(bf16[8,1,32,256]{3,2,1,0:T(8,128)(2,1)S(1)} %get-tuple-element.95), channel_id=1, source_target_pairs={{0,8},{1,9},{2,10},{3,11},{4,12},{5,13},{6,14},{7,15},{8,0},{9,1},... | collective-permute-start | bytes 393224 | tf_op jit(solution)/shard_map/chunk2_step2/ppermute | solution.py:361
  54.6 8.2 %collective-permute-start.17 = (bf16[4,2,32,256]{3,2,1,0:T(8,128)(2,1)S(1)}, bf16[4,2,32,256]{3,2,1,0:T(8,128)(2,1)S(1)}, u32[]{:S(2)}, u32[]{:S(2)}) collective-permute-start(bf16[4,2,32,256]{3,2,1,0:T(8,128)(2,1)S(1)} %get-tuple-element.94), channel_id=1, source_target_pairs={{0,4},{1,5},{2,6},{3,7},{4,0},{5,1},{6,2},{7,3},{8,12},{9,13},{10,... | collective-permute-start | bytes 393224 | tf_op jit(solution)/shard_map/chunk4_step1/ppermute | solution.py:361
  59.7 8.0 %collective-permute-start.16 = (bf16[6,1,32,256]{3,2,1,0:T(8,128)(2,1)S(1)}, bf16[6,1,32,256]{3,2,1,0:T(8,128)(2,1)S(1)}, u32[]{:S(2)}, u32[]{:S(2)}) collective-permute-start(bf16[6,1,32,256]{3,2,1,0:T(8,128)(2,1)S(1)} %get-tuple-element.93), channel_id=1, source_target_pairs={{0,8},{1,9},{2,10},{3,11},{4,12},{5,13},{6,14},{7,15},{8,0},{9,1},... | collective-permute-start | bytes 294920 | tf_op jit(solution)/shard_map/chunk3_step2/ppermute | solution.py:361
  61.4 6.3 %collective-permute-start.13 = (bf16[6,1,32,256]{3,2,1,0:T(8,128)(2,1)S(1)}, bf16[6,1,32,256]{3,2,1,0:T(8,128)(2,1)S(1)}, u32[]{:S(2)}, u32[]{:S(2)}) collective-permute-start(bf16[6,1,32,256]{3,2,1,0:T(8,128)(2,1)S(1)} %get-tuple-element.88), channel_id=1, source_target_pairs={{0,2},{1,3},{2,0},{3,1},{4,6},{5,7},{6,4},{7,5},{8,10},{9,11},{10,... | collective-permute-start | bytes 294920 | tf_op jit(solution)/shard_map/chunk1_step2/ppermute | solution.py:361
  62.8 5.6 %collective-permute-start.19 = (bf16[4,1,32,256]{3,2,1,0:T(8,128)(2,1)S(1)}, bf16[4,1,32,256]{3,2,1,0:T(8,128)(2,1)S(1)}, u32[]{:S(2)}, u32[]{:S(2)}) collective-permute-start(bf16[4,1,32,256]{3,2,1,0:T(8,128)(2,1)S(1)} %get-tuple-element.100), channel_id=1, source_target_pairs={{0,8},{1,9},{2,10},{3,11},{4,12},{5,13},{6,14},{7,15},{8,0},{9,1},... | collective-permute-start | bytes 196616 | tf_op jit(solution)/shard_map/chunk4_step2/ppermute | solution.py:361
  64.2 4.3 %collective-permute-start.20 = (f32[8,16,256]{2,1,0:T(8,128)S(1)}, f32[8,16,256]{2,1,0:T(8,128)S(1)}, u32[]{:S(2)}, u32[]{:S(2)}) collective-permute-start(f32[8,16,256]{2,1,0:T(8,128)S(1)} %get-tuple-element.102), channel_id=1, source_target_pairs={{0,1},{1,0},{2,3},{3,2},{4,5},{5,4},{6,7},{7,6},{8,9},{9,8},{10,11... | collective-permute-start | bytes 393224 | tf_op jit(solution)/shard_map/chunk0_step3/ppermute | solution.py:361
  64.2 4.3 %collective-permute-start.22 = (f32[8,16,256]{2,1,0:T(8,128)S(1)}, f32[8,16,256]{2,1,0:T(8,128)S(1)}, u32[]{:S(2)}, u32[]{:S(2)}) collective-permute-start(f32[8,16,256]{2,1,0:T(8,128)S(1)} %get-tuple-element.104), channel_id=1, source_target_pairs={{0,1},{1,0},{2,3},{3,2},{4,5},{5,4},{6,7},{7,6},{8,9},{9,8},{10,11... | collective-permute-start | bytes 393224 | tf_op jit(solution)/shard_map/chunk2_step3/ppermute | solution.py:361
  67.8 2.0 %collective-permute-start.21 = (f32[6,16,256]{2,1,0:T(8,128)S(1)}, f32[6,16,256]{2,1,0:T(8,128)S(1)}, u32[]{:S(2)}, u32[]{:S(2)}) collective-permute-start(f32[6,16,256]{2,1,0:T(8,128)S(1)} %get-tuple-element.103), channel_id=1, source_target_pairs={{0,1},{1,0},{2,3},{3,2},{4,5},{5,4},{6,7},{7,6},{8,9},{9,8},{10,11... | collective-permute-start | bytes 294920 | tf_op jit(solution)/shard_map/chunk1_step3/ppermute | solution.py:361
  67.8 2.0 %collective-permute-start.23 = (f32[6,16,256]{2,1,0:T(8,128)S(1)}, f32[6,16,256]{2,1,0:T(8,128)S(1)}, u32[]{:S(2)}, u32[]{:S(2)}) collective-permute-start(f32[6,16,256]{2,1,0:T(8,128)S(1)} %get-tuple-element.105), channel_id=1, source_target_pairs={{0,1},{1,0},{2,3},{3,2},{4,5},{5,4},{6,7},{7,6},{8,9},{9,8},{10,11... | collective-permute-start | bytes 294920 | tf_op jit(solution)/shard_map/chunk3_step3/ppermute | solution.py:361
  68.5 1.3 %collective-permute-start.24 = (f32[4,16,256]{2,1,0:T(8,128)S(1)}, f32[4,16,256]{2,1,0:T(8,128)S(1)}, u32[]{:S(2)}, u32[]{:S(2)}) collective-permute-start(f32[4,16,256]{2,1,0:T(8,128)S(1)} %get-tuple-element.106), channel_id=1, source_target_pairs={{0,1},{1,0},{2,3},{3,2},{4,5},{5,4},{6,7},{7,6},{8,9},{9,8},{10,11... | collective-permute-start | bytes 196616 | tf_op jit(solution)/shard_map/chunk4_step3/ppermute | solution.py:361
